TPU v7x, 32 devices: a whole 2x2x4 slice. The times are simulated.
32 devices in a mesh: groups: 2 (over y), expert: 4 (over z), dp: 2 (over x), tensor: 2 (over core).
Axes of the slice: x: 2, y: 2, z: 4, core: 2. Of those that a mesh axis runs over, the one named last changes fastest.
Arguments:
- tokens: bfloat16 [2048, 2048], P(('groups', 'expert', 'dp'), 'tensor'), parts along dimension 0, may hold values from -6 to 6
- cotangent: bfloat16 [2048, 2048], P(('groups', 'expert', 'dp'), 'tensor'), parts along dimension 0, may hold values from -6 to 6
- expert_ids: int32 [2048, 2], P(('groups', 'expert', 'dp')), parts along dimension 0, may hold values from 0 to 3, all different within a row; in each aligned block of 128 rows (0 to 127, 128 to 255, ...) at most 96 rows name the same one
- gate_probs: float32 [2048, 2], P(('groups', 'expert', 'dp')), parts along dimension 0, may hold values from 0.05 to 1
- w_gate: bfloat16 [4, 2048, 1408], P('expert', 'dp', 'tensor'), may hold values from -0.125 to 0.125
- w_up: bfloat16 [4, 2048, 1408], P('expert', 'dp', 'tensor'), may hold values from -0.125 to 0.125
- w_down: bfloat16 [4, 1408, 2048], P('expert', 'dp', 'tensor'), may hold values from -0.15625 to 0.15625
Outputs:
- layer_out: bfloat16 [2048, 2048], P(('groups', 'expert', 'dp'), 'tensor'), parts along dimension 0
- grad_tokens: bfloat16 [2048, 2048], P(('groups', 'expert', 'dp'), 'tensor'), parts along dimension 0
- grad_probs: float32 [2048, 2], P(('groups', 'expert', 'dp')), parts along dimension 0
There are 2 independent parts, one for each index of `groups`. A program takes and returns all parts, laid end to end along the dimension named above; an argument that names none is the same for every part. Nothing has to cross between parts.
Inputs may be any that keep to these rules, and one draw needn't show every extreme that they name: `expert_ids`: each token names 2 different experts. Among the 128 tokens of one index of expert and dp (aligned blocks of 128 rows), no expert is named more than 96 times, a bound that some block reaches.
All inputs are finite; a program needn't handle non-finite values.
Results may differ from a plain program's by a relative error of at most 0.015.
Values may be sent and summed in bfloat16 or wider, within the bound.
No kernel may reach another device: no remote copies, remote signals or barrier semaphores. Data moves between devices by JAX's collectives and lax.ppermute only.
A program may use at most 64 MiB of HBM per device.

v0:
```python
import jax
import jax.numpy as jnp
from jax import lax
from jax.sharding import PartitionSpec as P


def local(tokens, cotangent, expert_ids, gate_probs, w_gate, w_up, w_down):
    tok_count, half_width = tokens.shape
    top_count = expert_ids.shape[1]
    experts_here = lax.axis_size("expert")
    capacity = 3 * tok_count * top_count // (2 * experts_here)
    recv_rows = experts_here * capacity
    flat_ids = expert_ids.reshape(-1)
    onehot = (flat_ids[:, None] == jnp.arange(experts_here, dtype=jnp.int32)[None, :]).astype(
        jnp.int32
    )
    position = jnp.sum((jnp.cumsum(onehot, axis=0) - onehot) * onehot, axis=1)
    target = flat_ids * capacity + position
    dispatch = (jnp.arange(recv_rows, dtype=jnp.int32)[:, None] == target[None, :]).astype(
        jnp.bfloat16
    )
    dispatch_tok = jnp.sum(dispatch.reshape(recv_rows, tok_count, top_count), axis=2)
    scaled = (
        gate_probs.reshape(-1, 1) * jnp.repeat(cotangent, top_count, axis=0).astype(jnp.float32)
    ).astype(jnp.bfloat16)
    send_cot = jnp.dot(dispatch, scaled, preferred_element_type=jnp.float32).astype(jnp.bfloat16)
    send_cot = send_cot.reshape(experts_here, capacity, half_width)
    features = lax.all_gather(tokens, "tensor", axis=1, tiled=True)
    send_tok = jnp.dot(dispatch_tok, features, preferred_element_type=jnp.float32).astype(
        jnp.bfloat16
    )
    send_tok = send_tok.reshape(experts_here, capacity, features.shape[1])
    recv_tok, recv_cot = (
        lax.all_to_all(send_tok, "expert", split_axis=0, concat_axis=0, tiled=True),
        lax.all_to_all(send_cot, "expert", split_axis=0, concat_axis=0, tiled=True),
    )
    full_width = recv_tok.shape[2]
    gathered = (
        lax.all_gather(w_gate, "dp", axis=1, tiled=True),
        lax.all_gather(w_up, "dp", axis=1, tiled=True),
        lax.all_gather(w_down, "dp", axis=1, tiled=True),
    )
    gate_full = gathered[0][0]
    up_full = gathered[1][0]
    down_full = gathered[2][0]
    compact_tok = recv_tok.reshape(recv_rows, full_width)
    compact_cot = recv_cot.reshape(recv_rows, half_width)

    def run_rows(section_fn, inputs):
        return section_fn(*inputs)

    def spread(buffer):
        return buffer.reshape(experts_here, capacity, buffer.shape[1])

    def front_half(row_block):
        gate_act = jnp.dot(row_block, gate_full, preferred_element_type=jnp.float32)
        up_act = jnp.dot(row_block, up_full, preferred_element_type=jnp.float32)
        sigmoid_g = jax.nn.sigmoid(gate_act)
        hidden = (gate_act * sigmoid_g * up_act).astype(jnp.bfloat16)
        return (gate_act, up_act, hidden)

    gate_buf, up_buf, hidden_buf = run_rows(front_half, (compact_tok,))
    hidden_all = lax.all_gather(hidden_buf, "tensor", axis=1, tiled=True)

    def down_rows(row_block):
        return (
            jnp.dot(row_block, down_full, preferred_element_type=jnp.float32).astype(jnp.bfloat16),
        )

    expert_out = run_rows(down_rows, (hidden_all,))[0]
    returned = lax.all_to_all(spread(expert_out), "expert", split_axis=0, concat_axis=0, tiled=True)
    contract_last = (((1,), (1,)), ((), ()))

    def cot_rows(row_block):
        partial_value = lax.dot_general(
            row_block, down_full, contract_last, preferred_element_type=jnp.float32
        )
        return (partial_value.astype(jnp.bfloat16),)

    hidden_part = run_rows(cot_rows, (compact_cot,))[0]
    hidden_grad = lax.psum_scatter(
        lax.optimization_barrier(hidden_part).astype(jnp.float32).astype(jnp.bfloat16),
        "tensor",
        scatter_dimension=1,
        tiled=True,
    ).astype(jnp.float32)

    def grad_rows(gate_act, up_act, grad_hidden):
        sigmoid_g = jax.nn.sigmoid(gate_act)
        gate_grad = (
            grad_hidden * up_act * sigmoid_g * (1.0 + gate_act * (1.0 - sigmoid_g))
        ).astype(jnp.bfloat16)
        up_grad = (grad_hidden * gate_act * sigmoid_g).astype(jnp.bfloat16)
        partial_value = lax.dot_general(
            gate_grad, gate_full, contract_last, preferred_element_type=jnp.float32
        )
        partial_value = partial_value + lax.dot_general(
            up_grad, up_full, contract_last, preferred_element_type=jnp.float32
        )
        return (partial_value.astype(jnp.bfloat16),)

    slot_part = run_rows(grad_rows, (gate_buf, up_buf, hidden_grad))[0]
    slot_grad = lax.psum_scatter(
        lax.optimization_barrier(slot_part).astype(jnp.float32).astype(jnp.bfloat16),
        "tensor",
        scatter_dimension=1,
        tiled=True,
    )
    grad_back = lax.all_to_all(spread(slot_grad), "expert", split_axis=0, concat_axis=0, tiled=True)

    def to_slots(buffer):
        flat_rows = buffer.reshape(recv_rows, buffer.shape[2])
        slots = lax.dot_general(
            dispatch, flat_rows, (((0,), (0,)), ((), ())), preferred_element_type=jnp.float32
        )
        return slots.reshape(tok_count, top_count, buffer.shape[2])

    out_slots = to_slots(returned)
    layer_out = jnp.sum(gate_probs[:, :, None] * out_slots, axis=1).astype(jnp.bfloat16)
    prob_part = jnp.sum(out_slots * cotangent[:, None, :].astype(jnp.float32), axis=2)
    grad_probs = lax.psum(prob_part, "tensor")
    grad_tokens = jnp.sum(to_slots(grad_back), axis=1).astype(jnp.bfloat16)
    return (layer_out, grad_tokens, grad_probs)


def solution(mesh):
    in_specs = (
        P(("groups", "expert", "dp"), "tensor"),
        P(("groups", "expert", "dp"), "tensor"),
        P(("groups", "expert", "dp"), None),
        P(("groups", "expert", "dp"), None),
        P("expert", "dp", "tensor"),
        P("expert", "dp", "tensor"),
        P("expert", "dp", "tensor"),
    )
    out_specs = (
        P(("groups", "expert", "dp"), "tensor"),
        P(("groups", "expert", "dp"), "tensor"),
        P(("groups", "expert", "dp"), None),
    )
    return jax.shard_map(local, mesh=mesh, in_specs=in_specs, out_specs=out_specs, check_vma=False)
```

profile of v0, /device:TPU:0, one launch (start us, length us, event | category | flops | bytes accessed | tf_op | source)
XLA Modules:
  0.0 223.8 jit_solution(6356749942504009901)
XLA Ops:
  7.2 0.7 all-gather.11.cloned.1.call-update
  8.0 0.7 all-gather.5.cloned.1.call-update
  8.7 0.7 all-gather.7.cloned.1.call-update
  9.5 0.1 eq.65
  9.7 0.1 reshape.115
  9.8 1.2 reduce-window.6
  11.5 0.3 broadcast_in_dim.2.clone
  11.8 0.7 convert_element_type.70
  12.8 1.4 convolution_convert_fusion.1
  14.1 6.3 %all-to-all-start.2 = ((bf16[4,96,1024]{2,1,0:T(8,128)(2,1)}), bf16[4,96,1024]{2,1,0:T(8,128)(2,1)S(1)}, u32[]{:S(2)}, u32[]{:S(2)}) async-start(bf16[4,96,1024]{2,1,0:T(8,128)(2,1)} %bitcast.10), calls=%async_computation.2 | async-start | bytes 1572864 | tf_op jit(solution)/shard_map/all_to_all | solution.py:35
  20.7 2.2 all_gather.15
  22.9 1.8 convolution_convert_fusion
  24.7 15.9 %all-to-all-done.2 = bf16[4,96,1024]{2,1,0:T(8,128)(2,1)S(1)} async-done(((bf16[4,96,1024]{2,1,0:T(8,128)(2,1)}), bf16[4,96,1024]{2,1,0:T(8,128)(2,1)S(1)}, u32[]{:S(2)}, u32[]{:S(2)}) %all-to-all-start.2) | async-done | bytes 786464 | tf_op jit(solution)/shard_map/all_to_all | solution.py:35
  40.6 3.6 %all-to-all-start = ((bf16[4,96,2048]{2,1,0:T(8,128)(2,1)}), bf16[4,96,2048]{2,1,0:T(8,128)(2,1)S(1)}, u32[]{:S(2)}, u32[]{:S(2)}) async-start(bf16[4,96,2048]{2,1,0:T(8,128)(2,1)} %bitcast.2), calls=%async_computation | async-start | bytes 3145728 | tf_op jit(solution)/shard_map/all_to_all | solution.py:34
  44.2 10.1 %all-gather.11.cloned.1.call-done = bf16[1,1408,1024]{2,1,0:T(8,128)(2,1)} async-done(((bf16[1,704,1024]{2,1,0:T(8,128)(2,1)}), bf16[1,1408,1024]{2,1,0:T(8,128)(2,1)}) %all-gather.11.cloned.1.call-update) | async-done | bytes 2883600 | tf_op jit(solution)/shard_map/all_gather | solution.py:41
  54.3 4.5 %fusion.12 = bf16[384,1408]{0,1:T(8,128)(2,1)} fusion(bf16[384,1024]{1,0:T(8,128)(2,1)S(1)} %bitcast.65, bf16[1,1408,1024]{2,1,0:T(8,128)(2,1)} %all-gather.11.cloned.1.call-done), kind=kOutput, calls=%fused_computation.13 | convolution fusion | flops 1107836928 | bytes 4751360 | tf_op jit(solution)/shard_map/dot_general | solution.py:75
  58.8 21.7 %all-to-all-done = bf16[4,96,2048]{2,1,0:T(8,128)(2,1)S(1)} async-done(((bf16[4,96,2048]{2,1,0:T(8,128)(2,1)}), bf16[4,96,2048]{2,1,0:T(8,128)(2,1)S(1)}, u32[]{:S(2)}, u32[]{:S(2)}) %all-to-all-start) | async-done | bytes 1572896 | tf_op jit(solution)/shard_map/all_to_all | solution.py:34
  80.6 17.2 %all-gather.5.cloned.1.call-done = bf16[1,2048,704]{1,2,0:T(8,128)(2,1)} async-done(((bf16[1,1024,704]{1,2,0:T(8,128)(2,1)}), bf16[1,2048,704]{1,2,0:T(8,128)(2,1)}) %all-gather.5.cloned.1.call-update) | async-done | bytes 2883600 | tf_op jit(solution)/shard_map/all_gather | solution.py:39
  97.8 3.5 %fusion.10 = f32[384,704]{0,1:T(8,128)S(1)} fusion(bf16[384,2048]{1,0:T(8,128)(2,1)S(1)} %bitcast.62, bf16[1,2048,704]{1,2,0:T(8,128)(2,1)} %all-gather.5.cloned.1.call-done), kind=kOutput, calls=%fused_computation.11 | convolution fusion | flops 1107296256 | bytes 5537792 | tf_op jit(solution)/shard_map/dot_general | solution.py:56
  101.3 40.1 %all-gather.7.cloned.1.call-done = bf16[1,2048,704]{1,2,0:T(8,128)(2,1)} async-done(((bf16[1,1024,704]{1,2,0:T(8,128)(2,1)}), bf16[1,2048,704]{1,2,0:T(8,128)(2,1)}) %all-gather.7.cloned.1.call-update) | async-done | bytes 2883600 | tf_op jit(solution)/shard_map/all_gather | solution.py:40
  141.4 4.7 %multiply_convert_fusion = (bf16[384,704]{0,1:T(8,128)(2,1)}, f32[384,704]{0,1:T(8,128)}) fusion(f32[384,704]{0,1:T(8,128)S(1)} %fusion.10, bf16[384,2048]{1,0:T(8,128)(2,1)S(1)} %bitcast.63, bf16[1,2048,704]{1,2,0:T(8,128)(2,1)} %all-gather.7.cloned.1.call-done), kind=kOutput, calls=%fused_computation.25 | convolution fusion | flops 1108918272 | bytes 7159808 | tf_op jit(solution)/shard_map/dot_general | solution.py:57
  146.2 5.9 %reduce-scatter.3.cloned.1.call-done = bf16[384,704]{0,1:T(8,128)(2,1)} async-done(((bf16[384,1408]{0,1:T(8,128)(2,1)}), bf16[384,704]{0,1:T(8,128)(2,1)}) %reduce-scatter.3.cloned.1.call-update) | async-done | bytes 540688 | tf_op jit(solution)/shard_map/reduce_scatter | solution.py:81
  152.1 3.9 %fusion.4 = f32[384,2048]{1,0:T(8,128)S(1)} fusion(bf16[1,2048,704]{1,2,0:T(8,128)(2,1)} %all-gather.7.cloned.1.call-done, f32[384,704]{0,1:T(8,128)} %copy-done.1, bf16[384,704]{0,1:T(8,128)(2,1)} %reduce-scatter.3.cloned.1.call-done), kind=kOutput, calls=%fused_computation.5 | convolution fusion | flops 1109188608 | bytes 7651328 | tf_op jit(solution)/shard_map/dot_general | solution.py:97
  156.1 2.9 %add_convert_fusion = bf16[384,2048]{1,0:T(8,128)(2,1)} fusion(f32[384,2048]{1,0:T(8,128)S(1)} %fusion.4, bf16[1,2048,704]{1,2,0:T(8,128)(2,1)S(1)} %copy-done, f32[384,704]{0,1:T(8,128)S(1)} %copy-done.3, bf16[384,704]{0,1:T(8,128)(2,1)S(1)} %copy-done.5, f32[384,704]{0,1:T(8,128)S(1)} %copy-done.2), kind=kOutput, calls=%fused_computation | convolution fusion | flops 1111842816 | bytes 10305536 | tf_op jit(solution)/shard_map/dot_general | solution.py:94
  159.0 4.8 %all-gather.9.cloned.1.call-done = bf16[384,1408]{0,1:T(8,128)(2,1)} async-done(((bf16[384,704]{0,1:T(8,128)(2,1)}), bf16[384,1408]{0,1:T(8,128)(2,1)}) %all-gather.9.cloned.1.call-update) | async-done | bytes 1081360 | tf_op jit(solution)/shard_map/all_gather | solution.py:63
  163.8 3.6 %fusion.17 = bf16[384,1024]{1,0:T(8,128)(2,1)S(1)} fusion(bf16[384,1408]{0,1:T(8,128)(2,1)} %all-gather.9.cloned.1.call-done, bf16[1,1408,1024]{2,1,0:T(8,128)(2,1)} %all-gather.11.cloned.1.call-done), kind=kOutput, calls=%fused_computation.15 | convolution fusion | flops 1107689472 | bytes 4751360 | tf_op jit(solution)/shard_map/dot_general | solution.py:67
  167.3 25.3 %all_to_all.20 = bf16[4,96,1024]{2,1,0:T(8,128)(2,1)S(1)} all-to-all(bf16[4,96,1024]{2,1,0:T(8,128)(2,1)S(1)} %bitcast.68), channel_id=1, replica_groups=mesh['groups'=2,'expert'=4,'dp'=2,'tensor'=2] {'expert'}, dimensions={0} | all-to-all | bytes 1572864 | tf_op jit(solution)/shard_map/all_to_all | solution.py:71
  192.6 3.5 %all-to-all-start.3 = ((bf16[4,96,1024]{2,1,0:T(8,128)(2,1)}), bf16[4,96,1024]{2,1,0:T(8,128)(2,1)S(1)}, u32[]{:S(2)}, u32[]{:S(2)}) async-start(bf16[4,96,1024]{2,1,0:T(8,128)(2,1)} %bitcast.64), calls=%async_computation.5 | async-start | bytes 1572864 | tf_op jit(solution)/shard_map/all_to_all | solution.py:109
  196.4 1.3 multiply_reduce_fusion
  197.7 3.0 %psum.7 = f32[128,2]{0,1:T(2,128)} all-reduce(f32[128,2]{0,1:T(2,128)S(1)} %get-tuple-element.3), channel_id=1, replica_groups=mesh['groups'=2,'expert'=4,'dp'=2,'tensor'=2] {'tensor'}, use_global_device_ids=true, to_apply=%region_9.10 | all-reduce | flops 256 | bytes 2048 | tf_op jit(solution)/shard_map/psum | solution.py:121
  200.7 15.2 %all-to-all-done.3 = bf16[4,96,1024]{2,1,0:T(8,128)(2,1)S(1)} async-done(((bf16[4,96,1024]{2,1,0:T(8,128)(2,1)}), bf16[4,96,1024]{2,1,0:T(8,128)(2,1)S(1)}, u32[]{:S(2)}, u32[]{:S(2)}) %all-to-all-start.3) | async-done | bytes 786464 | tf_op jit(solution)/shard_map/all_to_all | solution.py:109
  215.8 1.1 convolution_reduce_fusion
  (47 shorter events, 1.7 us)
Async XLA Ops:
  7.2 47.1 %all-gather.11.cloned.1.call-start = ((), (), s32[]{:S(2)}) async-start(), calls=%async_computation.9 | async-start | bytes 4325376 | tf_op jit(solution)/shard_map/all_gather | solution.py:41
  7.9 1.5 copy-start.7
  7.9 3.6 %copy-start.4 = (bf16[128,1024]{1,0:T(8,128)(2,1)S(1)}, bf16[128,1024]{1,0:T(8,128)(2,1)}, u32[]{:S(2)}) copy-start(bf16[128,1024]{1,0:T(8,128)(2,1)} %param.8) | copy-start | bytes 786436
  7.9 89.9 %all-gather.5.cloned.1.call-start = ((), (), s32[]{:S(2)}) async-start(), calls=%async_computation.6 | async-start | bytes 4325376 | tf_op jit(solution)/shard_map/all_gather | solution.py:39
  8.7 132.7 %all-gather.7.cloned.1.call-start = ((), (), s32[]{:S(2)}) async-start(), calls=%async_computation.7 | async-start | bytes 4325376 | tf_op jit(solution)/shard_map/all_gather | solution.py:40
  11.5 1.0 copy-start.8
  12.8 8.0 %copy-start.6 = (bf16[128,1024]{1,0:T(8,128)(2,1)S(1)}, bf16[128,1024]{1,0:T(8,128)(2,1)}, u32[]{:S(2)}) copy-start(bf16[128,1024]{1,0:T(8,128)(2,1)} %param.7) | copy-start | bytes 786436
  14.1 26.4 %all-to-all-start.2 = ((bf16[4,96,1024]{2,1,0:T(8,128)(2,1)}), bf16[4,96,1024]{2,1,0:T(8,128)(2,1)S(1)}, u32[]{:S(2)}, u32[]{:S(2)}) async-start(bf16[4,96,1024]{2,1,0:T(8,128)(2,1)} %bitcast.10), calls=%async_computation.2 | async-start | bytes 1572864 | tf_op jit(solution)/shard_map/all_to_all | solution.py:35
  40.6 40.0 %all-to-all-start = ((bf16[4,96,2048]{2,1,0:T(8,128)(2,1)}), bf16[4,96,2048]{2,1,0:T(8,128)(2,1)S(1)}, u32[]{:S(2)}, u32[]{:S(2)}) async-start(bf16[4,96,2048]{2,1,0:T(8,128)(2,1)} %bitcast.2), calls=%async_computation | async-start | bytes 3145728 | tf_op jit(solution)/shard_map/all_to_all | solution.py:34
  44.1 108.0 %reduce-scatter.3.cloned.1.call-start = ((), (), s32[]{:S(2)}) async-start(), calls=%async_computation.10 | async-start | bytes 1622016 | tf_op jit(solution)/shard_map/reduce_scatter | solution.py:81
  58.8 105.0 %all-gather.9.cloned.1.call-start = ((), (), s32[]{:S(2)}) async-start(), calls=%async_computation.8 | async-start | bytes 1622016 | tf_op jit(solution)/shard_map/all_gather | solution.py:63
  101.3 44.8 %copy-start.1 = (f32[384,704]{0,1:T(8,128)}, f32[384,704]{0,1:T(8,128)S(1)}, u32[]{:S(2)}) copy-start(f32[384,704]{0,1:T(8,128)S(1)} %fusion.10) | copy-start | bytes 3244036
  146.1 9.9 %copy-start = (bf16[1,2048,704]{1,2,0:T(8,128)(2,1)S(1)}, bf16[1,2048,704]{1,2,0:T(8,128)(2,1)}, u32[]{:S(2)}) copy-start(bf16[1,2048,704]{1,2,0:T(8,128)(2,1)} %all-gather.5.cloned.1.call-done) | copy-start | bytes 8650756
  146.1 46.5 %reduce-scatter.5.cloned.1.call-start = ((), (), s32[]{:S(2)}) async-start(), calls=%async_computation.11 | async-start | bytes 2359296 | tf_op jit(solution)/shard_map/reduce_scatter | solution.py:103
  152.1 4.0 %copy-start.2 = (f32[384,704]{0,1:T(8,128)S(1)}, f32[384,704]{0,1:T(8,128)}, u32[]{:S(2)}) copy-start(f32[384,704]{0,1:T(8,128)} %copy-done.1) | copy-start | bytes 3244036
  152.1 4.0 %copy-start.3 = (f32[384,704]{0,1:T(8,128)S(1)}, f32[384,704]{0,1:T(8,128)}, u32[]{:S(2)}) copy-start(f32[384,704]{0,1:T(8,128)} %get-tuple-element.6) | copy-start | bytes 3244036
  152.1 4.0 %copy-start.5 = (bf16[384,704]{0,1:T(8,128)(2,1)S(1)}, bf16[384,704]{0,1:T(8,128)(2,1)}, u32[]{:S(2)}) copy-start(bf16[384,704]{0,1:T(8,128)(2,1)} %reduce-scatter.3.cloned.1.call-done) | copy-start | bytes 1622020
  192.6 23.2 %all-to-all-start.3 = ((bf16[4,96,1024]{2,1,0:T(8,128)(2,1)}), bf16[4,96,1024]{2,1,0:T(8,128)(2,1)S(1)}, u32[]{:S(2)}, u32[]{:S(2)}) async-start(bf16[4,96,1024]{2,1,0:T(8,128)(2,1)} %bitcast.64), calls=%async_computation.5 | async-start | bytes 1572864 | tf_op jit(solution)/shard_map/all_to_all | solution.py:109
Sparse Core Ops, SparseCore 0:
  9.5 44.6 all-gather.10
  55.8 41.9 all-gather.4
  99.4 41.9 all-gather.6
  143.5 8.5 reduce-scatter.2
  153.5 10.2 all-gather.8
  165.9 10.1 reduce-scatter.4
where the time goes:
time: 224 us
  waiting for transfers between devices  133 us (59%)
  blocking collectives  30.4 us (14%)
  matrix products  28.6 us (13%)
  between operations  14.3 us (6%)
  starting transfers between devices  13.6 us (6%)
  local copies, waits for them, and re-layouts  2.26 us (1%)
    all_gather x1, waiting for transfers between devices, local(): lax.all_gather(w_up, 'dp', axis=1, tiled=True)  40.1 us
    all_to_all x1, blocking collectives, local(): lax.all_to_all(spread(expert_out), 'expert', split_axis=0, concat_axis=0,...  25.3 us
    all_to_all x1, waiting for transfers between devices, local(): lax.all_to_all(send_tok, 'expert', split_axis=0, concat_axis=0, tiled=True)  21.7 us
    all_gather x1, waiting for transfers between devices, local(): lax.all_gather(w_gate, 'dp', axis=1, tiled=True)  17.2 us
    all_to_all x1, waiting for transfers between devices, local(): lax.all_to_all(send_cot, 'expert', split_axis=0, concat_axis=0, tiled=True)  15.9 us
    all_to_all x1, waiting for transfers between devices, local(): lax.all_to_all(spread(slot_grad), 'expert', split_axis=0, concat_axis=0,...  15.2 us
    all_gather x1, waiting for transfers between devices, local(): lax.all_gather(w_down, 'dp', axis=1, tiled=True)  10.1 us
    all_to_all x1, starting transfers between devices, local(): lax.all_to_all(send_cot, 'expert', split_axis=0, concat_axis=0, tiled=True)  6.32 us
  transfers between devices with their start and end apart: 9, of which 8 were waited for; matrix products, arithmetic and copies ran while one was open for 14% of the time, Pallas kernels for 0%

commit v1 on v0

v1 whole, which is shorter than its diff:
```python
import functools

import jax
import jax.numpy as jnp
from jax import lax
from jax.experimental import pallas as pl
from jax.experimental.pallas import tpu as pltpu
from jax.sharding import PartitionSpec as P

F32 = jnp.float32
BF16 = jnp.bfloat16
LAST = (((1,), (1,)), ((), ()))
ROW_CHUNKS = 2
COL_CHUNKS = 2
SHIFTED_UP_TO = 8

VMEM = pl.BlockSpec(memory_space=pltpu.VMEM)
SMEM = pl.BlockSpec(memory_space=pltpu.SMEM)
ANY = pl.BlockSpec(memory_space=pl.ANY)


def dot(a, b, dims=(((1,), (0,)), ((), ()))):
    return lax.dot_general(a, b, dims, preferred_element_type=F32)


def call(kernel, out_shape, args, spaces, scratch=(), flops=0, moved=0):
    return pl.pallas_call(
        kernel,
        out_shape=out_shape,
        in_specs=spaces,
        out_specs=jax.tree.map(lambda _: VMEM, out_shape),
        scratch_shapes=list(scratch),
        compiler_params=pltpu.CompilerParams(vmem_limit_bytes=40 * 1024 * 1024),
        cost_estimate=pl.CostEstimate(flops=flops, bytes_accessed=moved, transcendentals=0),
    )(*args)


def shape(rows, cols, dtype):
    return jax.ShapeDtypeStruct((rows, cols), dtype)


def padded(size):
    return -(-size // 128) * 128


class Copies:
    def __init__(self, sems):
        self.sems, self.all = sems, []

    def add(self, src, dst):
        copy = pltpu.make_async_copy(src, dst, self.sems.at[len(self.all)])
        copy.start()
        self.all.append(copy)

    def wait(self):
        for copy in self.all:
            copy.wait()


def before(index, step, size):
    moved = index - step
    return jnp.where(moved < 0, moved + size, moved)


def rows_at(start, size):
    return pl.ds(pl.multiple_of(start, 16), size)


def cols_at(start, size):
    return pl.ds(pl.multiple_of(start, 128), size)


def route_kernel(experts, cap, blocks, where, ids_t, probs_t, ids, tok, cot, *outs):
    tok_out, cot_out = outs[:blocks], outs[blocks : 2 * blocks]
    first_out, second_out = outs[2 * blocks :]
    rows, count = experts * cap, tok.shape[0]
    base = where[1] if blocks > 1 else 0

    def places(axis):
        row = lax.broadcasted_iota(jnp.int32, (rows, 1) if axis == 0 else (1, rows), axis)
        block = jnp.zeros_like(row)
        for later in range(1, experts):
            block = block + (row >= later * cap).astype(jnp.int32)
        expert = block + base
        expert = jnp.where(expert >= experts, expert - experts, expert)
        return expert, (row - block * cap).astype(F32)

    side = (lax.broadcasted_iota(jnp.int32, (count, count), 0), lax.broadcasted_iota(jnp.int32, (count, count), 1))
    expert, slot = places(0)
    first = ids_t[0:1, :] == expert
    named = first | (ids_t[1:2, :] == expert)
    earlier = dot(named.astype(F32).astype(BF16), (side[0] < side[1]).astype(F32).astype(BF16))
    chosen = named & (earlier == slot)
    weight = jnp.where(chosen, jnp.where(first, probs_t[0:1, :], probs_t[1:2, :]), 0.0)
    weight = jnp.sum(weight, axis=1, keepdims=True)
    chosen = chosen.astype(F32).astype(BF16)
    tok_rows = dot(chosen, tok[...]).astype(BF16)
    cot_rows = (weight * dot(chosen, cot[...])).astype(BF16)
    each = rows // blocks
    for i in range(blocks):
        tok_out[i][...] = tok_rows[i * each : (i + 1) * each]
        cot_out[i][...] = cot_rows[i * each : (i + 1) * each]

    expert, slot = places(1)
    first = ids[:, 0:1] == expert
    second = ids[:, 1:2] == expert
    named = (first | second).astype(F32).astype(BF16)
    earlier = dot((side[1] < side[0]).astype(F32).astype(BF16), named)
    here = earlier == slot
    first_out[...] = (first & here).astype(F32).astype(BF16)
    second_out[...] = (second & here).astype(F32).astype(BF16)


def fill_tokens(where, copies, own, other, dst):
    half = own[0].shape[1]
    at = 0
    for i in range(len(own)):
        rows = own[i].shape[0]
        copies.add(own[i], dst.at[pl.ds(at, rows), cols_at(where[3] * half, half)])
        copies.add(other[i], dst.at[pl.ds(at, rows), cols_at((1 - where[3]) * half, half)])
        at += rows


def fill_wide(where, copies, sizes, own, pieces, dst):
    n_dp, n_groups = sizes
    units, feats = own.shape
    copies.add(own, dst.at[pl.ds(0, units), cols_at(where[2] * feats, feats)])
    share = units // n_groups
    for (chunk, step, turn), ref in pieces:
        start = before(where[0], turn, n_groups) * share + chunk * ref.shape[0]
        feat = before(where[2], step, n_dp) * feats
        copies.add(ref, dst.at[rows_at(start, ref.shape[0]), cols_at(feat, feats)])
    if dst.shape[0] > units:
        dst[units:, :] = jnp.zeros((dst.shape[0] - units, dst.shape[1]), dst.dtype)


def fill_down(where, copies, sizes, own, pieces, parts, dst):
    n_dp, n_groups = sizes
    units, feats = own.shape
    half = dst.shape[0] // 2
    per_half = n_dp // 2
    share = feats // n_groups
    width = share // COL_CHUNKS

    def start(index):
        upper = (index >= per_half).astype(jnp.int32)
        return upper * half + (index - upper * per_half) * units

    for place, part in enumerate(parts):
        for group in range(n_groups):
            copies.add(
                own.at[:, pl.ds(group * share + part * width, width)],
                dst.at[rows_at(start(where[2]), units), pl.ds((place * n_groups + group) * width, width)],
            )
    for (part, step, turn), ref in pieces:
        col = (parts.index(part) * n_groups + before(where[0], turn, n_groups)) * width
        copies.add(ref, dst.at[rows_at(start(before(where[2], step, n_dp)), units), cols_at(col, width)])
    used = per_half * units
    if half > used:
        for side in range(2):
            dst[side * half + used : (side + 1) * half, :] = jnp.zeros((half - used, dst.shape[1]), dst.dtype)


def front_kernel(sizes, keys, blocks, final, where, *refs):
    own_tok, other_tok, refs = refs[:blocks], refs[blocks : 2 * blocks], refs[2 * blocks :]
    own, refs = refs[0], refs[1:]
    pieces, refs = list(zip(keys, refs[: len(keys)])), refs[len(keys) :]
    if final:
        gate, up_out, hidden_out, tok, weight, sems = refs
    else:
        gate_out, tok, weight, sems = refs
    copies = Copies(sems)
    fill_tokens(where, copies, own_tok, other_tok, tok)
    fill_wide(where, copies, sizes, own, pieces, weight)
    copies.wait()
    value = dot(tok[...], weight[...], LAST)
    if final:
        up_out[...] = value
        hidden_out[...] = (gate[...] * jax.nn.sigmoid(gate[...]) * value).astype(BF16)
    else:
        gate_out[...] = value


def out_kernel(sizes, keys, part, where, own_hidden, other_hidden, own, *refs):
    pieces, refs = list(zip(keys, refs[: len(keys)])), refs[len(keys) :]
    outs, (hidden, weight, sems) = refs[:-3], refs[-3:]
    copies = Copies(sems)
    half = own_hidden.shape[1]
    copies.add(own_hidden, hidden.at[:, cols_at(where[3] * half, half)])
    copies.add(other_hidden, hidden.at[:, cols_at((1 - where[3]) * half, half)])
    fill_down(where, copies, sizes, own, pieces, [part], weight)
    copies.wait()
    value = dot(hidden[...], weight[...]).astype(BF16)
    each = outs[0].shape[0]
    for i, out in enumerate(outs):
        out[...] = value[i * each : (i + 1) * each]


def cot_kernel(sizes, keys, blocks, where, *refs):
    cots, own, refs = refs[:blocks], refs[blocks], refs[blocks + 1 :]
    pieces, refs = list(zip(keys, refs[: len(keys)])), refs[len(keys) :]
    keep, send, cot, weight, sems = refs
    copies = Copies(sems)
    share = own.shape[1] // sizes[1]
    width = share // COL_CHUNKS
    at = 0
    for ref in cots:
        rows = ref.shape[0]
        for part in range(COL_CHUNKS):
            for group in range(sizes[1]):
                copies.add(
                    ref.at[:, pl.ds(group * share + part * width, width)],
                    cot.at[pl.ds(at, rows), pl.ds((part * sizes[1] + group) * width, width)],
                )
        at += rows
    fill_down(where, copies, sizes, own, pieces, list(range(COL_CHUNKS)), weight)
    copies.wait()
    half = weight.shape[0] // 2
    send[...] = dot(cot[...], weight[rows_at((1 - where[3]) * half, half), :], LAST).astype(BF16)
    keep[...] = dot(cot[...], weight[rows_at(where[3] * half, half), :], LAST)


def grad_kernel(sizes, gate_keys, up_keys, where, gate, up, kept, received, own_gate, own_up, *refs):
    gate_pieces = list(zip(gate_keys, refs[: len(gate_keys)]))
    refs = refs[len(gate_keys) :]
    up_pieces = list(zip(up_keys, refs[: len(up_keys)]))
    keep, send, w_gate, w_up, sems = refs[len(up_keys) :]
    copies = Copies(sems)
    fill_wide(where, copies, sizes, own_gate, gate_pieces, w_gate)
    fill_wide(where, copies, sizes, own_up, up_pieces, w_up)
    gate_act = gate[...]
    sigmoid_g = jax.nn.sigmoid(gate_act)
    hidden_grad = kept[...] + received[...].astype(F32)
    gate_grad = (hidden_grad * up[...] * sigmoid_g * (1.0 + gate_act * (1.0 - sigmoid_g))).astype(BF16)
    up_grad = (hidden_grad * gate_act * sigmoid_g).astype(BF16)
    copies.wait()
    half = keep.shape[1]
    mine, theirs = cols_at(where[3] * half, half), cols_at((1 - where[3]) * half, half)
    send[...] = (dot(gate_grad, w_gate[:, theirs]) + dot(up_grad, w_up[:, theirs])).astype(BF16)
    keep[...] = dot(gate_grad, w_gate[:, mine]) + dot(up_grad, w_up[:, mine])


def add_kernel(kept, received, *outs):
    value = (kept[...] + received[...].astype(F32)).astype(BF16)
    each = outs[0].shape[0]
    for i, out in enumerate(outs):
        out[...] = value[i * each : (i + 1) * each]


def layer_kernel(blocks, n_groups, first, second, probs, cot, *refs):
    out, prob_out = refs[-2:]
    share = cot.shape[1] // n_groups
    width = share // COL_CHUNKS
    sums = [0.0, 0.0]
    for part in range(COL_CHUNKS):
        back = jnp.concatenate([r[...] for r in refs[part * blocks : (part + 1) * blocks]], axis=0)
        slots = dot(first[...], back), dot(second[...], back)
        total = probs[:, 0:1] * slots[0] + probs[:, 1:2] * slots[1]
        for group in range(n_groups):
            cols = pl.ds(group * share + part * width, width)
            out[:, cols] = total[:, group * width : (group + 1) * width].astype(BF16)
            cot_here = cot[:, cols].astype(F32)
            for k in range(2):
                held = slots[k][:, group * width : (group + 1) * width] * cot_here
                sums[k] = sums[k] + jnp.sum(held, axis=1, keepdims=True)
    lane = lax.broadcasted_iota(jnp.int32, prob_out.shape, 1)
    prob_out[...] = jnp.where(lane == 0, sums[0], sums[1])


def token_kernel(first, second, *refs):
    back = jnp.concatenate([r[...] for r in refs[:-1]], axis=0)
    refs[-1][...] = dot(first[...] + second[...], back).astype(BF16)


def shift(value, axis, step):
    size = lax.axis_size(axis)
    return lax.ppermute(value, axis, [(i, (i + step) % size) for i in range(size)])


def local(tokens, cotangent, expert_ids, gate_probs, w_gate, w_up, w_down):
    count, half = tokens.shape
    experts, n_dp, n_groups = lax.axis_size("expert"), lax.axis_size("dp"), lax.axis_size("groups")
    sizes = (n_dp, n_groups)
    cap = 3 * count * expert_ids.shape[1] // (2 * experts)
    rows = experts * cap
    shifted = experts <= SHIFTED_UP_TO
    blocks = experts if shifted else 1
    each = rows // blocks
    group = lax.axis_index("groups")
    where = jnp.stack([lax.axis_index(a) for a in ("groups", "expert", "dp", "tensor")]).astype(jnp.int32)

    def exchange(parts, sign):
        if shifted:
            return [parts[0]] + [shift(parts[s], "expert", sign * s) for s in range(1, experts)]
        whole = parts[0].reshape(experts, cap, -1)
        whole = lax.all_to_all(whole, "expert", split_axis=0, concat_axis=0, tiled=True)
        return [whole.reshape(rows, -1)]

    def gather(weight, axis, chunks):
        share = weight.shape[axis] // n_groups
        size = share // chunks
        keys, pieces = [], []
        for chunk in range(chunks):
            mine = lax.dynamic_slice_in_dim(weight, group * share + chunk * size, size, axis)
            for step in range(1, n_dp):
                came = shift(mine, "dp", step)
                for turn in range(n_groups):
                    keys.append((chunk, step, turn))
                    pieces.append(shift(came, "groups", turn) if turn else came)
        return keys, pieces

    gate_t, up_t, down = jnp.swapaxes(w_gate[0], 0, 1), jnp.swapaxes(w_up[0], 0, 1), w_down[0]
    units = gate_t.shape[0]
    wide = padded(units)
    feats = n_dp * gate_t.shape[1]
    gate_keys, gate_pieces = gather(gate_t, 0, ROW_CHUNKS)

    routed = call(
        functools.partial(route_kernel, experts, cap, blocks),
        [shape(each, half, BF16)] * (2 * blocks) + [shape(count, rows, BF16)] * 2,
        (where, expert_ids.T, gate_probs.T, expert_ids, tokens, cotangent),
        [SMEM] + [VMEM] * 5,
        flops=4 * rows * count * half,
        moved=4 * count * half + 4 * rows * half,
    )
    first, second = routed[2 * blocks :]
    tok = exchange(routed[:blocks], 1)
    cot = exchange(routed[blocks : 2 * blocks], 1)
    other_tok = [shift(part, "tensor", 1) for part in tok]
    up_keys, up_pieces = gather(up_t, 0, ROW_CHUNKS)
    down_keys, down_pieces = gather(down, 1, COL_CHUNKS)

    def front(own, keys, pieces, gate):
        final = gate is not None
        act = shape(rows, wide, F32)
        return call(
            functools.partial(front_kernel, sizes, keys, blocks, final),
            [act, shape(rows, wide, BF16)] if final else [act],
            (where, *tok, *other_tok, own, *pieces, *([gate] if final else [])),
            [SMEM] + [ANY] * (2 * blocks + 1 + len(pieces)) + [VMEM] * final,
            [
                pltpu.VMEM((rows, feats), BF16),
                pltpu.VMEM((wide, feats), BF16),
                pltpu.SemaphoreType.DMA((2 * blocks + 1 + len(pieces),)),
            ],
            flops=2 * rows * feats * units,
            moved=2 * feats * (rows + units),
        )

    (gate,) = front(gate_t, gate_keys, gate_pieces, None)
    up, hidden = front(up_t, up_keys, up_pieces, gate)
    other_hidden = shift(hidden, "tensor", 1)

    width = half // n_groups // COL_CHUNKS
    back = []
    for part in range(COL_CHUNKS):
        picked = [i for i, key in enumerate(down_keys) if key[0] == part]
        outs = call(
            functools.partial(out_kernel, sizes, [down_keys[i] for i in picked], part),
            [shape(each, n_groups * width, BF16)] * blocks,
            (where, hidden, other_hidden, down, *[down_pieces[i] for i in picked]),
            [SMEM] + [ANY] * (3 + len(picked)),
            [
                pltpu.VMEM((rows, 2 * wide), BF16),
                pltpu.VMEM((2 * wide, n_groups * width), BF16),
                pltpu.SemaphoreType.DMA((2 + n_groups + len(picked),)),
            ],
            flops=4 * rows * units * n_groups * width,
            moved=4 * units * n_groups * width,
        )
        back.append(exchange(outs, -1))

    kept, sent = call(
        functools.partial(cot_kernel, sizes, down_keys, blocks),
        [shape(rows, wide, F32), shape(rows, wide, BF16)],
        (where, *cot, down, *down_pieces),
        [SMEM] + [ANY] * (blocks + 1 + len(down_pieces)),
        [
            pltpu.VMEM((rows, half), BF16),
            pltpu.VMEM((2 * wide, half), BF16),
            pltpu.SemaphoreType.DMA((COL_CHUNKS * n_groups * (blocks + 1) + len(down_pieces),)),
        ],
        flops=4 * rows * half * units,
        moved=4 * half * units,
    )
    received = shift(sent, "tensor", 1)
    kept, sent = call(
        functools.partial(grad_kernel, sizes, gate_keys, up_keys),
        [shape(rows, half, F32), shape(rows, half, BF16)],
        (where, gate, up, kept, received, gate_t, up_t, *gate_pieces, *up_pieces),
        [SMEM] + [VMEM] * 4 + [ANY] * (2 + len(gate_pieces) + len(up_pieces)),
        [
            pltpu.VMEM((wide, feats), BF16),
            pltpu.VMEM((wide, feats), BF16),
            pltpu.SemaphoreType.DMA((2 + len(gate_pieces) + len(up_pieces),)),
        ],
        flops=4 * rows * feats * units,
        moved=4 * feats * units,
    )
    received = shift(sent, "tensor", 1)
    slots = call(add_kernel, [shape(each, half, BF16)] * blocks, (kept, received), [VMEM] * 2, moved=8 * rows * half)
    grad_back = exchange(slots, -1)

    layer_out, prob_part = call(
        functools.partial(layer_kernel, blocks, n_groups),
        [shape(count, half, BF16), shape(count, expert_ids.shape[1], F32)],
        (first, second, gate_probs, cotangent, *[part for parts in back for part in parts]),
        [VMEM] * (4 + COL_CHUNKS * blocks),
        flops=4 * count * rows * half,
        moved=2 * rows * half,
    )
    grad_probs = prob_part + shift(prob_part, "tensor", 1)
    (grad_tokens,) = call(
        token_kernel,
        [shape(count, half, BF16)],
        (first, second, *grad_back),
        [VMEM] * (2 + blocks),
        flops=2 * count * rows * half,
        moved=2 * rows * half,
    )
    return (layer_out, grad_tokens, grad_probs)


def solution(mesh):
    by_token = ("groups", "expert", "dp")
    weight = P("expert", "dp", "tensor")
    in_specs = (P(by_token, "tensor"), P(by_token, "tensor"), P(by_token, None), P(by_token, None)) + (weight,) * 3
    out_specs = (P(by_token, "tensor"), P(by_token, "tensor"), P(by_token, None))
    return jax.shard_map(local, mesh=mesh, in_specs=in_specs, out_specs=out_specs, check_vma=False)
```

time: 224 us -> 162 us (0.72)
  waiting for transfers between devices: 133 us -> 74.4 us
  starting transfers between devices: 13.6 us -> 50.2 us
  blocking collectives: 30.4 us -> 0 us
  matrix products: 28.6 us -> 0 us
  Pallas kernels: 0 us -> 24.8 us
  between operations: 14.3 us -> 0.85 us
  local copies, waits for them, and re-layouts: 2.26 us -> 11.1 us
    ppermute x0 -> x35, waiting for transfers between devices: none -> 74.4 us  [shift(): lax.ppermute(value, axis, [(i, (i + step) % size) for i in range(size)])]
    all_gather x4 -> x0, waiting for transfers between devices: 72.2 us -> none  [the longest x1 40.1 us: local(): lax.all_gather(w_up, 'dp', axis=1, tiled=True)]
    all_to_all x3 -> x0, waiting for transfers between devices: 52.7 us -> none  [the longest x1 21.7 us: local(): lax.all_to_all(send_tok, 'expert', split_axis=0, concat_axis=0, tiled=True)]
    ppermute x0 -> x35, starting transfers between devices: none -> 50.2 us  [shift(): lax.ppermute(value, axis, [(i, (i + step) % size) for i in range(size)])]
    dot_general x10 -> x0, matrix products: 28.6 us -> none  [the longest x1 4.71 us: front_half(): up_act = jnp.dot(row_block, up_full, preferred_element_type=jnp.float32)]
    all_to_all x1 -> x0, blocking collectives: 25.3 us -> none  [local(): lax.all_to_all(spread(expert_out), 'expert', split_axis=0, concat_axis=0,...]
    pallas_call x0 -> x10, Pallas kernels: none -> 24.8 us  [call(): pl.pallas_call(kernel, out_shape=out_shape, in_specs=spaces, out_specs=ja...]
    all_to_all x3 -> x0, starting transfers between devices: 13.4 us -> none  [the longest x1 6.32 us: local(): lax.all_to_all(send_cot, 'expert', split_axis=0, concat_axis=0, tiled=True)]
  transfers between devices with their start and end apart: 9 -> 35, of which waited for: 8 -> 16; matrix products, arithmetic and copies ran while one was open for 14% -> 2% of each run, Pallas kernels for 0% -> 10%
where the time goes in v1:
time: 162 us; the launch traced here: 161 us
  waiting for transfers between devices  74.4 us (46%)
  starting transfers between devices  50.2 us (31%)
  Pallas kernels  24.8 us (15%)
  local copies, waits for them, and re-layouts  11.1 us (7%)
    ppermute x35, waiting for transfers between devices, shift(): lax.ppermute(value, axis, [(i, (i + step) % size) for i in range(size)])  74.4 us
    ppermute x35, starting transfers between devices, shift(): lax.ppermute(value, axis, [(i, (i + step) % size) for i in range(size)])  50.2 us
    pallas_call x10, Pallas kernels, call(): pl.pallas_call(kernel, out_shape=out_shape, in_specs=spaces, out_specs=ja...  24.8 us
    unnamed x41, local copies, waits for them, and re-layouts  8.93 us
  transfers between devices with their start and end apart: 35, of which 16 were waited for; matrix products, arithmetic and copies ran while one was open for 2% of the time, Pallas kernels for 10%

profile of v1, /device:TPU:0, one launch (start us, length us, event | category | flops | bytes accessed | tf_op | source)
XLA Modules:
  0.0 161.5 jit_solution(4661539000079268818)
XLA Ops:
  4.9 1.8 %shard_map.94 = (bf16[96,1024]{1,0:T(8,128)(2,1)S(1)}, bf16[96,1024]{1,0:T(8,128)(2,1)}, bf16[96,1024]{1,0:T(8,128)(2,1)}, bf16[96,1024]{1,0:T(8,128)(2,1)}, bf1...) custom-call(s32[4]{0:T(128)S(1)} %pad_add_fusion.where, ...), custom_call_target="tpu_custom_call" | custom-call | flops 201326592 | bytes 2097152 | tf_op jit(solution)/shard_map/pallas_call | solution.py:27
  10.6 3.0 %collective-permute-start = (bf16[96,1024]{1,0:T(8,128)(2,1)}, bf16[96,1024]{1,0:T(8,128)(2,1)S(1)}, u32[]{:S(2)}, u32[]{:S(2)}) collective-permute-start(bf16[96,1024]{1,0:T(8,128)(2,1)} %get-tuple-element.36), channel_id=1, source_target_pairs={{0,4},{4,8},{8,12},{12,0},{1,5},{5,9},{9,13},{13,1},{2,6},{6,10},{... | collective-permute-start | bytes 589832 | tf_op jit(solution)/shard_map/ppermute | solution.py:277
  13.7 2.6 %collective-permute-start.1 = (bf16[96,1024]{1,0:T(8,128)(2,1)}, bf16[96,1024]{1,0:T(8,128)(2,1)S(1)}, u32[]{:S(2)}, u32[]{:S(2)}) collective-permute-start(bf16[96,1024]{1,0:T(8,128)(2,1)} %get-tuple-element.37), channel_id=1, source_target_pairs={{0,8},{4,12},{8,0},{12,4},{1,9},{5,13},{9,1},{13,5},{2,10},{6,14},... | collective-permute-start | bytes 589832 | tf_op jit(solution)/shard_map/ppermute | solution.py:277
  17.6 2.1 %dynamic-slice_bitcast_fusion = (bf16[704,256]{1,0:T(8,128)(2,1)}, bf16[704,256]{1,0:T(8,128)(2,1)}) fusion(bf16[1,704,1024]{2,1,0:T(8,128)(2,1)} %param.13, s32[]{:T(128)S(6)} %select_n.17, s32[]{:T(128)S(6)} %select_n.16), kind=kLoop, calls=%fused_computation | loop fusion | bytes 1441800 | tf_op jit(solution)/shard_map/dynamic_slice | solution.py:304
  21.8 1.7 %collective-permute-start.16 = (bf16[704,256]{1,0:T(8,128)(2,1)}, bf16[704,256]{1,0:T(8,128)(2,1)}, u32[]{:S(2)}, u32[]{:S(2)}) collective-permute-start(bf16[704,256]{1,0:T(8,128)(2,1)} %get-tuple-element.67), channel_id=1, source_target_pairs={{0,2},{2,0},{1,3},{3,1},{4,6},{6,4},{5,7},{7,5},{8,10},{10,8},{9,1... | collective-permute-start | bytes 1081352 | tf_op jit(solution)/shard_map/ppermute | solution.py:277
  23.5 5.9 %collective-permute-done.1.refs_2_ = bf16[96,1024]{1,0:T(8,128)(2,1)S(1)} collective-permute-done((bf16[96,1024]{1,0:T(8,128)(2,1)}, bf16[96,1024]{1,0:T(8,128)(2,1)S(1)}, u32[]{:S(2)}, u32[]{:S(2)}) %collective-permute-start.1) | collective-permute-done | bytes 196640 | tf_op jit(solution)/shard_map/ppermute | solution.py:277
  29.3 3.3 %collective-permute-start.26 = (bf16[96,1024]{1,0:T(8,128)(2,1)}, bf16[96,1024]{1,0:T(8,128)(2,1)S(1)}, u32[]{:S(2)}, u32[]{:S(2)}) collective-permute-start(bf16[96,1024]{1,0:T(8,128)(2,1)} %copy-done.16), channel_id=1, source_target_pairs={{0,4},{4,8},{8,12},{12,0},{1,5},{5,9},{9,13},{13,1},{2,6},{6,10},{... | collective-permute-start | bytes 589832 | tf_op jit(solution)/shard_map/ppermute | solution.py:277
  32.6 3.3 %collective-permute-start.27 = (bf16[96,1024]{1,0:T(8,128)(2,1)}, bf16[96,1024]{1,0:T(8,128)(2,1)S(1)}, u32[]{:S(2)}, u32[]{:S(2)}) collective-permute-start(bf16[96,1024]{1,0:T(8,128)(2,1)} %copy-done.15), channel_id=1, source_target_pairs={{0,8},{4,12},{8,0},{12,4},{1,9},{5,13},{9,1},{13,5},{2,10},{6,14},... | collective-permute-start | bytes 589832 | tf_op jit(solution)/shard_map/ppermute | solution.py:277
  36.0 1.6 collective-permute-start.11
  37.5 3.9 %collective-permute-done.26.refs_1_ = bf16[96,1024]{1,0:T(8,128)(2,1)S(1)} collective-permute-done((bf16[96,1024]{1,0:T(8,128)(2,1)}, bf16[96,1024]{1,0:T(8,128)(2,1)S(1)}, u32[]{:S(2)}, u32[]{:S(2)}) %collective-permute-start.26) | collective-permute-done | bytes 196640 | tf_op jit(solution)/shard_map/ppermute | solution.py:277
  42.3 5.5 %collective-permute-done.27.refs_2_ = bf16[96,1024]{1,0:T(8,128)(2,1)S(1)} collective-permute-done((bf16[96,1024]{1,0:T(8,128)(2,1)}, bf16[96,1024]{1,0:T(8,128)(2,1)S(1)}, u32[]{:S(2)}, u32[]{:S(2)}) %collective-permute-start.27) | collective-permute-done | bytes 196640 | tf_op jit(solution)/shard_map/ppermute | solution.py:277
  53.6 5.6 %collective-permute-done.13.refs_11_.refs_2_ = bf16[176,1024]{1,0:T(8,128)(2,1)S(1)} collective-permute-done((bf16[176,1024]{1,0:T(8,128)(2,1)S(1)}, bf16[176,1024]{1,0:T(8,128)(2,1)S(1)}, u32[]{:S(2)}, u32[]{:S(2)}) %collective-permute-start.13) | collective-permute-done | bytes 360480 | tf_op jit(solution)/shard_map/ppermute | solution.py:277
  59.1 1.8 %collective-permute-done.22.refs_1_.refs_8_ = bf16[704,256]{1,0:T(8,128)(2,1)S(1)} collective-permute-done((bf16[704,256]{1,0:T(8,128)(2,1)}, bf16[704,256]{1,0:T(8,128)(2,1)S(1)}, u32[]{:S(2)}, u32[]{:S(2)}) %collective-permute-start.22) | collective-permute-done | bytes 360480 | tf_op jit(solution)/shard_map/ppermute | solution.py:277
  60.9 6.3 %collective-permute-done.17.refs_1_.refs_6_ = bf16[704,256]{1,0:T(8,128)(2,1)S(1)} collective-permute-done((bf16[704,256]{1,0:T(8,128)(2,1)}, bf16[704,256]{1,0:T(8,128)(2,1)S(1)}, u32[]{:S(2)}, u32[]{:S(2)}) %collective-permute-start.17) | collective-permute-done | bytes 360480 | tf_op jit(solution)/shard_map/ppermute | solution.py:277
  67.3 3.7 %shard_map.100 = (f32[384,768]{1,0:T(8,128)S(1)}, bf16[384,768]{1,0:T(8,128)(2,1)S(1)}) custom-call(s32[4]{0:T(128)S(1)} %pad_add_fusion.where, bf16[96,1024]{1,0:T(8,128)(2,1)S(1)} %copy-done.18, bf16[96,1024]{1,0:T(8,128)(2,1)S(1)} %collective-permute-done.26.refs_1_, bf16[96,1024]{1,0:T(8,128)(2,1)S(1)} %collective-permute-done.27.refs_2_, ...), custom_call_target="tpu_custom_call" | custom-call | flops 1107296256 | bytes 2883584 | tf_op jit(solution)/shard_map/pallas_call | solution.py:27
  71.5 2.0 %collective-permute-done.7.refs_9_.refs_4_ = bf16[176,1024]{1,0:T(8,128)(2,1)S(1)} collective-permute-done((bf16[176,1024]{1,0:T(8,128)(2,1)S(1)}, bf16[176,1024]{1,0:T(8,128)(2,1)S(1)}, u32[]{:S(2)}, u32[]{:S(2)}) %collective-permute-start.7) | collective-permute-done | bytes 360480 | tf_op jit(solution)/shard_map/ppermute | solution.py:277
  75.6 1.5 collective-permute-start.10
  77.6 7.3 %collective-permute-done.12.refs_10_.refs_1_ = bf16[176,1024]{1,0:T(8,128)(2,1)S(1)} collective-permute-done((bf16[176,1024]{1,0:T(8,128)(2,1)S(1)}, bf16[176,1024]{1,0:T(8,128)(2,1)S(1)}, u32[]{:S(2)}, u32[]{:S(2)}) %collective-permute-start.12) | collective-permute-done | bytes 360480 | tf_op jit(solution)/shard_map/ppermute | solution.py:277
  84.9 7.7 %collective-permute-done.14.refs_12_.refs_3_ = bf16[176,1024]{1,0:T(8,128)(2,1)S(1)} collective-permute-done((bf16[176,1024]{1,0:T(8,128)(2,1)S(1)}, bf16[176,1024]{1,0:T(8,128)(2,1)S(1)}, u32[]{:S(2)}, u32[]{:S(2)}) %collective-permute-start.14) | collective-permute-done | bytes 360480 | tf_op jit(solution)/shard_map/ppermute | solution.py:277
  92.6 3.2 %shard_map.95.refs_13_.gate = f32[384,768]{1,0:T(8,128)S(1)} custom-call(s32[4]{0:T(128)S(1)} %pad_add_fusion.where, bf16[96,1024]{1,0:T(8,128)(2,1)S(1)} %get-tuple-element.35.refs_0_, bf16[96,1024]{1,0:T(8,128)(2,1)S(1)} %collective-permute-done.refs_1_, bf16[96,1024]{1,0:T(8,128)(2,1)S(1)} %collective-permute-done.1.refs_2_, ...), custom_call_target="tpu_custom_call" | custom-call | flops 1107296256 | bytes 4456448 | tf_op jit(solution)/shard_map/pallas_call | solution.py:27
  95.8 4.5 %collective-permute-done.10.refs_12_.refs_7_ = bf16[176,1024]{1,0:T(8,128)(2,1)S(1)} collective-permute-done((bf16[176,1024]{1,0:T(8,128)(2,1)S(1)}, bf16[176,1024]{1,0:T(8,128)(2,1)S(1)}, u32[]{:S(2)}, u32[]{:S(2)}) %collective-permute-start.10) | collective-permute-done | bytes 360480 | tf_op jit(solution)/shard_map/ppermute | solution.py:277
  100.3 5.7 %collective-permute-done.8.refs_10_.refs_5_ = bf16[176,1024]{1,0:T(8,128)(2,1)S(1)} collective-permute-done((bf16[176,1024]{1,0:T(8,128)(2,1)S(1)}, bf16[176,1024]{1,0:T(8,128)(2,1)S(1)}, u32[]{:S(2)}, u32[]{:S(2)}) %collective-permute-start.8) | collective-permute-done | bytes 360480 | tf_op jit(solution)/shard_map/ppermute | solution.py:277
  106.1 3.2 %shard_map.96 = (f32[384,768]{1,0:T(8,128)S(1)}, bf16[384,768]{1,0:T(8,128)(2,1)S(1)}) custom-call(s32[4]{0:T(128)S(1)} %pad_add_fusion.where, bf16[96,1024]{1,0:T(8,128)(2,1)S(1)} %get-tuple-element.35.refs_0_, bf16[96,1024]{1,0:T(8,128)(2,1)S(1)} %collective-permute-done.refs_1_, bf16[96,1024]{1,0:T(8,128)(2,1)S(1)} %collective-permute-done.1.refs_2_, ...), custom_call_target="tpu_custom_call" | custom-call | flops 1107296256 | bytes 4456448 | tf_op jit(solution)/shard_map/pallas_call | solution.py:27
  109.3 5.5 %shard_map.101 = (f32[384,1024]{1,0:T(8,128)S(1)}, bf16[384,1024]{1,0:T(8,128)(2,1)S(1)}) custom-call(s32[4]{0:T(128)S(1)} %pad_add_fusion.where, f32[384,768]{1,0:T(8,128)S(1)} %shard_map.95.refs_13_.gate, f32[384,768]{1,0:T(8,128)S(1)} %get-tuple-element.49.up, f32[384,768]{1,0:T(8,128)S(1)} %get-tuple-element.54.kept, ...), custom_call_target="tpu_custom_call" | custom-call | flops 2214592512 | bytes 5767168 | tf_op jit(solution)/shard_map/pallas_call | solution.py:27
  115.4 2.6 %collective-permute-done.15.other_hidden = bf16[384,768]{1,0:T(8,128)(2,1)S(1)} collective-permute-done((bf16[384,768]{1,0:T(8,128)(2,1)S(1)}, bf16[384,768]{1,0:T(8,128)(2,1)S(1)}, u32[]{:S(2)}, u32[]{:S(2)}) %collective-permute-start.15) | collective-permute-done | bytes 589856 | tf_op jit(solution)/shard_map/ppermute | solution.py:277
  118.0 2.6 %shard_map.98 = (bf16[96,512]{1,0:T(8,128)(2,1)S(1)}, bf16[96,512]{1,0:T(8,128)(2,1)S(1)}, bf16[96,512]{1,0:T(8,128)(2,1)S(1)}, bf16[96,512]{1,0:T(8,128)(2,1)S(1)}) custom-call(s32[4]{0:T(128)S(1)} %pad_add_fusion.where, bf16[384,768]{1,0:T(8,128)(2,1)S(1)} %get-tuple-element.39.own_hidden, bf16[384,768]{1,0:T(8,128)(2,1)S(1)} %collective-permute-done.15.other_hidden, ...), custom_call_target="tpu_custom_call" | custom-call | flops 553648128 | bytes 1441792 | tf_op jit(solution)/shard_map/pallas_call | solution.py:27
  120.6 2.0 %collective-permute-start.23 = (bf16[96,512]{1,0:T(8,128)(2,1)S(1)}, bf16[96,512]{1,0:T(8,128)(2,1)S(1)}, u32[]{:S(2)}, u32[]{:S(2)}) collective-permute-start(bf16[96,512]{1,0:T(8,128)(2,1)S(1)} %get-tuple-element.45), channel_id=1, source_target_pairs={{0,12},{4,0},{8,4},{12,8},{1,13},{5,1},{9,5},{13,9},{2,14},{6,2},{... | collective-permute-start | bytes 294920 | tf_op jit(solution)/shard_map/ppermute | solution.py:277
  123.3 2.6 %shard_map.97 = (bf16[96,512]{1,0:T(8,128)(2,1)S(1)}, bf16[96,512]{1,0:T(8,128)(2,1)S(1)}, bf16[96,512]{1,0:T(8,128)(2,1)S(1)}, bf16[96,512]{1,0:T(8,128)(2,1)S(1)}) custom-call(s32[4]{0:T(128)S(1)} %pad_add_fusion.where, bf16[384,768]{1,0:T(8,128)(2,1)S(1)} %get-tuple-element.39.own_hidden, bf16[384,768]{1,0:T(8,128)(2,1)S(1)} %collective-permute-done.15.other_hidden, ...), custom_call_target="tpu_custom_call" | custom-call | flops 553648128 | bytes 1441792 | tf_op jit(solution)/shard_map/pallas_call | solution.py:27
  125.9 3.2 %collective-permute-start.18 = (bf16[96,512]{1,0:T(8,128)(2,1)S(1)}, bf16[96,512]{1,0:T(8,128)(2,1)S(1)}, u32[]{:S(2)}, u32[]{:S(2)}) collective-permute-start(bf16[96,512]{1,0:T(8,128)(2,1)S(1)} %get-tuple-element.41), channel_id=1, source_target_pairs={{0,12},{4,0},{8,4},{12,8},{1,13},{5,1},{9,5},{13,9},{2,14},{6,2},{... | collective-permute-start | bytes 294920 | tf_op jit(solution)/shard_map/ppermute | solution.py:277
  130.5 1.6 %collective-permute-done.24.refs_6_ = bf16[96,512]{1,0:T(8,128)(2,1)S(1)} collective-permute-done((bf16[96,512]{1,0:T(8,128)(2,1)S(1)}, bf16[96,512]{1,0:T(8,128)(2,1)S(1)}, u32[]{:S(2)}, u32[]{:S(2)}) %collective-permute-start.24) | collective-permute-done | bytes 98336 | tf_op jit(solution)/shard_map/ppermute | solution.py:277
  132.5 12.7 %collective-permute-start.19 = (bf16[96,512]{1,0:T(8,128)(2,1)S(1)}, bf16[96,512]{1,0:T(8,128)(2,1)S(1)}, u32[]{:S(2)}, u32[]{:S(2)}) collective-permute-start(bf16[96,512]{1,0:T(8,128)(2,1)S(1)} %get-tuple-element.42), channel_id=1, source_target_pairs={{0,8},{4,12},{8,0},{12,4},{1,9},{5,13},{9,1},{13,5},{2,10},{6,14},... | collective-permute-start | bytes 294920 | tf_op jit(solution)/shard_map/ppermute | solution.py:277
  145.3 12.0 %collective-permute-done.19.refs_2_ = bf16[96,512]{1,0:T(8,128)(2,1)S(1)} collective-permute-done((bf16[96,512]{1,0:T(8,128)(2,1)S(1)}, bf16[96,512]{1,0:T(8,128)(2,1)S(1)}, u32[]{:S(2)}, u32[]{:S(2)}) %collective-permute-start.19) | collective-permute-done | bytes 98336 | tf_op jit(solution)/shard_map/ppermute | solution.py:277
  (94 shorter events, 28.5 us)
Async XLA Ops:
  10.6 11.1 %collective-permute-start = (bf16[96,1024]{1,0:T(8,128)(2,1)}, bf16[96,1024]{1,0:T(8,128)(2,1)S(1)}, u32[]{:S(2)}, u32[]{:S(2)}) collective-permute-start(bf16[96,1024]{1,0:T(8,128)(2,1)} %get-tuple-element.36), channel_id=1, source_target_pairs={{0,4},{4,8},{8,12},{12,0},{1,5},{5,9},{9,13},{13,1},{2,6},{6,10},{... | collective-permute-start | bytes 589832 | tf_op jit(solution)/shard_map/ppermute | solution.py:277
  13.7 15.7 %collective-permute-start.1 = (bf16[96,1024]{1,0:T(8,128)(2,1)}, bf16[96,1024]{1,0:T(8,128)(2,1)S(1)}, u32[]{:S(2)}, u32[]{:S(2)}) collective-permute-start(bf16[96,1024]{1,0:T(8,128)(2,1)} %get-tuple-element.37), channel_id=1, source_target_pairs={{0,8},{4,12},{8,0},{12,4},{1,9},{5,13},{9,1},{13,5},{2,10},{6,14},... | collective-permute-start | bytes 589832 | tf_op jit(solution)/shard_map/ppermute | solution.py:277
  16.3 16.4 %collective-permute-start.2 = (bf16[96,1024]{1,0:T(8,128)(2,1)}, bf16[96,1024]{1,0:T(8,128)(2,1)}, u32[]{:S(2)}, u32[]{:S(2)}) collective-permute-start(bf16[96,1024]{1,0:T(8,128)(2,1)} %get-tuple-element.38), channel_id=1, source_target_pairs={{0,12},{4,0},{8,4},{12,8},{1,13},{5,1},{9,5},{13,9},{2,14},{6,2},{... | collective-permute-start | bytes 589832 | tf_op jit(solution)/shard_map/ppermute | solution.py:277
  17.6 18.4 %collective-permute-start.3 = (bf16[96,1024]{1,0:T(8,128)(2,1)S(1)}, bf16[96,1024]{1,0:T(8,128)(2,1)}, u32[]{:S(2)}, u32[]{:S(2)}) collective-permute-start(bf16[96,1024]{1,0:T(8,128)(2,1)S(1)} %get-tuple-element.35.refs_0_), channel_id=1, source_target_pairs={{0,1},{1,0},{2,3},{3,2},{4,5},{5,4},{6,7},{7,6},{8,9},{9,8},{10,11... | collective-permute-start | bytes 589832 | tf_op jit(solution)/shard_map/ppermute | solution.py:277
  19.7 29.6 %collective-permute-start.21 = (bf16[704,256]{1,0:T(8,128)(2,1)}, bf16[704,256]{1,0:T(8,128)(2,1)}, u32[]{:S(2)}, u32[]{:S(2)}) collective-permute-start(bf16[704,256]{1,0:T(8,128)(2,1)} %get-tuple-element.66), channel_id=1, source_target_pairs={{0,2},{2,0},{1,3},{3,1},{4,6},{6,4},{5,7},{7,5},{8,10},{10,8},{9,1... | collective-permute-start | bytes 1081352 | tf_op jit(solution)/shard_map/ppermute | solution.py:277
  21.8 29.1 %collective-permute-start.16 = (bf16[704,256]{1,0:T(8,128)(2,1)}, bf16[704,256]{1,0:T(8,128)(2,1)}, u32[]{:S(2)}, u32[]{:S(2)}) collective-permute-start(bf16[704,256]{1,0:T(8,128)(2,1)} %get-tuple-element.67), channel_id=1, source_target_pairs={{0,2},{2,0},{1,3},{3,1},{4,6},{6,4},{5,7},{7,5},{8,10},{10,8},{9,1... | collective-permute-start | bytes 1081352 | tf_op jit(solution)/shard_map/ppermute | solution.py:277
  29.3 12.1 %collective-permute-start.26 = (bf16[96,1024]{1,0:T(8,128)(2,1)}, bf16[96,1024]{1,0:T(8,128)(2,1)S(1)}, u32[]{:S(2)}, u32[]{:S(2)}) collective-permute-start(bf16[96,1024]{1,0:T(8,128)(2,1)} %copy-done.16), channel_id=1, source_target_pairs={{0,4},{4,8},{8,12},{12,0},{1,5},{5,9},{9,13},{13,1},{2,6},{6,10},{... | collective-permute-start | bytes 589832 | tf_op jit(solution)/shard_map/ppermute | solution.py:277
  32.6 15.2 %collective-permute-start.27 = (bf16[96,1024]{1,0:T(8,128)(2,1)}, bf16[96,1024]{1,0:T(8,128)(2,1)S(1)}, u32[]{:S(2)}, u32[]{:S(2)}) collective-permute-start(bf16[96,1024]{1,0:T(8,128)(2,1)} %copy-done.15), channel_id=1, source_target_pairs={{0,8},{4,12},{8,0},{12,4},{1,9},{5,13},{9,1},{13,5},{2,10},{6,14},... | collective-permute-start | bytes 589832 | tf_op jit(solution)/shard_map/ppermute | solution.py:277
  36.0 16.1 %collective-permute-start.11 = (bf16[176,1024]{1,0:T(8,128)(2,1)S(1)}, bf16[176,1024]{1,0:T(8,128)(2,1)S(1)}, u32[]{:S(2)}, u32[]{:S(2)}) collective-permute-start(bf16[176,1024]{1,0:T(8,128)(2,1)S(1)} %get-tuple-element.69), channel_id=1, source_target_pairs={{0,2},{2,0},{1,3},{3,1},{4,6},{6,4},{5,7},{7,5},{8,10},{10,8},{9,1... | collective-permute-start | bytes 1081352 | tf_op jit(solution)/shard_map/ppermute | solution.py:277
  41.4 10.0 %collective-permute-start.28 = (bf16[96,1024]{1,0:T(8,128)(2,1)S(1)}, bf16[96,1024]{1,0:T(8,128)(2,1)S(1)}, u32[]{:S(2)}, u32[]{:S(2)}) collective-permute-start(bf16[96,1024]{1,0:T(8,128)(2,1)S(1)} %copy-done.14), channel_id=1, source_target_pairs={{0,12},{4,0},{8,4},{12,8},{1,13},{5,1},{9,5},{13,9},{2,14},{6,2},{... | collective-permute-start | bytes 589832 | tf_op jit(solution)/shard_map/ppermute | solution.py:277
  47.8 11.3 %collective-permute-start.13 = (bf16[176,1024]{1,0:T(8,128)(2,1)S(1)}, bf16[176,1024]{1,0:T(8,128)(2,1)S(1)}, u32[]{:S(2)}, u32[]{:S(2)}) collective-permute-start(bf16[176,1024]{1,0:T(8,128)(2,1)S(1)} %get-tuple-element.68), channel_id=1, source_target_pairs={{0,2},{2,0},{1,3},{3,1},{4,6},{6,4},{5,7},{7,5},{8,10},{10,8},{9,1... | collective-permute-start | bytes 1081352 | tf_op jit(solution)/shard_map/ppermute | solution.py:277
  49.4 11.5 %collective-permute-start.22 = (bf16[704,256]{1,0:T(8,128)(2,1)}, bf16[704,256]{1,0:T(8,128)(2,1)S(1)}, u32[]{:S(2)}, u32[]{:S(2)}) collective-permute-start(bf16[704,256]{1,0:T(8,128)(2,1)} %collective-permute-done.21.refs_0_.refs_7_), channel_id=1, source_target_pairs={{0,16},{16,0},{1,17},{17,1},{2,18},{18,2},{3,19},{19,3},{4,20},{20... | collective-permute-start | bytes 1081352 | tf_op jit(solution)/shard_map/ppermute | solution.py:277
  50.9 16.4 %collective-permute-start.17 = (bf16[704,256]{1,0:T(8,128)(2,1)}, bf16[704,256]{1,0:T(8,128)(2,1)S(1)}, u32[]{:S(2)}, u32[]{:S(2)}) collective-permute-start(bf16[704,256]{1,0:T(8,128)(2,1)} %collective-permute-done.16.refs_0_.refs_5_), channel_id=1, source_target_pairs={{0,16},{16,0},{1,17},{17,1},{2,18},{18,2},{3,19},{19,3},{4,20},{20... | collective-permute-start | bytes 1081352 | tf_op jit(solution)/shard_map/ppermute | solution.py:277
  51.5 19.5 %collective-permute-start.9 = (bf16[176,1024]{1,0:T(8,128)(2,1)S(1)}, bf16[176,1024]{1,0:T(8,128)(2,1)S(1)}, u32[]{:S(2)}, u32[]{:S(2)}) collective-permute-start(bf16[176,1024]{1,0:T(8,128)(2,1)S(1)} %get-tuple-element.70), channel_id=1, source_target_pairs={{0,2},{2,0},{1,3},{3,1},{4,6},{6,4},{5,7},{7,5},{8,10},{10,8},{9,1... | collective-permute-start | bytes 1081352 | tf_op jit(solution)/shard_map/ppermute | solution.py:277
  52.0 21.5 %collective-permute-start.7 = (bf16[176,1024]{1,0:T(8,128)(2,1)S(1)}, bf16[176,1024]{1,0:T(8,128)(2,1)S(1)}, u32[]{:S(2)}, u32[]{:S(2)}) collective-permute-start(bf16[176,1024]{1,0:T(8,128)(2,1)S(1)} %get-tuple-element.71), channel_id=1, source_target_pairs={{0,2},{2,0},{1,3},{3,1},{4,6},{6,4},{5,7},{7,5},{8,10},{10,8},{9,1... | collective-permute-start | bytes 1081352 | tf_op jit(solution)/shard_map/ppermute | solution.py:277
  59.1 15.9 %collective-permute-start.4 = (bf16[96,1024]{1,0:T(8,128)(2,1)S(1)}, bf16[96,1024]{1,0:T(8,128)(2,1)S(1)}, u32[]{:S(2)}, u32[]{:S(2)}) collective-permute-start(bf16[96,1024]{1,0:T(8,128)(2,1)S(1)} %collective-permute-done.refs_1_), channel_id=1, source_target_pairs={{0,1},{1,0},{2,3},{3,2},{4,5},{5,4},{6,7},{7,6},{8,9},{9,8},{10,11... | collective-permute-start | bytes 589832 | tf_op jit(solution)/shard_map/ppermute | solution.py:277
  60.9 14.7 %collective-permute-start.5 = (bf16[96,1024]{1,0:T(8,128)(2,1)S(1)}, bf16[96,1024]{1,0:T(8,128)(2,1)S(1)}, u32[]{:S(2)}, u32[]{:S(2)}) collective-permute-start(bf16[96,1024]{1,0:T(8,128)(2,1)S(1)} %collective-permute-done.1.refs_2_), channel_id=1, source_target_pairs={{0,1},{1,0},{2,3},{3,2},{4,5},{5,4},{6,7},{7,6},{8,9},{9,8},{10,11... | collective-permute-start | bytes 589832 | tf_op jit(solution)/shard_map/ppermute | solution.py:277
  67.3 9.8 %collective-permute-start.6 = (bf16[96,1024]{1,0:T(8,128)(2,1)}, bf16[96,1024]{1,0:T(8,128)(2,1)S(1)}, u32[]{:S(2)}, u32[]{:S(2)}) collective-permute-start(bf16[96,1024]{1,0:T(8,128)(2,1)} %collective-permute-done.2.refs_3_), channel_id=1, source_target_pairs={{0,1},{1,0},{2,3},{3,2},{4,5},{5,4},{6,7},{7,6},{8,9},{9,8},{10,11... | collective-permute-start | bytes 589832 | tf_op jit(solution)/shard_map/ppermute | solution.py:277
  70.9 38.4 %collective-permute-start.29 = (bf16[384,768]{1,0:T(8,128)(2,1)S(1)}, bf16[384,768]{1,0:T(8,128)(2,1)S(1)}, u32[]{:S(2)}, u32[]{:S(2)}) collective-permute-start(bf16[384,768]{1,0:T(8,128)(2,1)S(1)} %get-tuple-element.55), channel_id=1, source_target_pairs={{0,1},{1,0},{2,3},{3,2},{4,5},{5,4},{6,7},{7,6},{8,9},{9,8},{10,11... | collective-permute-start | bytes 1769480 | tf_op jit(solution)/shard_map/ppermute | solution.py:277
  73.5 11.3 %collective-permute-start.12 = (bf16[176,1024]{1,0:T(8,128)(2,1)S(1)}, bf16[176,1024]{1,0:T(8,128)(2,1)S(1)}, u32[]{:S(2)}, u32[]{:S(2)}) collective-permute-start(bf16[176,1024]{1,0:T(8,128)(2,1)S(1)} %collective-permute-done.11.refs_9_.refs_0_), channel_id=1, source_target_pairs={{0,16},{16,0},{1,17},{17,1},{2,18},{18,2},{3,19},{19,3},{4,20},{20... | collective-permute-start | bytes 1081352 | tf_op jit(solution)/shard_map/ppermute | solution.py:277
  75.1 17.5 %collective-permute-start.14 = (bf16[176,1024]{1,0:T(8,128)(2,1)S(1)}, bf16[176,1024]{1,0:T(8,128)(2,1)S(1)}, u32[]{:S(2)}, u32[]{:S(2)}) collective-permute-start(bf16[176,1024]{1,0:T(8,128)(2,1)S(1)} %collective-permute-done.13.refs_11_.refs_2_), channel_id=1, source_target_pairs={{0,16},{16,0},{1,17},{17,1},{2,18},{18,2},{3,19},{19,3},{4,20},{20... | collective-permute-start | bytes 1081352 | tf_op jit(solution)/shard_map/ppermute | solution.py:277
  75.6 24.8 %collective-permute-start.10 = (bf16[176,1024]{1,0:T(8,128)(2,1)S(1)}, bf16[176,1024]{1,0:T(8,128)(2,1)S(1)}, u32[]{:S(2)}, u32[]{:S(2)}) collective-permute-start(bf16[176,1024]{1,0:T(8,128)(2,1)S(1)} %collective-permute-done.9.refs_11_.refs_6_), channel_id=1, source_target_pairs={{0,16},{16,0},{1,17},{17,1},{2,18},{18,2},{3,19},{19,3},{4,20},{20... | collective-permute-start | bytes 1081352 | tf_op jit(solution)/shard_map/ppermute | solution.py:277
  77.1 29.0 %collective-permute-start.8 = (bf16[176,1024]{1,0:T(8,128)(2,1)S(1)}, bf16[176,1024]{1,0:T(8,128)(2,1)S(1)}, u32[]{:S(2)}, u32[]{:S(2)}) collective-permute-start(bf16[176,1024]{1,0:T(8,128)(2,1)S(1)} %collective-permute-done.7.refs_9_.refs_4_), channel_id=1, source_target_pairs={{0,16},{16,0},{1,17},{17,1},{2,18},{18,2},{3,19},{19,3},{4,20},{20... | collective-permute-start | bytes 1081352 | tf_op jit(solution)/shard_map/ppermute | solution.py:277
  114.8 14.3 %collective-permute-start.30 = (bf16[384,1024]{1,0:T(8,128)(2,1)S(1)}, bf16[384,1024]{1,0:T(8,128)(2,1)S(1)}, u32[]{:S(2)}, u32[]{:S(2)}) collective-permute-start(bf16[384,1024]{1,0:T(8,128)(2,1)S(1)} %get-tuple-element.57), channel_id=1, source_target_pairs={{0,1},{1,0},{2,3},{3,2},{4,5},{5,4},{6,7},{7,6},{8,9},{9,8},{10,11... | collective-permute-start | bytes 2359304 | tf_op jit(solution)/shard_map/ppermute | solution.py:277
  122.6 9.6 %collective-permute-start.24 = (bf16[96,512]{1,0:T(8,128)(2,1)S(1)}, bf16[96,512]{1,0:T(8,128)(2,1)S(1)}, u32[]{:S(2)}, u32[]{:S(2)}) collective-permute-start(bf16[96,512]{1,0:T(8,128)(2,1)S(1)} %get-tuple-element.46), channel_id=1, source_target_pairs={{0,8},{4,12},{8,0},{12,4},{1,9},{5,13},{9,1},{13,5},{2,10},{6,14},... | collective-permute-start | bytes 294920 | tf_op jit(solution)/shard_map/ppermute | solution.py:277
  122.6 9.8 %collective-permute-start.25 = (bf16[96,512]{1,0:T(8,128)(2,1)S(1)}, bf16[96,512]{1,0:T(8,128)(2,1)S(1)}, u32[]{:S(2)}, u32[]{:S(2)}) collective-permute-start(bf16[96,512]{1,0:T(8,128)(2,1)S(1)} %get-tuple-element.47), channel_id=1, source_target_pairs={{0,4},{4,8},{8,12},{12,0},{1,5},{5,9},{9,13},{13,1},{2,6},{6,10},{... | collective-permute-start | bytes 294920 | tf_op jit(solution)/shard_map/ppermute | solution.py:277
  125.9 19.3 %collective-permute-start.18 = (bf16[96,512]{1,0:T(8,128)(2,1)S(1)}, bf16[96,512]{1,0:T(8,128)(2,1)S(1)}, u32[]{:S(2)}, u32[]{:S(2)}) collective-permute-start(bf16[96,512]{1,0:T(8,128)(2,1)S(1)} %get-tuple-element.41), channel_id=1, source_target_pairs={{0,12},{4,0},{8,4},{12,8},{1,13},{5,1},{9,5},{13,9},{2,14},{6,2},{... | collective-permute-start | bytes 294920 | tf_op jit(solution)/shard_map/ppermute | solution.py:277
  129.2 31.2 %collective-permute-start.31 = (bf16[96,1024]{1,0:T(8,128)(2,1)S(1)}, bf16[96,1024]{1,0:T(8,128)(2,1)S(1)}, u32[]{:S(2)}, u32[]{:S(2)}) collective-permute-start(bf16[96,1024]{1,0:T(8,128)(2,1)S(1)} %get-tuple-element.59), channel_id=1, source_target_pairs={{0,12},{4,0},{8,4},{12,8},{1,13},{5,1},{9,5},{13,9},{2,14},{6,2},{... | collective-permute-start | bytes 589832 | tf_op jit(solution)/shard_map/ppermute | solution.py:277
  130.1 30.4 %collective-permute-start.32 = (bf16[96,1024]{1,0:T(8,128)(2,1)S(1)}, bf16[96,1024]{1,0:T(8,128)(2,1)S(1)}, u32[]{:S(2)}, u32[]{:S(2)}) collective-permute-start(bf16[96,1024]{1,0:T(8,128)(2,1)S(1)} %get-tuple-element.60), channel_id=1, source_target_pairs={{0,8},{4,12},{8,0},{12,4},{1,9},{5,13},{9,1},{13,5},{2,10},{6,14},... | collective-permute-start | bytes 589832 | tf_op jit(solution)/shard_map/ppermute | solution.py:277
  132.2 28.3 %collective-permute-start.33 = (bf16[96,1024]{1,0:T(8,128)(2,1)S(1)}, bf16[96,1024]{1,0:T(8,128)(2,1)S(1)}, u32[]{:S(2)}, u32[]{:S(2)}) collective-permute-start(bf16[96,1024]{1,0:T(8,128)(2,1)S(1)} %get-tuple-element.61), channel_id=1, source_target_pairs={{0,4},{4,8},{8,12},{12,0},{1,5},{5,9},{9,13},{13,1},{2,6},{6,10},{... | collective-permute-start | bytes 589832 | tf_op jit(solution)/shard_map/ppermute | solution.py:277
  132.5 24.9 %collective-permute-start.19 = (bf16[96,512]{1,0:T(8,128)(2,1)S(1)}, bf16[96,512]{1,0:T(8,128)(2,1)S(1)}, u32[]{:S(2)}, u32[]{:S(2)}) collective-permute-start(bf16[96,512]{1,0:T(8,128)(2,1)S(1)} %get-tuple-element.42), channel_id=1, source_target_pairs={{0,8},{4,12},{8,0},{12,4},{1,9},{5,13},{9,1},{13,5},{2,10},{6,14},... | collective-permute-start | bytes 294920 | tf_op jit(solution)/shard_map/ppermute | solution.py:277
  145.2 12.2 %collective-permute-start.20 = (bf16[96,512]{1,0:T(8,128)(2,1)S(1)}, bf16[96,512]{1,0:T(8,128)(2,1)S(1)}, u32[]{:S(2)}, u32[]{:S(2)}) collective-permute-start(bf16[96,512]{1,0:T(8,128)(2,1)S(1)} %get-tuple-element.43), channel_id=1, source_target_pairs={{0,4},{4,8},{8,12},{12,0},{1,5},{5,9},{9,13},{13,1},{2,6},{6,10},{... | collective-permute-start | bytes 294920 | tf_op jit(solution)/shard_map/ppermute | solution.py:277
  (22 other events, 291.3 us)

commit v2 on v1

v2 whole, which is shorter than its diff:
```python
import functools

import jax
import jax.numpy as jnp
from jax import lax
from jax.experimental import pallas as pl
from jax.experimental.pallas import tpu as pltpu
from jax.sharding import PartitionSpec as P

F32 = jnp.float32
BF16 = jnp.bfloat16
LAST = (((1,), (1,)), ((), ()))
ROW_CHUNKS = 2
COL_CHUNKS = 2
WHOLE = 60
SHIFTED_UP_TO = 8

VMEM = pl.BlockSpec(memory_space=pltpu.VMEM)
SMEM = pl.BlockSpec(memory_space=pltpu.SMEM)
ANY = pl.BlockSpec(memory_space=pl.ANY)
HBM = pl.BlockSpec(memory_space=pltpu.HBM)


def dot(a, b, dims=(((1,), (0,)), ((), ()))):
    return lax.dot_general(a, b, dims, preferred_element_type=F32)


def call(kernel, out_shape, args, spaces, scratch=(), flops=0, moved=0, outs=VMEM, grant=40):
    return pl.pallas_call(
        kernel,
        out_shape=out_shape,
        in_specs=spaces,
        out_specs=jax.tree.map(lambda _: outs, out_shape),
        scratch_shapes=list(scratch),
        compiler_params=pltpu.CompilerParams(vmem_limit_bytes=grant * 1024 * 1024),
        cost_estimate=pl.CostEstimate(flops=flops, bytes_accessed=moved, transcendentals=0),
    )(*args)


def shape(rows, cols, dtype):
    return jax.ShapeDtypeStruct((rows, cols), dtype)


def padded(size):
    return -(-size // 128) * 128


class Copies:
    def __init__(self, sems):
        self.sems, self.all = sems, []

    def add(self, src, dst):
        copy = pltpu.make_async_copy(src, dst, self.sems.at[len(self.all)])
        copy.start()
        self.all.append(copy)

    def wait(self):
        for copy in self.all:
            copy.wait()


def before(index, step, size):
    moved = index - step
    return jnp.where(moved < 0, moved + size, moved)


def rows_at(start, size):
    return pl.ds(pl.multiple_of(start, 16), size)


def cols_at(start, size):
    return pl.ds(pl.multiple_of(start, 128), size)


def places(experts, cap, blocks, where, ids_t):
    rows, count = experts * cap, ids_t.shape[1]
    row = lax.broadcasted_iota(jnp.int32, (rows, 1), 0)
    block = jnp.zeros_like(row)
    for later in range(1, experts):
        block = block + (row >= later * cap).astype(jnp.int32)
    expert = block + (where[1] if blocks > 1 else 0)
    expert = jnp.where(expert >= experts, expert - experts, expert)
    slot = (row - block * cap).astype(F32)
    first = ids_t[0:1, :] == expert
    second = ids_t[1:2, :] == expert
    before_it = lax.broadcasted_iota(jnp.int32, (count, count), 0) < lax.broadcasted_iota(jnp.int32, (count, count), 1)
    earlier = dot((first | second).astype(F32).astype(BF16), before_it.astype(F32).astype(BF16))
    here = earlier == slot
    return first & here, second & here


def route_kernel(experts, cap, blocks, where, ids_in, probs_in, tok_in, cot_in, *refs):
    tok_out, cot_out = refs[:blocks], refs[blocks : 2 * blocks]
    ids_t, probs_t, tok, cot, sems = refs[2 * blocks :]
    copies = Copies(sems)
    copies.add(ids_in, ids_t)
    copies.add(probs_in, probs_t)
    copies.add(tok_in, tok)
    copies.add(cot_in, cot)
    copies.wait()
    first, second = places(experts, cap, blocks, where, ids_t)
    weight = jnp.where(first, probs_t[0:1, :], jnp.where(second, probs_t[1:2, :], 0.0))
    weight = jnp.sum(weight, axis=1, keepdims=True)
    chosen = (first | second).astype(F32).astype(BF16)
    tok_rows = dot(chosen, tok[...]).astype(BF16)
    cot_rows = (weight * dot(chosen, cot[...])).astype(BF16)
    each = tok_rows.shape[0] // blocks
    for i in range(blocks):
        tok_out[i][...] = tok_rows[i * each : (i + 1) * each]
        cot_out[i][...] = cot_rows[i * each : (i + 1) * each]


def cut_kernel(axis, chunk, n_groups, where, weight, *refs):
    out, sems = refs[-2:]
    share = weight.shape[axis] // n_groups
    start, size = where[0] * share + chunk * out.shape[axis], out.shape[axis]
    copies = Copies(sems)
    copies.add(weight.at[rows_at(start, size), :] if axis == 0 else weight.at[:, cols_at(start, size)], out)
    copies.wait()


def join_kernel(*refs):
    parts, out, sems = refs[:-2], refs[-2], refs[-1]
    copies, at = Copies(sems), 0
    for part in parts:
        copies.add(part, out.at[pl.ds(at, part.shape[0]), :])
        at += part.shape[0]
    copies.wait()


def after_kernel(*refs):
    pass


def after(value, *others):
    return pl.pallas_call(
        after_kernel,
        out_shape=jax.ShapeDtypeStruct(value.shape, value.dtype),
        in_specs=[ANY] * (1 + len(others)),
        out_specs=ANY,
        input_output_aliases={0: 0},
    )(value, *others)


def fill_tokens(where, copies, own, other, dst):
    half = own.shape[1]
    copies.add(own, dst.at[:, cols_at(where[3] * half, half)])
    copies.add(other, dst.at[:, cols_at((1 - where[3]) * half, half)])


def fill_wide(where, copies, sizes, own, pieces, dst):
    n_dp, n_groups = sizes
    units, feats = own.shape
    copies.add(own, dst.at[pl.ds(0, units), cols_at(where[2] * feats, feats)])
    share = units // n_groups
    for (chunk, step, turn), ref in pieces:
        start = before(where[0], turn, n_groups) * share + chunk * ref.shape[0]
        feat = before(where[2], step, n_dp) * feats
        copies.add(ref, dst.at[rows_at(start, ref.shape[0]), cols_at(feat, feats)])
    if dst.shape[0] > units:
        dst[units:, :] = jnp.zeros((dst.shape[0] - units, dst.shape[1]), dst.dtype)


def fill_down(where, copies, sizes, own, pieces, parts, dst):
    n_dp, n_groups = sizes
    units, feats = own.shape
    half = dst.shape[0] // 2
    per_half = n_dp // 2
    share = feats // n_groups
    width = share // COL_CHUNKS

    def start(index):
        upper = (index >= per_half).astype(jnp.int32)
        return upper * half + (index - upper * per_half) * units

    for place, part in enumerate(parts):
        for group in range(n_groups):
            copies.add(
                own.at[:, pl.ds(group * share + part * width, width)],
                dst.at[rows_at(start(where[2]), units), pl.ds((place * n_groups + group) * width, width)],
            )
    for (part, step, turn), ref in pieces:
        col = (parts.index(part) * n_groups + before(where[0], turn, n_groups)) * width
        copies.add(ref, dst.at[rows_at(start(before(where[2], step, n_dp)), units), cols_at(col, width)])
    used = per_half * units
    if half > used:
        for side in range(2):
            dst[side * half + used : (side + 1) * half, :] = jnp.zeros((half - used, dst.shape[1]), dst.dtype)


def front_kernel(sizes, keys, final, where, own_tok, other_tok, own, *refs):
    pieces, refs = list(zip(keys, refs[: len(keys)])), refs[len(keys) :]
    if final:
        gate, (up_out, hidden_out, tok, weight, sems) = refs[0], refs[-5:]
    else:
        gate_out, tok, weight, sems = refs
    copies = Copies(sems)
    fill_tokens(where, copies, own_tok, other_tok, tok)
    fill_wide(where, copies, sizes, own, pieces, weight)
    copies.wait()
    value = dot(tok[...], weight[...], LAST)
    if final:
        up_out[...] = value
        hidden_out[...] = (gate[...] * jax.nn.sigmoid(gate[...]) * value).astype(BF16)
    else:
        gate_out[...] = value


def out_kernel(sizes, keys, part, blocks, where, own_hidden, other_hidden, own, *refs):
    pieces = list(zip(keys, refs[: len(keys)]))
    outs, (hidden, weight, sems) = refs[-3 - blocks : -3], refs[-3:]
    copies = Copies(sems)
    half = own_hidden.shape[1]
    copies.add(own_hidden, hidden.at[:, cols_at(where[3] * half, half)])
    copies.add(other_hidden, hidden.at[:, cols_at((1 - where[3]) * half, half)])
    fill_down(where, copies, sizes, own, pieces, [part], weight)
    copies.wait()
    value = dot(hidden[...], weight[...]).astype(BF16)
    each = outs[0].shape[0]
    for i, out in enumerate(outs):
        out[...] = value[i * each : (i + 1) * each]


def cot_kernel(sizes, keys, blocks, where, *refs):
    cots, own, refs = refs[:blocks], refs[blocks], refs[blocks + 1 :]
    pieces, refs = list(zip(keys, refs[: len(keys)])), refs[len(keys) :]
    keep, send, cot, weight, sems = refs[1:]
    copies = Copies(sems)
    share = own.shape[1] // sizes[1]
    width = share // COL_CHUNKS
    at = 0
    for ref in cots:
        rows = ref.shape[0]
        for part in range(COL_CHUNKS):
            for group in range(sizes[1]):
                copies.add(
                    ref.at[:, pl.ds(group * share + part * width, width)],
                    cot.at[pl.ds(at, rows), pl.ds((part * sizes[1] + group) * width, width)],
                )
        at += rows
    fill_down(where, copies, sizes, own, pieces, list(range(COL_CHUNKS)), weight)
    copies.wait()
    half = weight.shape[0] // 2
    send[...] = dot(cot[...], weight[rows_at((1 - where[3]) * half, half), :], LAST).astype(BF16)
    keep[...] = dot(cot[...], weight[rows_at(where[3] * half, half), :], LAST)


def grad_kernel(sizes, gate_keys, up_keys, where, gate, up, kept, received, own_gate, own_up, *refs):
    gate_pieces = list(zip(gate_keys, refs[: len(gate_keys)]))
    refs = refs[len(gate_keys) :]
    up_pieces = list(zip(up_keys, refs[: len(up_keys)]))
    keep, send, w_gate, w_up, sems = refs[-5:]
    copies = Copies(sems)
    fill_wide(where, copies, sizes, own_gate, gate_pieces, w_gate)
    fill_wide(where, copies, sizes, own_up, up_pieces, w_up)
    gate_act = gate[...]
    sigmoid_g = jax.nn.sigmoid(gate_act)
    hidden_grad = kept[...] + received[...].astype(F32)
    gate_grad = (hidden_grad * up[...] * sigmoid_g * (1.0 + gate_act * (1.0 - sigmoid_g))).astype(BF16)
    up_grad = (hidden_grad * gate_act * sigmoid_g).astype(BF16)
    copies.wait()
    half = keep.shape[1]
    mine, theirs = cols_at(where[3] * half, half), cols_at((1 - where[3]) * half, half)
    send[...] = (dot(gate_grad, w_gate[:, theirs]) + dot(up_grad, w_up[:, theirs])).astype(BF16)
    keep[...] = dot(gate_grad, w_gate[:, mine]) + dot(up_grad, w_up[:, mine])


def add_kernel(kept, received, *outs):
    value = (kept[...] + received[...].astype(F32)).astype(BF16)
    each = outs[0].shape[0]
    for i, out in enumerate(outs):
        out[...] = value[i * each : (i + 1) * each]


def layer_kernel(experts, cap, blocks, n_groups, where, ids_t, probs_t, cot, *refs):
    out, prob_out, both_out = refs[-3:]
    share = cot.shape[1] // n_groups
    width = share // COL_CHUNKS
    sums = [0.0, 0.0]
    first, second = (m.astype(F32).T.astype(BF16) for m in places(experts, cap, blocks, where, ids_t))
    both_out[...] = first + second
    probs = jnp.concatenate([probs_t[...], jnp.zeros((6, probs_t.shape[1]), F32)], axis=0).T
    for part in range(COL_CHUNKS):
        back = jnp.concatenate([r[...] for r in refs[part * blocks : (part + 1) * blocks]], axis=0)
        slots = dot(first, back), dot(second, back)
        total = probs[:, 0:1] * slots[0] + probs[:, 1:2] * slots[1]
        for group in range(n_groups):
            cols = pl.ds(group * share + part * width, width)
            out[:, cols] = total[:, group * width : (group + 1) * width].astype(BF16)
            cot_here = cot[:, cols].astype(F32)
            for k in range(2):
                held = slots[k][:, group * width : (group + 1) * width] * cot_here
                sums[k] = sums[k] + jnp.sum(held, axis=1, keepdims=True)
    lane = lax.broadcasted_iota(jnp.int32, (cot.shape[0], 128), 1)
    prob_out[...] = jnp.where(lane == 0, sums[0], sums[1]).T[0:2, :]


def token_kernel(both, *refs):
    back = jnp.concatenate([r[...] for r in refs[:-1]], axis=0)
    refs[-1][...] = dot(both[...], back).astype(BF16)


def shift(value, axis, step):
    size = lax.axis_size(axis)
    return lax.ppermute(value, axis, [(i, (i + step) % size) for i in range(size)])


def local(tokens, cotangent, expert_ids, gate_probs, w_gate, w_up, w_down):
    count, half = tokens.shape
    experts, n_dp, n_groups = lax.axis_size("expert"), lax.axis_size("dp"), lax.axis_size("groups")
    sizes = (n_dp, n_groups)
    cap = 3 * count * expert_ids.shape[1] // (2 * experts)
    rows = experts * cap
    shifted = experts <= SHIFTED_UP_TO
    blocks = experts if shifted else 1
    each = rows // blocks
    group = lax.axis_index("groups")
    where = jnp.stack([lax.axis_index(a) for a in ("groups", "expert", "dp", "tensor")]).astype(jnp.int32)

    def exchange(parts, sign):
        whole = parts[0].reshape(experts, cap, -1)
        whole = lax.all_to_all(whole, "expert", split_axis=0, concat_axis=0, tiled=True)
        return [whole.reshape(rows, -1)]

    order = [experts // 2] + [s for s in range(1, experts) if s != experts // 2]

    def travel(parts, sign, earlier=(), held=(), seen=None):
        if not shifted:
            came = exchange(parts, sign)
            if seen is not None:
                seen.extend(came * 3)
            return came
        came = list(parts)
        for i, s in enumerate(order):
            wait = [earlier[s]] if len(earlier) else []
            wait += list(held[i]()) if i < len(held) else []
            came[s] = shift(after(parts[s], *wait) if wait else parts[s], "expert", sign * s)
            if seen is not None:
                seen.append(came[s])
        return came

    cuts = []

    def cut(i, *held):
        weight, axis, chunk = plan[i]
        size = weight.shape[axis] // n_groups // (COL_CHUNKS if axis else ROW_CHUNKS)
        mine = call(
            functools.partial(cut_kernel, axis, chunk, n_groups),
            shape(weight.shape[0] if axis else size, size if axis else weight.shape[1], BF16),
            (where, weight, *held, *cuts[-1:]),
            [SMEM, HBM] + [ANY] * (len(held) + len(cuts[-1:])),
            [pltpu.SemaphoreType.DMA((1,))],
            outs=ANY,
            grant=WHOLE,
        )
        cuts.append(mine)
        return [shift(mine, "dp", step) for step in range(1, n_dp)]

    def turn_over(i, came, *held):
        keys, pieces = [], []
        for step, here in enumerate(came, 1):
            here = after(here, *held) if held else here
            for turn in range(n_groups):
                keys.append((plan[i][2], step, turn))
                pieces.append(shift(here, "groups", turn) if turn else here)
        return keys, pieces

    gate_t, up_t, down = jnp.swapaxes(w_gate[0], 0, 1), jnp.swapaxes(w_up[0], 0, 1), w_down[0]
    units = gate_t.shape[0]
    wide = padded(units)
    feats = n_dp * gate_t.shape[1]
    plan = [(gate_t, 0, c) for c in range(ROW_CHUNKS)] + [(up_t, 0, c) for c in range(ROW_CHUNKS)]
    plan += [(down, 1, c) for c in range(COL_CHUNKS)]
    x = {0: cut(0), 1: cut(1)}
    y = {}

    routed = call(
        functools.partial(route_kernel, experts, cap, blocks),
        [shape(each, half, BF16)] * (2 * blocks),
        (where, expert_ids.T, gate_probs.T, tokens, cotangent),
        [SMEM] + [HBM] * 4,
        [
            pltpu.VMEM(expert_ids.T.shape, jnp.int32),
            pltpu.VMEM(gate_probs.T.shape, F32),
            pltpu.VMEM(tokens.shape, BF16),
            pltpu.VMEM(cotangent.shape, BF16),
            pltpu.SemaphoreType.DMA((4,)),
        ],
        grant=WHOLE,
        flops=4 * rows * count * half,
        moved=4 * count * half + 4 * rows * half,
    )
    seen, cot_seen = [], []
    tok = travel(routed[:blocks], 1, held=[lambda: (), lambda: (seen[0], x[0][-1]), lambda: (seen[1], x[1][-1])], seen=seen)
    y[0] = turn_over(0, x[0])
    x[2] = cut(2, x[0][-1])
    y[1] = turn_over(1, x[1])
    x[3] = cut(3, x[1][-1], seen[1])
    cot_held = [lambda: (seen[-1], x[2][-1]), lambda: cot_seen[:1], lambda: cot_seen[1:2]]
    cot = travel(list(routed[blocks:]), 1, held=cot_held, seen=cot_seen)
    y[2] = turn_over(2, x[2], y[0][1][-1])
    x[4] = cut(4, x[2][-1], seen[-1])
    y[3] = turn_over(3, x[3], y[1][1][-1])
    x[5] = cut(5, x[3][-1], cot_seen[0])
    y[4] = turn_over(4, x[4], y[2][1][-1], cot_seen[1])
    y[5] = turn_over(5, x[5], y[3][1][-1], x[4][-1])
    if shifted:
        tok = call(
            join_kernel,
            shape(rows, half, BF16),
            tok,
            [ANY] * blocks,
            [pltpu.SemaphoreType.DMA((blocks,))],
            outs=ANY,
            moved=4 * rows * half,
        )
    else:
        tok = tok[0]
    other_tok = shift(tok, "tensor", 1)

    def held_by(picked):
        return [k for i in picked for k in y[i][0]], [p for i in picked for p in y[i][1]]

    gate_keys, gate_pieces = held_by([0, 1])
    up_keys, up_pieces = held_by([2, 3])
    down_keys, down_pieces = held_by([4, 5])

    def front(own, keys, pieces, gate, *held):
        final = gate is not None
        act = shape(rows, wide, F32)
        return call(
            functools.partial(front_kernel, sizes, keys, final),
            [act, shape(rows, wide, BF16)] if final else [act],
            (where, tok, other_tok, own, *pieces, *([gate] if final else []), *held),
            [SMEM] + [ANY] * (3 + len(pieces)) + [VMEM] * final + [ANY] * len(held),
            [
                pltpu.VMEM((rows, feats), BF16),
                pltpu.VMEM((wide, feats), BF16),
                pltpu.SemaphoreType.DMA((3 + len(pieces),)),
            ],
            flops=2 * rows * feats * units,
            moved=2 * feats * (rows + units),
        )

    (gate,) = front(gate_t, gate_keys, gate_pieces, None)
    up, hidden = front(up_t, up_keys, up_pieces, gate, cot_seen[1])
    other_hidden = shift(hidden, "tensor", 1)

    width = half // n_groups // COL_CHUNKS
    back = []
    for part in range(COL_CHUNKS):
        picked = [i for i, key in enumerate(down_keys) if key[0] == part]
        held = [b[0] for b in back]
        outs = call(
            functools.partial(out_kernel, sizes, [down_keys[i] for i in picked], part, blocks),
            [shape(each, n_groups * width, BF16)] * blocks,
            (where, hidden, other_hidden, down, *[down_pieces[i] for i in picked], cot_seen[2], *held),
            [SMEM] + [ANY] * (4 + len(picked) + len(held)),
            [
                pltpu.VMEM((rows, 2 * wide), BF16),
                pltpu.VMEM((2 * wide, n_groups * width), BF16),
                pltpu.SemaphoreType.DMA((2 + n_groups + len(picked),)),
            ],
            flops=4 * rows * units * n_groups * width,
            moved=4 * units * n_groups * width,
        )
        back.append(travel(outs, -1, back[-1] if back else ()))

    kept, sent = call(
        functools.partial(cot_kernel, sizes, down_keys, blocks),
        [shape(rows, wide, F32), shape(rows, wide, BF16)],
        (where, *cot, down, *down_pieces, back[-1][0]),
        [SMEM] + [ANY] * (blocks + 2 + len(down_pieces)),
        [
            pltpu.VMEM((rows, half), BF16),
            pltpu.VMEM((2 * wide, half), BF16),
            pltpu.SemaphoreType.DMA((COL_CHUNKS * n_groups * (blocks + 1) + len(down_pieces),)),
        ],
        flops=4 * rows * half * units,
        moved=4 * half * units,
    )
    received = shift(sent, "tensor", 1)
    kept, sent = call(
        functools.partial(grad_kernel, sizes, gate_keys, up_keys),
        [shape(rows, half, F32), shape(rows, half, BF16)],
        (where, gate, up, kept, received, gate_t, up_t, *gate_pieces, *up_pieces, *[back[0][s] for s in order[:2] if shifted]),
        [SMEM] + [VMEM] * 4 + [ANY] * (2 + len(gate_pieces) + len(up_pieces) + 2 * shifted),
        [
            pltpu.VMEM((wide, feats), BF16),
            pltpu.VMEM((wide, feats), BF16),
            pltpu.SemaphoreType.DMA((2 + len(gate_pieces) + len(up_pieces),)),
        ],
        flops=4 * rows * feats * units,
        moved=4 * feats * units,
    )
    received = shift(sent, "tensor", 1)
    slots = call(add_kernel, [shape(each, half, BF16)] * blocks, (kept, received), [VMEM] * 2, moved=8 * rows * half)
    grad_back = travel(slots, -1, back[-1])

    layer_out, prob_part, both = call(
        functools.partial(layer_kernel, experts, cap, blocks, n_groups),
        [shape(count, half, BF16), shape(expert_ids.shape[1], count, F32), shape(count, rows, BF16)],
        (where, expert_ids.T, gate_probs.T, cotangent, *[part for parts in back for part in parts]),
        [SMEM] + [VMEM] * (3 + COL_CHUNKS * blocks),
        flops=4 * count * rows * half,
        moved=2 * rows * half,
    )
    grad_probs = (prob_part + shift(prob_part, "tensor", 1)).T
    (grad_tokens,) = call(
        token_kernel,
        [shape(count, half, BF16)],
        (both, *grad_back),
        [VMEM] * (1 + blocks),
        flops=2 * count * rows * half,
        moved=2 * rows * half,
    )
    return (layer_out, grad_tokens, grad_probs)


def solution(mesh):
    by_token = ("groups", "expert", "dp")
    weight = P("expert", "dp", "tensor")
    in_specs = (P(by_token, "tensor"), P(by_token, "tensor"), P(by_token, None), P(by_token, None)) + (weight,) * 3
    out_specs = (P(by_token, "tensor"), P(by_token, "tensor"), P(by_token, None))
    return jax.shard_map(local, mesh=mesh, in_specs=in_specs, out_specs=out_specs, check_vma=False)
```

time: 162 us -> 216 us (1.33)
  Pallas kernels: 24.8 us -> 107 us
  waiting for transfers between devices: 74.4 us -> 47 us
  starting transfers between devices: 50.2 us -> 36.6 us
  local copies, waits for them, and re-layouts: 11.1 us -> 21.1 us
    pallas_call x10 -> x17, Pallas kernels: 24.8 us -> 107 us  [call(): pl.pallas_call(kernel, out_shape=out_shape, in_specs=spaces, out_specs=ja...]
    ppermute x35 -> x32, waiting for transfers between devices: 74.4 us -> 47 us  [shift(): lax.ppermute(value, axis, [(i, (i + step) % size) for i in range(size)])]
    ppermute x35 -> x32, starting transfers between devices: 50.2 us -> 36.6 us  [shift(): lax.ppermute(value, axis, [(i, (i + step) % size) for i in range(size)])]
    unnamed x41 -> x118, local copies, waits for them, and re-layouts: 8.93 us -> 21.1 us
    dynamic_slice x3 -> x0, local copies, waits for them, and re-layouts: 2.21 us -> none  [gather(): lax.dynamic_slice_in_dim(weight, group * share + chunk * size, size, axis)]
  transfers between devices with their start and end apart: 35 -> 32, of which waited for: 16 -> 11; matrix products, arithmetic and copies ran while one was open for 2% -> 0% of each run, Pallas kernels for 10% -> 38%
where the time goes in v2:
time: 216 us; the launch traced here: 214 us
  Pallas kernels  107 us (50%)
  waiting for transfers between devices  47 us (22%)
  starting transfers between devices  36.6 us (17%)
  local copies, waits for them, and re-layouts  21.1 us (10%)
    pallas_call x17, Pallas kernels, call(): pl.pallas_call(kernel, out_shape=out_shape, in_specs=spaces, out_specs=ja...  107 us
    ppermute x32, waiting for transfers between devices, shift(): lax.ppermute(value, axis, [(i, (i + step) % size) for i in range(size)])  47 us
    ppermute x32, starting transfers between devices, shift(): lax.ppermute(value, axis, [(i, (i + step) % size) for i in range(size)])  36.6 us
    unnamed x118, local copies, waits for them, and re-layouts  21.1 us
  transfers between devices with their start and end apart: 32, of which 11 were waited for; matrix products, arithmetic and copies ran while one was open for 0% of the time, Pallas kernels for 38%

profile of v2, /device:TPU:0, one launch (start us, length us, event | category | flops | bytes accessed | tf_op | source)
XLA Modules:
  0.0 213.9 jit_solution(10060609163355227109)
XLA Ops:
  1.2 12.7 %shard_map.95.refs_0_ = bf16[176,1024]{1,0:T(8,128)(2,1)} custom-call(s32[4]{0:T(128)} %pad_add_fusion.where, bf16[704,1024]{1,0:T(8,128)(2,1)} %bitcast.19), custom_call_target="tpu_custom_call" | custom-call | tf_op jit(solution)/shard_map/pallas_call | solution.py:29
  13.9 3.0 %collective-permute-start.1 = (bf16[176,1024]{1,0:T(8,128)(2,1)}, bf16[176,1024]{1,0:T(8,128)(2,1)S(1)}, u32[]{:S(2)}, u32[]{:S(2)}) collective-permute-start(bf16[176,1024]{1,0:T(8,128)(2,1)} %shard_map.95.refs_0_), channel_id=1, source_target_pairs={{0,2},{2,0},{1,3},{3,1},{4,6},{6,4},{5,7},{7,5},{8,10},{10,8},{9,1... | collective-permute-start | bytes 1081352 | tf_op jit(solution)/shard_map/ppermute | solution.py:305
  16.9 3.3 %shard_map.94 = (bf16[96,1024]{1,0:T(8,128)(2,1)}, bf16[96,1024]{1,0:T(8,128)(2,1)}, bf16[96,1024]{1,0:T(8,128)(2,1)}, bf16[96,1024]{1,0:T(8,128)(2,1)}, bf16[96...) custom-call(s32[4]{0:T(128)} %pad_add_fusion.where, ...), custom_call_target="tpu_custom_call" | custom-call | flops 201326592 | bytes 2097152 | tf_op jit(solution)/shard_map/pallas_call | solution.py:29
  20.3 2.7 %collective-permute-start = (bf16[96,1024]{1,0:T(8,128)(2,1)}, bf16[96,1024]{1,0:T(8,128)(2,1)S(1)}, u32[]{:S(2)}, u32[]{:S(2)}) collective-permute-start(bf16[96,1024]{1,0:T(8,128)(2,1)} %get-tuple-element.34), channel_id=1, source_target_pairs={{0,8},{4,12},{8,0},{12,4},{1,9},{5,13},{9,1},{13,5},{2,10},{6,14},... | collective-permute-start | bytes 589832 | tf_op jit(solution)/shard_map/ppermute | solution.py:305
  22.9 12.7 %shard_map.97.refs_1_ = bf16[176,1024]{1,0:T(8,128)(2,1)} custom-call(s32[4]{0:T(128)} %pad_add_fusion.where, bf16[704,1024]{1,0:T(8,128)(2,1)} %bitcast.20, bf16[176,1024]{1,0:T(8,128)(2,1)} %shard_map.95.refs_0_), custom_call_target="tpu_custom_call" | custom-call | tf_op jit(solution)/shard_map/pallas_call | solution.py:29
  38.7 6.8 %collective-permute-done.3.refs_2_.refs_0_ = bf16[176,1024]{1,0:T(8,128)(2,1)S(1)} collective-permute-done((bf16[176,1024]{1,0:T(8,128)(2,1)}, bf16[176,1024]{1,0:T(8,128)(2,1)S(1)}, u32[]{:S(2)}, u32[]{:S(2)}) %collective-permute-start.3) | collective-permute-done | bytes 360480 | tf_op jit(solution)/shard_map/ppermute | solution.py:305
  47.7 12.8 %shard_map.100.refs_2_ = bf16[176,1024]{1,0:T(8,128)(2,1)} custom-call(s32[4]{0:T(128)} %pad_add_fusion.where, bf16[704,1024]{1,0:T(8,128)(2,1)} %bitcast.15, bf16[176,1024]{1,0:T(8,128)(2,1)} %copy-done.8, bf16[176,1024]{1,0:T(8,128)(2,1)} %shard_map.97.refs_1_), custom_call_target="tpu_custom_call" | custom-call | tf_op jit(solution)/shard_map/pallas_call | solution.py:29
  62.3 1.6 collective-permute-start.7
  63.8 12.7 %shard_map.102.refs_2_ = bf16[176,1024]{1,0:T(8,128)(2,1)} custom-call(s32[4]{0:T(128)} %pad_add_fusion.where, bf16[704,1024]{1,0:T(8,128)(2,1)} %bitcast.16, bf16[176,1024]{1,0:T(8,128)(2,1)} %copy-done.12, bf16[96,1024]{1,0:T(8,128)(2,1)} %copy-done.28, bf16[176,1024]{1,0:T(8,128)(2,1)} %shard_map.100.refs_2_), custom_call_target="tpu_custom_call" | custom-call | tf_op jit(solution)/shard_map/pallas_call | solution.py:29
  79.4 1.7 collective-permute-start.12
  81.1 12.7 %shard_map.108.refs_2_ = bf16[704,256]{1,0:T(8,128)(2,1)} custom-call(s32[4]{0:T(128)} %pad_add_fusion.where, bf16[704,1024]{1,0:T(8,128)(2,1)} %bitcast.23, bf16[176,1024]{1,0:T(8,128)(2,1)} %copy-done.6, bf16[96,1024]{1,0:T(8,128)(2,1)} %copy-done.27, bf16[176,1024]{1,0:T(8,128)(2,1)} %shard_map.102.refs_2_), custom_call_target="tpu_custom_call" | custom-call | tf_op jit(solution)/shard_map/pallas_call | solution.py:29
  97.5 12.7 %shard_map.112 = bf16[704,256]{1,0:T(8,128)(2,1)} custom-call(s32[4]{0:T(128)} %pad_add_fusion.where, bf16[704,1024]{1,0:T(8,128)(2,1)} %bitcast.24, bf16[176,1024]{1,0:T(8,128)(2,1)} %copy-done.16, bf16[96,1024]{1,0:T(8,128)(2,1)} %copy-done.38, bf16[704,256]{1,0:T(8,128)(2,1)} %shard_map.108.refs_2_), custom_call_target="tpu_custom_call" | custom-call | tf_op jit(solution)/shard_map/pallas_call | solution.py:29
  117.5 3.4 %shard_map.104.refs_4_.gate = f32[384,768]{1,0:T(8,128)S(1)} custom-call(s32[4]{0:T(128)S(1)} %copy-done.55, bf16[384,1024]{1,0:T(8,128)(2,1)} %shard_map.99.own_tok, bf16[384,1024]{1,0:T(8,128)(2,1)} %collective-permute-done.5.other_tok, bf16[704,1024]{1,0:T(8,128)(2,1)S(1)} %bitcast.21, bf16[176,1024]{1,0:T(8,128)(2,1)S(1)} %copy-done.10, ...), custom_call_target="tpu_custom_call" | custom-call | flops 1107296256 | bytes 4456448 | tf_op jit(solution)/shard_map/pallas_call | solution.py:29
  121.0 4.5 %shard_map.107 = (f32[384,768]{1,0:T(8,128)S(1)}, bf16[384,768]{1,0:T(8,128)(2,1)}) custom-call(s32[4]{0:T(128)S(1)} %copy-done.55, bf16[384,1024]{1,0:T(8,128)(2,1)} %shard_map.99.own_tok, bf16[384,1024]{1,0:T(8,128)(2,1)} %collective-permute-done.5.other_tok, bf16[704,1024]{1,0:T(8,128)(2,1)S(1)} %bitcast.17, bf16[176,1024]{1,0:T(8,128)(2,1)S(1)} %copy-done.7, ...), custom_call_target="tpu_custom_call" | custom-call | flops 1107296256 | bytes 4456448 | tf_op jit(solution)/shard_map/pallas_call | solution.py:29
  126.6 2.1 collective-permute-done.21.refs_0_
  130.7 3.5 %collective-permute-start.17 = (bf16[96,1024]{1,0:T(8,128)(2,1)}, bf16[96,1024]{1,0:T(8,128)(2,1)S(1)}, u32[]{:S(2)}, u32[]{:S(2)}) collective-permute-start(bf16[96,1024]{1,0:T(8,128)(2,1)} %shard_map.110), channel_id=1, source_target_pairs={{0,12},{4,0},{8,4},{12,8},{1,13},{5,1},{9,5},{13,9},{2,14},{6,2},{... | collective-permute-start | bytes 589832 | tf_op jit(solution)/shard_map/ppermute | solution.py:305
  134.1 3.5 %collective-permute-done.17.refs_2_.refs_3_ = bf16[96,1024]{1,0:T(8,128)(2,1)S(1)} collective-permute-done((bf16[96,1024]{1,0:T(8,128)(2,1)}, bf16[96,1024]{1,0:T(8,128)(2,1)S(1)}, u32[]{:S(2)}, u32[]{:S(2)}) %collective-permute-start.17) | collective-permute-done | bytes 196640 | tf_op jit(solution)/shard_map/ppermute | solution.py:305
  137.7 2.7 %collective-permute-done.16.refs_1_.refs_6_ = bf16[704,256]{1,0:T(8,128)(2,1)} collective-permute-done((bf16[704,256]{1,0:T(8,128)(2,1)}, bf16[704,256]{1,0:T(8,128)(2,1)}, u32[]{:S(2)}, u32[]{:S(2)}) %collective-permute-start.16) | collective-permute-done | bytes 360480 | tf_op jit(solution)/shard_map/ppermute | solution.py:305
  141.7 2.8 %shard_map.111 = (bf16[96,512]{1,0:T(8,128)(2,1)S(1)}, bf16[96,512]{1,0:T(8,128)(2,1)S(1)}, bf16[96,512]{1,0:T(8,128)(2,1)S(1)}, bf16[96,512]{1,0:T(8,128)(2,1)S(1)}) custom-call(s32[4]{0:T(128)S(1)} %copy-done.55, bf16[384,768]{1,0:T(8,128)(2,1)} %get-tuple-element.38.own_hidden, bf16[384,768]{1,0:T(8,128)(2,1)} %collective-permute-done.14.other_hidden, ...), custom_call_target="tpu_custom_call" | custom-call | flops 553648128 | bytes 1441792 | tf_op jit(solution)/shard_map/pallas_call | solution.py:29
  145.5 3.2 %shard_map.114 = (bf16[96,512]{1,0:T(8,128)(2,1)S(1)}, bf16[96,512]{1,0:T(8,128)(2,1)S(1)}, bf16[96,512]{1,0:T(8,128)(2,1)S(1)}, bf16[96,512]{1,0:T(8,128)(2,1)S(1)}) custom-call(s32[4]{0:T(128)S(1)} %copy-done.55, bf16[384,768]{1,0:T(8,128)(2,1)} %get-tuple-element.38.own_hidden, bf16[384,768]{1,0:T(8,128)(2,1)} %collective-permute-done.14.other_hidden, ...), custom_call_target="tpu_custom_call" | custom-call | flops 553648128 | bytes 1441792 | tf_op jit(solution)/shard_map/pallas_call | solution.py:29
  150.8 3.8 %shard_map.119 = (f32[384,768]{1,0:T(8,128)S(1)}, bf16[384,768]{1,0:T(8,128)(2,1)S(1)}) custom-call(s32[4]{0:T(128)S(1)} %copy-done.55, bf16[96,1024]{1,0:T(8,128)(2,1)S(1)} %copy-done.58, bf16[96,1024]{1,0:T(8,128)(2,1)S(1)} %copy-done.26, bf16[96,1024]{1,0:T(8,128)(2,1)S(1)} %copy-done.39, bf16[96,1024]{1,0:T(8,128)(2,1)S(1)} %collective-permute-done.17.refs_2_.refs_3_, ...), custom_call_target="tpu_custom_call" | custom-call | flops 1107296256 | bytes 2883584 | tf_op jit(solution)/shard_map/pallas_call | solution.py:29
  154.7 4.0 %collective-permute-start.18 = (bf16[96,512]{1,0:T(8,128)(2,1)S(1)}, bf16[96,512]{1,0:T(8,128)(2,1)S(1)}, u32[]{:S(2)}, u32[]{:S(2)}) collective-permute-start(bf16[96,512]{1,0:T(8,128)(2,1)S(1)} %get-tuple-element.41), channel_id=1, source_target_pairs={{0,12},{4,0},{8,4},{12,8},{1,13},{5,1},{9,5},{13,9},{2,14},{6,2},{... | collective-permute-start | bytes 294920 | tf_op jit(solution)/shard_map/ppermute | solution.py:305
  158.7 3.2 %collective-permute-done.18.refs_1_.refs_9_ = bf16[96,512]{1,0:T(8,128)(2,1)S(1)} collective-permute-done((bf16[96,512]{1,0:T(8,128)(2,1)S(1)}, bf16[96,512]{1,0:T(8,128)(2,1)S(1)}, u32[]{:S(2)}, u32[]{:S(2)}) %collective-permute-start.18) | collective-permute-done | bytes 98336 | tf_op jit(solution)/shard_map/ppermute | solution.py:305
  161.9 4.2 %collective-permute-done.19.refs_1_.refs_2_.refs_8_ = bf16[96,512]{1,0:T(8,128)(2,1)S(1)} collective-permute-done((bf16[96,512]{1,0:T(8,128)(2,1)S(1)}, bf16[96,512]{1,0:T(8,128)(2,1)S(1)}, u32[]{:S(2)}, u32[]{:S(2)}) %collective-permute-start.19) | collective-permute-done | bytes 98336 | tf_op jit(solution)/shard_map/ppermute | solution.py:305
  166.2 5.3 %shard_map.120 = (f32[384,1024]{1,0:T(8,128)S(1)}, bf16[384,1024]{1,0:T(8,128)(2,1)}) custom-call(s32[4]{0:T(128)S(1)} %copy-done.55, f32[384,768]{1,0:T(8,128)S(1)} %copy-done.5, f32[384,768]{1,0:T(8,128)S(1)} %copy-done.33, f32[384,768]{1,0:T(8,128)S(1)} %get-tuple-element.52.kept, bf16[384,768]{1,0:T(8,128)(2,1)S(1)} %collective-permute-done.26.received, ...), custom_call_target="tpu_custom_call" | custom-call | flops 2214592512 | bytes 5767168 | tf_op jit(solution)/shard_map/pallas_call | solution.py:29
  172.7 3.8 %collective-permute-start.23 = (bf16[96,512]{1,0:T(8,128)(2,1)}, bf16[96,512]{1,0:T(8,128)(2,1)S(1)}, u32[]{:S(2)}, u32[]{:S(2)}) collective-permute-start(bf16[96,512]{1,0:T(8,128)(2,1)} %shard_map.115), channel_id=1, source_target_pairs={{0,12},{4,0},{8,4},{12,8},{1,13},{5,1},{9,5},{13,9},{2,14},{6,2},{... | collective-permute-start | bytes 294920 | tf_op jit(solution)/shard_map/ppermute | solution.py:305
  176.5 3.6 %collective-permute-done.20.refs_1_.refs_3_ = bf16[96,512]{1,0:T(8,128)(2,1)S(1)} collective-permute-done((bf16[96,512]{1,0:T(8,128)(2,1)S(1)}, bf16[96,512]{1,0:T(8,128)(2,1)S(1)}, u32[]{:S(2)}, u32[]{:S(2)}) %collective-permute-start.20) | collective-permute-done | bytes 98336 | tf_op jit(solution)/shard_map/ppermute | solution.py:305
  180.8 7.0 %collective-permute-done.24.refs_6_.refs_1_ = bf16[96,512]{1,0:T(8,128)(2,1)S(1)} collective-permute-done((bf16[96,512]{1,0:T(8,128)(2,1)}, bf16[96,512]{1,0:T(8,128)(2,1)S(1)}, u32[]{:S(2)}, u32[]{:S(2)}) %collective-permute-start.24) | collective-permute-done | bytes 98336 | tf_op jit(solution)/shard_map/ppermute | solution.py:305
  191.4 1.9 shard_map.118
  196.4 3.1 %collective-permute-start.28 = (bf16[96,1024]{1,0:T(8,128)(2,1)}, bf16[96,1024]{1,0:T(8,128)(2,1)S(1)}, u32[]{:S(2)}, u32[]{:S(2)}) collective-permute-start(bf16[96,1024]{1,0:T(8,128)(2,1)} %shard_map.122), channel_id=1, source_target_pairs={{0,12},{4,0},{8,4},{12,8},{1,13},{5,1},{9,5},{13,9},{2,14},{6,2},{... | collective-permute-start | bytes 589832 | tf_op jit(solution)/shard_map/ppermute | solution.py:305
  200.0 5.5 %collective-permute-done.30.refs_3_ = bf16[96,1024]{1,0:T(8,128)(2,1)S(1)} collective-permute-done((bf16[96,1024]{1,0:T(8,128)(2,1)}, bf16[96,1024]{1,0:T(8,128)(2,1)S(1)}, u32[]{:S(2)}, u32[]{:S(2)}) %collective-permute-start.30) | collective-permute-done | bytes 196640 | tf_op jit(solution)/shard_map/ppermute | solution.py:305
  205.5 7.4 %collective-permute-done.29.refs_2_ = bf16[96,1024]{1,0:T(8,128)(2,1)S(1)} collective-permute-done((bf16[96,1024]{1,0:T(8,128)(2,1)}, bf16[96,1024]{1,0:T(8,128)(2,1)S(1)}, u32[]{:S(2)}, u32[]{:S(2)}) %collective-permute-start.29) | collective-permute-done | bytes 196640 | tf_op jit(solution)/shard_map/ppermute | solution.py:305
  (184 shorter events, 38.7 us)
Async XLA Ops:
  13.9 22.3 %collective-permute-start.1 = (bf16[176,1024]{1,0:T(8,128)(2,1)}, bf16[176,1024]{1,0:T(8,128)(2,1)S(1)}, u32[]{:S(2)}, u32[]{:S(2)}) collective-permute-start(bf16[176,1024]{1,0:T(8,128)(2,1)} %shard_map.95.refs_0_), channel_id=1, source_target_pairs={{0,2},{2,0},{1,3},{3,1},{4,6},{6,4},{5,7},{7,5},{8,10},{10,8},{9,1... | collective-permute-start | bytes 1081352 | tf_op jit(solution)/shard_map/ppermute | solution.py:305
  20.3 16.0 %collective-permute-start = (bf16[96,1024]{1,0:T(8,128)(2,1)}, bf16[96,1024]{1,0:T(8,128)(2,1)S(1)}, u32[]{:S(2)}, u32[]{:S(2)}) collective-permute-start(bf16[96,1024]{1,0:T(8,128)(2,1)} %get-tuple-element.34), channel_id=1, source_target_pairs={{0,8},{4,12},{8,0},{12,4},{1,9},{5,13},{9,1},{13,5},{2,10},{6,14},... | collective-permute-start | bytes 589832 | tf_op jit(solution)/shard_map/ppermute | solution.py:305
  35.6 9.9 %collective-permute-start.3 = (bf16[176,1024]{1,0:T(8,128)(2,1)}, bf16[176,1024]{1,0:T(8,128)(2,1)S(1)}, u32[]{:S(2)}, u32[]{:S(2)}) collective-permute-start(bf16[176,1024]{1,0:T(8,128)(2,1)} %shard_map.97.refs_1_), channel_id=1, source_target_pairs={{0,2},{2,0},{1,3},{3,1},{4,6},{6,4},{5,7},{7,5},{8,10},{10,8},{9,1... | collective-permute-start | bytes 1081352 | tf_op jit(solution)/shard_map/ppermute | solution.py:305
  37.1 8.4 %collective-permute-start.2 = (bf16[96,1024]{1,0:T(8,128)(2,1)}, bf16[96,1024]{1,0:T(8,128)(2,1)S(1)}, u32[]{:S(2)}, u32[]{:S(2)}) collective-permute-start(bf16[96,1024]{1,0:T(8,128)(2,1)} %shard_map.96), channel_id=1, source_target_pairs={{0,4},{4,8},{8,12},{12,0},{1,5},{5,9},{9,13},{13,1},{2,6},{6,10},{... | collective-permute-start | bytes 589832 | tf_op jit(solution)/shard_map/ppermute | solution.py:305
  46.3 14.8 %collective-permute-start.4 = (bf16[96,1024]{1,0:T(8,128)(2,1)}, bf16[96,1024]{1,0:T(8,128)(2,1)S(1)}, u32[]{:S(2)}, u32[]{:S(2)}) collective-permute-start(bf16[96,1024]{1,0:T(8,128)(2,1)} %shard_map.98), channel_id=1, source_target_pairs={{0,12},{4,0},{8,4},{12,8},{1,13},{5,1},{9,5},{13,9},{2,14},{6,2},{... | collective-permute-start | bytes 589832 | tf_op jit(solution)/shard_map/ppermute | solution.py:305
  60.5 18.1 %collective-permute-start.6 = (bf16[176,1024]{1,0:T(8,128)(2,1)}, bf16[176,1024]{1,0:T(8,128)(2,1)S(1)}, u32[]{:S(2)}, u32[]{:S(2)}) collective-permute-start(bf16[176,1024]{1,0:T(8,128)(2,1)} %shard_map.100.refs_2_), channel_id=1, source_target_pairs={{0,2},{2,0},{1,3},{3,1},{4,6},{6,4},{5,7},{7,5},{8,10},{10,8},{9,1... | collective-permute-start | bytes 1081352 | tf_op jit(solution)/shard_map/ppermute | solution.py:305
  62.2 49.9 %collective-permute-start.5 = (bf16[384,1024]{1,0:T(8,128)(2,1)}, bf16[384,1024]{1,0:T(8,128)(2,1)}, u32[]{:S(2)}, u32[]{:S(2)}) collective-permute-start(bf16[384,1024]{1,0:T(8,128)(2,1)} %shard_map.99.own_tok), channel_id=1, source_target_pairs={{0,1},{1,0},{2,3},{3,2},{4,5},{5,4},{6,7},{7,6},{8,9},{9,8},{10,11... | collective-permute-start | bytes 2359304 | tf_op jit(solution)/shard_map/ppermute | solution.py:305
  62.3 31.5 %collective-permute-start.7 = (bf16[176,1024]{1,0:T(8,128)(2,1)S(1)}, bf16[176,1024]{1,0:T(8,128)(2,1)S(1)}, u32[]{:S(2)}, u32[]{:S(2)}) collective-permute-start(bf16[176,1024]{1,0:T(8,128)(2,1)S(1)} %copy-done.9), channel_id=1, source_target_pairs={{0,16},{16,0},{1,17},{17,1},{2,18},{18,2},{3,19},{19,3},{4,20},{20... | collective-permute-start | bytes 1081352 | tf_op jit(solution)/shard_map/ppermute | solution.py:305
  76.6 19.5 %collective-permute-start.9 = (bf16[176,1024]{1,0:T(8,128)(2,1)}, bf16[176,1024]{1,0:T(8,128)(2,1)S(1)}, u32[]{:S(2)}, u32[]{:S(2)}) collective-permute-start(bf16[176,1024]{1,0:T(8,128)(2,1)} %shard_map.102.refs_2_), channel_id=1, source_target_pairs={{0,2},{2,0},{1,3},{3,1},{4,6},{6,4},{5,7},{7,5},{8,10},{10,8},{9,1... | collective-permute-start | bytes 1081352 | tf_op jit(solution)/shard_map/ppermute | solution.py:305
  78.1 32.1 %collective-permute-start.10 = (bf16[176,1024]{1,0:T(8,128)(2,1)S(1)}, bf16[176,1024]{1,0:T(8,128)(2,1)S(1)}, u32[]{:S(2)}, u32[]{:S(2)}) collective-permute-start(bf16[176,1024]{1,0:T(8,128)(2,1)S(1)} %copy-done.13), channel_id=1, source_target_pairs={{0,16},{16,0},{1,17},{17,1},{2,18},{18,2},{3,19},{19,3},{4,20},{20... | collective-permute-start | bytes 1081352 | tf_op jit(solution)/shard_map/ppermute | solution.py:305
  79.4 16.7 %collective-permute-start.12 = (bf16[96,1024]{1,0:T(8,128)(2,1)}, bf16[96,1024]{1,0:T(8,128)(2,1)S(1)}, u32[]{:S(2)}, u32[]{:S(2)}) collective-permute-start(bf16[96,1024]{1,0:T(8,128)(2,1)} %shard_map.105), channel_id=1, source_target_pairs={{0,8},{4,12},{8,0},{12,4},{1,9},{5,13},{9,1},{13,5},{2,10},{6,14},... | collective-permute-start | bytes 589832 | tf_op jit(solution)/shard_map/ppermute | solution.py:305
  94.5 26.4 %collective-permute-start.8 = (bf16[176,1024]{1,0:T(8,128)(2,1)}, bf16[176,1024]{1,0:T(8,128)(2,1)}, u32[]{:S(2)}, u32[]{:S(2)}) collective-permute-start(bf16[176,1024]{1,0:T(8,128)(2,1)} %shard_map.101.refs_0_.refs_4_), channel_id=1, source_target_pairs={{0,16},{16,0},{1,17},{17,1},{2,18},{18,2},{3,19},{19,3},{4,20},{20... | collective-permute-start | bytes 1081352 | tf_op jit(solution)/shard_map/ppermute | solution.py:305
  110.9 10.0 %collective-permute-start.11 = (bf16[176,1024]{1,0:T(8,128)(2,1)}, bf16[176,1024]{1,0:T(8,128)(2,1)}, u32[]{:S(2)}, u32[]{:S(2)}) collective-permute-start(bf16[176,1024]{1,0:T(8,128)(2,1)} %shard_map.103.refs_2_.refs_6_), channel_id=1, source_target_pairs={{0,16},{16,0},{1,17},{17,1},{2,18},{18,2},{3,19},{19,3},{4,20},{20... | collective-permute-start | bytes 1081352 | tf_op jit(solution)/shard_map/ppermute | solution.py:305
  111.5 9.5 %collective-permute-start.13 = (bf16[96,1024]{1,0:T(8,128)(2,1)}, bf16[96,1024]{1,0:T(8,128)(2,1)S(1)}, u32[]{:S(2)}, u32[]{:S(2)}) collective-permute-start(bf16[96,1024]{1,0:T(8,128)(2,1)} %shard_map.106), channel_id=1, source_target_pairs={{0,4},{4,8},{8,12},{12,0},{1,5},{5,9},{9,13},{13,1},{2,6},{6,10},{... | collective-permute-start | bytes 589832 | tf_op jit(solution)/shard_map/ppermute | solution.py:305
  111.5 15.1 %collective-permute-start.15 = (bf16[704,256]{1,0:T(8,128)(2,1)}, bf16[704,256]{1,0:T(8,128)(2,1)}, u32[]{:S(2)}, u32[]{:S(2)}) collective-permute-start(bf16[704,256]{1,0:T(8,128)(2,1)} %shard_map.108.refs_2_), channel_id=1, source_target_pairs={{0,2},{2,0},{1,3},{3,1},{4,6},{6,4},{5,7},{7,5},{8,10},{10,8},{9,1... | collective-permute-start | bytes 1081352 | tf_op jit(solution)/shard_map/ppermute | solution.py:305
  112.1 16.6 %collective-permute-start.21 = (bf16[704,256]{1,0:T(8,128)(2,1)}, bf16[704,256]{1,0:T(8,128)(2,1)}, u32[]{:S(2)}, u32[]{:S(2)}) collective-permute-start(bf16[704,256]{1,0:T(8,128)(2,1)} %shard_map.112), channel_id=1, source_target_pairs={{0,2},{2,0},{1,3},{3,1},{4,6},{6,4},{5,7},{7,5},{8,10},{10,8},{9,1... | collective-permute-start | bytes 1081352 | tf_op jit(solution)/shard_map/ppermute | solution.py:305
  126.5 13.8 %collective-permute-start.14 = (bf16[384,768]{1,0:T(8,128)(2,1)}, bf16[384,768]{1,0:T(8,128)(2,1)}, u32[]{:S(2)}, u32[]{:S(2)}) collective-permute-start(bf16[384,768]{1,0:T(8,128)(2,1)} %get-tuple-element.38.own_hidden), channel_id=1, source_target_pairs={{0,1},{1,0},{2,3},{3,2},{4,5},{5,4},{6,7},{7,6},{8,9},{9,8},{10,11... | collective-permute-start | bytes 1769480 | tf_op jit(solution)/shard_map/ppermute | solution.py:305
  128.6 11.7 %collective-permute-start.16 = (bf16[704,256]{1,0:T(8,128)(2,1)}, bf16[704,256]{1,0:T(8,128)(2,1)}, u32[]{:S(2)}, u32[]{:S(2)}) collective-permute-start(bf16[704,256]{1,0:T(8,128)(2,1)} %shard_map.109.refs_0_.refs_5_), channel_id=1, source_target_pairs={{0,16},{16,0},{1,17},{17,1},{2,18},{18,2},{3,19},{19,3},{4,20},{20... | collective-permute-start | bytes 1081352 | tf_op jit(solution)/shard_map/ppermute | solution.py:305
  130.2 15.3 %collective-permute-start.22 = (bf16[704,256]{1,0:T(8,128)(2,1)}, bf16[704,256]{1,0:T(8,128)(2,1)}, u32[]{:S(2)}, u32[]{:S(2)}) collective-permute-start(bf16[704,256]{1,0:T(8,128)(2,1)} %shard_map.113.refs_0_.refs_7_), channel_id=1, source_target_pairs={{0,16},{16,0},{1,17},{17,1},{2,18},{18,2},{3,19},{19,3},{4,20},{20... | collective-permute-start | bytes 1081352 | tf_op jit(solution)/shard_map/ppermute | solution.py:305
  130.7 7.0 %collective-permute-start.17 = (bf16[96,1024]{1,0:T(8,128)(2,1)}, bf16[96,1024]{1,0:T(8,128)(2,1)S(1)}, u32[]{:S(2)}, u32[]{:S(2)}) collective-permute-start(bf16[96,1024]{1,0:T(8,128)(2,1)} %shard_map.110), channel_id=1, source_target_pairs={{0,12},{4,0},{8,4},{12,8},{1,13},{5,1},{9,5},{13,9},{2,14},{6,2},{... | collective-permute-start | bytes 589832 | tf_op jit(solution)/shard_map/ppermute | solution.py:305
  154.6 11.5 %collective-permute-start.26 = (bf16[384,768]{1,0:T(8,128)(2,1)S(1)}, bf16[384,768]{1,0:T(8,128)(2,1)S(1)}, u32[]{:S(2)}, u32[]{:S(2)}) collective-permute-start(bf16[384,768]{1,0:T(8,128)(2,1)S(1)} %get-tuple-element.53), channel_id=1, source_target_pairs={{0,1},{1,0},{2,3},{3,2},{4,5},{5,4},{6,7},{7,6},{8,9},{9,8},{10,11... | collective-permute-start | bytes 1769480 | tf_op jit(solution)/shard_map/ppermute | solution.py:305
  154.7 7.2 %collective-permute-start.18 = (bf16[96,512]{1,0:T(8,128)(2,1)S(1)}, bf16[96,512]{1,0:T(8,128)(2,1)S(1)}, u32[]{:S(2)}, u32[]{:S(2)}) collective-permute-start(bf16[96,512]{1,0:T(8,128)(2,1)S(1)} %get-tuple-element.41), channel_id=1, source_target_pairs={{0,12},{4,0},{8,4},{12,8},{1,13},{5,1},{9,5},{13,9},{2,14},{6,2},{... | collective-permute-start | bytes 294920 | tf_op jit(solution)/shard_map/ppermute | solution.py:305
  158.7 7.4 %collective-permute-start.19 = (bf16[96,512]{1,0:T(8,128)(2,1)S(1)}, bf16[96,512]{1,0:T(8,128)(2,1)S(1)}, u32[]{:S(2)}, u32[]{:S(2)}) collective-permute-start(bf16[96,512]{1,0:T(8,128)(2,1)S(1)} %get-tuple-element.42), channel_id=1, source_target_pairs={{0,8},{4,12},{8,0},{12,4},{1,9},{5,13},{9,1},{13,5},{2,10},{6,14},... | collective-permute-start | bytes 294920 | tf_op jit(solution)/shard_map/ppermute | solution.py:305
  172.7 20.7 %collective-permute-start.27 = (bf16[384,1024]{1,0:T(8,128)(2,1)}, bf16[384,1024]{1,0:T(8,128)(2,1)S(1)}, u32[]{:S(2)}, u32[]{:S(2)}) collective-permute-start(bf16[384,1024]{1,0:T(8,128)(2,1)} %get-tuple-element.55), channel_id=1, source_target_pairs={{0,1},{1,0},{2,3},{3,2},{4,5},{5,4},{6,7},{7,6},{8,9},{9,8},{10,11... | collective-permute-start | bytes 2359304 | tf_op jit(solution)/shard_map/ppermute | solution.py:305
  172.7 7.4 %collective-permute-start.20 = (bf16[96,512]{1,0:T(8,128)(2,1)S(1)}, bf16[96,512]{1,0:T(8,128)(2,1)S(1)}, u32[]{:S(2)}, u32[]{:S(2)}) collective-permute-start(bf16[96,512]{1,0:T(8,128)(2,1)S(1)} %get-tuple-element.43), channel_id=1, source_target_pairs={{0,4},{4,8},{8,12},{12,0},{1,5},{5,9},{9,13},{13,1},{2,6},{6,10},{... | collective-permute-start | bytes 294920 | tf_op jit(solution)/shard_map/ppermute | solution.py:305
  172.7 8.1 %collective-permute-start.23 = (bf16[96,512]{1,0:T(8,128)(2,1)}, bf16[96,512]{1,0:T(8,128)(2,1)S(1)}, u32[]{:S(2)}, u32[]{:S(2)}) collective-permute-start(bf16[96,512]{1,0:T(8,128)(2,1)} %shard_map.115), channel_id=1, source_target_pairs={{0,12},{4,0},{8,4},{12,8},{1,13},{5,1},{9,5},{13,9},{2,14},{6,2},{... | collective-permute-start | bytes 294920 | tf_op jit(solution)/shard_map/ppermute | solution.py:305
  176.5 11.3 %collective-permute-start.24 = (bf16[96,512]{1,0:T(8,128)(2,1)}, bf16[96,512]{1,0:T(8,128)(2,1)S(1)}, u32[]{:S(2)}, u32[]{:S(2)}) collective-permute-start(bf16[96,512]{1,0:T(8,128)(2,1)} %shard_map.116), channel_id=1, source_target_pairs={{0,8},{4,12},{8,0},{12,4},{1,9},{5,13},{9,1},{13,5},{2,10},{6,14},... | collective-permute-start | bytes 294920 | tf_op jit(solution)/shard_map/ppermute | solution.py:305
  180.8 7.0 %collective-permute-start.25 = (bf16[96,512]{1,0:T(8,128)(2,1)}, bf16[96,512]{1,0:T(8,128)(2,1)S(1)}, u32[]{:S(2)}, u32[]{:S(2)}) collective-permute-start(bf16[96,512]{1,0:T(8,128)(2,1)} %shard_map.117), channel_id=1, source_target_pairs={{0,4},{4,8},{8,12},{12,0},{1,5},{5,9},{9,13},{13,1},{2,6},{6,10},{... | collective-permute-start | bytes 294920 | tf_op jit(solution)/shard_map/ppermute | solution.py:305
  193.4 6.1 %collective-permute-start.31 = (f32[2,128]{1,0:T(2,128)S(1)}, f32[2,128]{1,0:T(2,128)S(1)}, u32[]{:S(2)}, u32[]{:S(2)}) collective-permute-start(f32[2,128]{1,0:T(2,128)S(1)} %get-tuple-element.60), channel_id=1, source_target_pairs={{0,1},{1,0},{2,3},{3,2},{4,5},{5,4},{6,7},{7,6},{8,9},{9,8},{10,11... | collective-permute-start | bytes 3080 | tf_op jit(solution)/shard_map/ppermute | solution.py:305
  195.6 9.9 %collective-permute-start.30 = (bf16[96,1024]{1,0:T(8,128)(2,1)}, bf16[96,1024]{1,0:T(8,128)(2,1)S(1)}, u32[]{:S(2)}, u32[]{:S(2)}) collective-permute-start(bf16[96,1024]{1,0:T(8,128)(2,1)} %shard_map.124), channel_id=1, source_target_pairs={{0,4},{4,8},{8,12},{12,0},{1,5},{5,9},{9,13},{13,1},{2,6},{6,10},{... | collective-permute-start | bytes 589832 | tf_op jit(solution)/shard_map/ppermute | solution.py:305
  195.6 17.3 %collective-permute-start.29 = (bf16[96,1024]{1,0:T(8,128)(2,1)}, bf16[96,1024]{1,0:T(8,128)(2,1)S(1)}, u32[]{:S(2)}, u32[]{:S(2)}) collective-permute-start(bf16[96,1024]{1,0:T(8,128)(2,1)} %shard_map.123), channel_id=1, source_target_pairs={{0,8},{4,12},{8,0},{12,4},{1,9},{5,13},{9,1},{13,5},{2,10},{6,14},... | collective-permute-start | bytes 589832 | tf_op jit(solution)/shard_map/ppermute | solution.py:305
  196.4 16.5 %collective-permute-start.28 = (bf16[96,1024]{1,0:T(8,128)(2,1)}, bf16[96,1024]{1,0:T(8,128)(2,1)S(1)}, u32[]{:S(2)}, u32[]{:S(2)}) collective-permute-start(bf16[96,1024]{1,0:T(8,128)(2,1)} %shard_map.122), channel_id=1, source_target_pairs={{0,12},{4,0},{8,4},{12,8},{1,13},{5,1},{9,5},{13,9},{2,14},{6,2},{... | collective-permute-start | bytes 589832 | tf_op jit(solution)/shard_map/ppermute | solution.py:305
  (59 other events, 384.8 us)

commit v3 on v0

v3 whole, which is shorter than its diff:
```python
import functools

import jax
import jax.numpy as jnp
from jax import lax
from jax.experimental import pallas as pl
from jax.experimental.pallas import tpu as pltpu
from jax.sharding import PartitionSpec as P

F32 = jnp.float32
BF16 = jnp.bfloat16
LAST = (((1,), (1,)), ((), ()))
ROW_CHUNKS = 2
COL_CHUNKS = 2
SHIFTED_UP_TO = 8

VMEM = pl.BlockSpec(memory_space=pltpu.VMEM)
ANY = pl.BlockSpec(memory_space=pl.ANY)


def dot(a, b, dims=(((1,), (0,)), ((), ()))):
    return lax.dot_general(a, b, dims, preferred_element_type=F32)


def call(kernel, out_shape, args, held=(), scratch=(), flops=0, moved=0):
    several = isinstance(out_shape, list)
    given = len(args)

    def body(*refs):
        kernel(*refs[:given], *refs[given + len(held) :])

    return pl.pallas_call(
        body,
        out_shape=out_shape,
        in_specs=[VMEM] * given + [ANY] * len(held),
        out_specs=[VMEM] * len(out_shape) if several else VMEM,
        scratch_shapes=list(scratch),
        compiler_params=pltpu.CompilerParams(vmem_limit_bytes=24 * 1024 * 1024),
        cost_estimate=pl.CostEstimate(flops=flops, bytes_accessed=moved, transcendentals=0),
    )(*args, *held)


def shape(rows, cols, dtype):
    return jax.ShapeDtypeStruct((rows, cols), dtype)


def padded(size):
    return -(-size // 128) * 128


def before(index, step, size):
    moved = index - step
    return jnp.where(moved < 0, moved + size, moved)


def rows_at(start, size):
    return pl.ds(pl.multiple_of(start, 16), size)


def cols_at(start, size):
    return pl.ds(pl.multiple_of(start, 128), size)


def places(experts, cap, rotated, start, size, ids_t):
    count = ids_t.shape[1]
    row = lax.broadcasted_iota(jnp.int32, (size, 1), 0) + start
    block = jnp.zeros_like(row)
    for later in range(1, experts):
        block = block + (row >= later * cap).astype(jnp.int32)
    expert = block + (lax.axis_index("expert") if rotated else 0)
    expert = jnp.where(expert >= experts, expert - experts, expert)
    slot = (row - block * cap).astype(F32)
    first = ids_t[0:1, :] == expert
    second = ids_t[1:2, :] == expert
    before_it = lax.broadcasted_iota(jnp.int32, (count, count), 0) < lax.broadcasted_iota(jnp.int32, (count, count), 1)
    earlier = dot((first | second).astype(F32).astype(BF16), before_it.astype(F32).astype(BF16))
    here = earlier == slot
    return first & here, second & here


def token_rows_kernel(experts, cap, rotated, ids_t, tok, *outs):
    each = outs[0].shape[0]
    first, second = places(experts, cap, rotated, 0, each * len(outs), ids_t)
    rows = dot((first | second).astype(F32).astype(BF16), tok[...]).astype(BF16)
    for i, out in enumerate(outs):
        out[...] = rows[i * each : (i + 1) * each]


def cot_rows_kernel(experts, cap, rotated, blocks, ids_t, probs_t, cot, *outs):
    each = outs[0].shape[0]
    for block, out in zip(blocks, outs):
        first, second = places(experts, cap, rotated, block * each, each, ids_t)
        weight = jnp.where(first, probs_t[0:1, :], jnp.where(second, probs_t[1:2, :], 0.0))
        weight = jnp.sum(weight, axis=1, keepdims=True)
        rows = dot((first | second).astype(F32).astype(BF16), cot[...])
        out[...] = (weight * rows).astype(BF16)


def cut_kernel(axis, chunk, n_groups, weight, out):
    size = out.shape[axis]
    start = lax.axis_index("groups") * (weight.shape[axis] // n_groups) + chunk * size
    out[...] = weight[rows_at(start, size), :] if axis == 0 else weight[:, cols_at(start, size)]


def join_kernel(*refs):
    at = 0
    for part in refs[:-1]:
        refs[-1][pl.ds(at, part.shape[0]), :] = part[...]
        at += part.shape[0]


def fill_wide(sizes, own, pieces, dst):
    n_dp, n_groups = sizes
    units, feats = own.shape
    group, place = lax.axis_index("groups"), lax.axis_index("dp")
    dst[pl.ds(0, units), cols_at(place * feats, feats)] = own[...]
    share = units // n_groups
    for (chunk, step, turn), ref in pieces:
        start = before(group, turn, n_groups) * share + chunk * ref.shape[0]
        dst[rows_at(start, ref.shape[0]), cols_at(before(place, step, n_dp) * feats, feats)] = ref[...]
    if dst.shape[0] > units:
        dst[units:, :] = jnp.zeros((dst.shape[0] - units, dst.shape[1]), dst.dtype)


def fill_down(sizes, part, own, pieces, dst):
    n_dp, n_groups = sizes
    units, feats = own.shape
    half = dst.shape[0] // 2
    per_half = n_dp // 2
    share = feats // n_groups
    width = share // COL_CHUNKS
    group, place = lax.axis_index("groups"), lax.axis_index("dp")

    def start(index):
        upper = (index >= per_half).astype(jnp.int32)
        return upper * half + (index - upper * per_half) * units

    for g in range(n_groups):
        dst[rows_at(start(place), units), pl.ds(g * width, width)] = own[:, pl.ds(g * share + part * width, width)]
    for (_, step, turn), ref in pieces:
        cols = cols_at(before(group, turn, n_groups) * width, width)
        dst[rows_at(start(before(place, step, n_dp)), units), cols] = ref[...]
    used = per_half * units
    if half > used:
        for side in range(2):
            dst[side * half + used : (side + 1) * half, :] = jnp.zeros((half - used, dst.shape[1]), dst.dtype)


def halves(size):
    core = lax.axis_index("tensor")
    return core * size, (1 - core) * size


def front_kernel(sizes, keys, final, own_tok, other_tok, own, *refs):
    pieces, refs = list(zip(keys, refs[: len(keys)])), refs[len(keys) :]
    weight, act_out = refs[-2:]
    fill_wide(sizes, own, pieces, weight)
    half = own_tok.shape[1]
    mine, theirs = halves(half)
    value = dot(own_tok[...], weight[:, cols_at(mine, half)], LAST) + dot(other_tok[...], weight[:, cols_at(theirs, half)], LAST)
    act_out[...] = value
    if final:
        gate, hidden_out = refs[:2]
        hidden_out[...] = (gate[...] * jax.nn.sigmoid(gate[...]) * value).astype(BF16)


def out_kernel(sizes, keys, part, own_hidden, other_hidden, own, *refs):
    pieces, (weight, *outs) = list(zip(keys, refs[: len(keys)])), refs[len(keys) :]
    fill_down(sizes, part, own, pieces, weight)
    half = own_hidden.shape[1]
    mine, theirs = halves(half)
    value = dot(own_hidden[...], weight[rows_at(mine, half), :]) + dot(other_hidden[...], weight[rows_at(theirs, half), :])
    value = value.astype(BF16)
    each = outs[0].shape[0]
    for i, out in enumerate(outs):
        out[...] = value[i * each : (i + 1) * each]


def cot_kernel(n_groups, cots, *refs):
    weights, (send, keep) = refs[:-2], refs[-2:]
    half = send.shape[1]
    share = cots.shape[1] // n_groups
    width = share // COL_CHUNKS
    mine, theirs = halves(half)
    for start, out in ((theirs, send), (mine, keep)):
        total = 0.0
        for part, weight in enumerate(weights):
            for g in range(n_groups):
                rows = cots[:, pl.ds(g * share + part * width, width)]
                total = total + dot(rows, weight[rows_at(start, half), pl.ds(g * width, width)], LAST)
        out[...] = total.astype(out.dtype)


def grad_kernel(gate, up, kept, received, w_gate, w_up, send, keep):
    gate_act = gate[...]
    sigmoid_g = jax.nn.sigmoid(gate_act)
    hidden_grad = kept[...] + received[...].astype(F32)
    gate_grad = (hidden_grad * up[...] * sigmoid_g * (1.0 + gate_act * (1.0 - sigmoid_g))).astype(BF16)
    up_grad = (hidden_grad * gate_act * sigmoid_g).astype(BF16)
    half = keep.shape[1]
    mine, theirs = halves(half)
    for start, out in ((theirs, send), (mine, keep)):
        cols = cols_at(start, half)
        out[...] = (dot(gate_grad, w_gate[:, cols]) + dot(up_grad, w_up[:, cols])).astype(out.dtype)


def add_kernel(kept, received, *outs):
    value = (kept[...] + received[...].astype(F32)).astype(BF16)
    each = outs[0].shape[0]
    for i, out in enumerate(outs):
        out[...] = value[i * each : (i + 1) * each]


def layer_kernel(experts, cap, rotated, n_groups, part, ids_t, probs_t, cot, *refs):
    back, (out, prob_out, both_out) = refs[:-3], refs[-3:]
    share = cot.shape[1] // n_groups
    width = share // COL_CHUNKS
    back = jnp.concatenate([r[...] for r in back], axis=0)
    first, second = (m.astype(F32).T.astype(BF16) for m in places(experts, cap, rotated, 0, back.shape[0], ids_t))
    both_out[...] = first + second
    probs = jnp.concatenate([probs_t[...], jnp.zeros((6, probs_t.shape[1]), F32)], axis=0).T
    slots = dot(first, back), dot(second, back)
    out[...] = (probs[:, 0:1] * slots[0] + probs[:, 1:2] * slots[1]).astype(BF16)
    sums = [0.0, 0.0]
    for g in range(n_groups):
        cot_here = cot[:, pl.ds(g * share + part * width, width)].astype(F32)
        for k in range(2):
            sums[k] = sums[k] + jnp.sum(slots[k][:, g * width : (g + 1) * width] * cot_here, axis=1, keepdims=True)
    lane = lax.broadcasted_iota(jnp.int32, (cot.shape[0], 128), 1)
    prob_out[...] = jnp.where(lane == 0, sums[0], sums[1]).T[0:2, :]


def token_kernel(n_groups, both, *refs):
    back, layers, (grad_out, layer_out) = refs[: -2 - COL_CHUNKS], refs[-2 - COL_CHUNKS : -2], refs[-2:]
    width = layers[0].shape[1] // n_groups
    for part, layer in enumerate(layers):
        for g in range(n_groups):
            layer_out[:, pl.ds((g * COL_CHUNKS + part) * width, width)] = layer[:, pl.ds(g * width, width)]
    grad_out[...] = dot(both[...], jnp.concatenate([r[...] for r in back], axis=0)).astype(BF16)


def shift(value, axis, step):
    size = lax.axis_size(axis)
    return lax.ppermute(value, axis, [(i, (i + step) % size) for i in range(size)])


def local(tokens, cotangent, expert_ids, gate_probs, w_gate, w_up, w_down):
    count, half = tokens.shape
    experts, n_dp, n_groups = lax.axis_size("expert"), lax.axis_size("dp"), lax.axis_size("groups")
    sizes = (n_dp, n_groups)
    cap = 3 * count * expert_ids.shape[1] // (2 * experts)
    rows = experts * cap
    shifted = experts <= SHIFTED_UP_TO
    blocks = experts if shifted else 1
    each = rows // blocks
    routing = (experts, cap, shifted)
    order = [experts // 2] + [s for s in range(1, experts) if s != experts // 2]

    def travel(part, sign, s):
        if shifted:
            return shift(part, "expert", sign * s) if s else part
        part = lax.all_to_all(part.reshape(experts, cap, -1), "expert", split_axis=0, concat_axis=0, tiled=True)
        return part.reshape(rows, -1)

    gate_t, up_t, down = jnp.swapaxes(w_gate[0], 0, 1), jnp.swapaxes(w_up[0], 0, 1), w_down[0]
    ids_t, probs_t = expert_ids.T, gate_probs.T
    units = gate_t.shape[0]
    wide = padded(units)
    feats = n_dp * gate_t.shape[1]
    plan = [(gate_t, 0, c) for c in range(ROW_CHUNKS)] + [(up_t, 0, c) for c in range(ROW_CHUNKS)]
    plan += [(down, 1, c) for c in range(COL_CHUNKS)]
    x, y, cuts = {}, {}, []

    def cut(i, *held):
        weight, axis, chunk = plan[i]
        size = weight.shape[axis] // n_groups // (COL_CHUNKS if axis else ROW_CHUNKS)
        mine = call(
            functools.partial(cut_kernel, axis, chunk, n_groups),
            shape(weight.shape[0] if axis else size, size if axis else weight.shape[1], BF16),
            (weight,),
            (*held, *cuts[-1:]),
        )
        cuts.append(mine)
        x[i] = [shift(mine, "dp", step) for step in range(1, n_dp)]

    def turn_over(i):
        y[i] = []
        for step, here in enumerate(x[i], 1):
            for turn in range(n_groups):
                y[i].append(((plan[i][2], step, turn), shift(here, "groups", turn) if turn else here))

    cut(0)
    tok_send = call(
        functools.partial(token_rows_kernel, *routing),
        [shape(each, half, BF16)] * blocks,
        (ids_t, tokens),
        cuts[-1:],
        flops=2 * rows * count * half,
        moved=2 * (count + rows) * half,
    )
    cut(1)

    def send_cot(picked, *held):
        made = call(
            functools.partial(cot_rows_kernel, *routing, picked),
            [shape(each, half, BF16)] * len(picked),
            (ids_t, probs_t, cotangent),
            held,
            flops=2 * each * len(picked) * count * half,
            moved=2 * (count + each * len(picked)) * half,
        )
        return [travel(part, 1, s) for part, s in zip(made, picked)]

    tok = [travel(part, 1, s) for s, part in enumerate(tok_send)]
    turn_over(0)
    turn_over(1)
    if shifted:
        t = [tok[s] for s in order]
        cut(2, x[0][-1])
        cut(3, x[1][-1], t[0], t[1])
        cot = dict(zip((0, order[0]), send_cot((0, order[0]), *t[:-1], x[1][-1])))
        cut(4, x[2][-1], *t)
        for i in range(1, len(order)):
            (cot[order[i]],) = send_cot((order[i],), cot[order[i - 1]], *t)
        cut(5, x[3][-1], cot[order[0]])
        cot_parts = [cot[s] for s in range(blocks)]
        tok_all = call(join_kernel, shape(rows, half, BF16), tok)
    else:
        cut(2, x[0][-1])
        cut(3, x[1][-1])
        cut(4, x[2][-1])
        cut(5, x[3][-1])
        cot_parts = send_cot((0,))
        (tok_all,) = tok
    for i in range(2, len(plan)):
        turn_over(i)
    other_tok = shift(tok_all, "tensor", 1)

    def front(own, picked, gate, *held):
        final = gate is not None
        keys, pieces = zip(*[kp for i in picked for kp in y[i]])
        act = shape(rows, wide, F32)
        return call(
            functools.partial(front_kernel, sizes, keys, final),
            ([shape(rows, wide, BF16)] if final else []) + [shape(wide, feats, BF16), act],
            (tok_all, other_tok, own, *pieces, *([gate] if final else [])),
            held,
            flops=2 * rows * feats * units,
            moved=2 * feats * (rows + units),
        )

    first_pieces = range(ROW_CHUNKS)
    gate_weight, gate = front(gate_t, list(first_pieces), None)
    hidden, up_weight, up = front(up_t, [ROW_CHUNKS + i for i in first_pieces], gate, *cot_parts[1:2])
    other_hidden = shift(hidden, "tensor", 1)
    cot_all = call(join_kernel, shape(rows, half, BF16), cot_parts) if shifted else cot_parts[0]

    width = half // n_groups // COL_CHUNKS
    down_weights, layers, sent, prob_part = [], [], [], 0.0
    made = ()
    for part in range(COL_CHUNKS):
        keys, pieces = zip(*y[2 * ROW_CHUNKS + part])
        weight, *made = call(
            functools.partial(out_kernel, sizes, keys, part),
            [shape(2 * wide, n_groups * width, BF16)] + [shape(each, n_groups * width, BF16)] * blocks,
            (hidden, other_hidden, down, *pieces),
            made[:1],
            flops=4 * rows * units * n_groups * width,
            moved=4 * units * n_groups * width,
        )
        down_weights.append(weight)
        back = [travel(out, -1, s) for s, out in enumerate(made)]
        sent.append(back)
        layer, prob, both = call(
            functools.partial(layer_kernel, *routing, n_groups, part),
            [shape(count, n_groups * width, BF16), shape(expert_ids.shape[1], count, F32), shape(count, rows, BF16)],
            (ids_t, probs_t, cotangent, *back),
            flops=4 * count * rows * n_groups * width,
            moved=2 * rows * n_groups * width,
        )
        layers.append(layer)
        prob_part = prob_part + prob

    crossing, kept = call(
        functools.partial(cot_kernel, n_groups),
        [shape(rows, wide, BF16), shape(rows, wide, F32)],
        (cot_all, *down_weights),
        made[:1],
        flops=4 * rows * half * units,
        moved=4 * half * units,
    )
    received = shift(crossing, "tensor", 1)
    crossing, kept = call(
        grad_kernel,
        [shape(rows, half, BF16), shape(rows, half, F32)],
        (gate, up, kept, received, gate_weight, up_weight),
        layers[:1],
        flops=4 * rows * feats * units,
        moved=4 * feats * units,
    )
    received = shift(crossing, "tensor", 1)
    slots = call(add_kernel, [shape(each, half, BF16)] * blocks, (kept, received), sent[-1][1:3], moved=8 * rows * half)
    grad_back = [travel(part, -1, s) for s, part in enumerate(slots)]
    grad_probs = (prob_part + shift(prob_part, "tensor", 1)).T
    grad_tokens, layer_out = call(
        functools.partial(token_kernel, n_groups),
        [shape(count, half, BF16)] * 2,
        (both, *grad_back, *layers),
        flops=2 * count * rows * half,
        moved=2 * rows * half,
    )
    return (layer_out, grad_tokens, grad_probs)


def solution(mesh):
    by_token = ("groups", "expert", "dp")
    weight = P("expert", "dp", "tensor")
    in_specs = (P(by_token, "tensor"), P(by_token, "tensor"), P(by_token, None), P(by_token, None)) + (weight,) * 3
    out_specs = (P(by_token, "tensor"), P(by_token, "tensor"), P(by_token, None))
    return jax.shard_map(local, mesh=mesh, in_specs=in_specs, out_specs=out_specs, check_vma=False)
```

time: 224 us -> 137 us (0.61)
  waiting for transfers between devices: 133 us -> 79.1 us
  blocking collectives: 30.4 us -> 0 us
  matrix products: 28.6 us -> 0 us
  starting transfers between devices: 13.6 us -> 40.3 us
  Pallas kernels: 0 us -> 14.1 us
  between operations: 14.3 us -> 0.92 us
    ppermute x0 -> x32, waiting for transfers between devices: none -> 79.1 us  [shift(): lax.ppermute(value, axis, [(i, (i + step) % size) for i in range(size)])]
    all_gather x4 -> x0, waiting for transfers between devices: 72.2 us -> none  [the longest x1 40.1 us: local(): lax.all_gather(w_up, 'dp', axis=1, tiled=True)]
    all_to_all x3 -> x0, waiting for transfers between devices: 52.7 us -> none  [the longest x1 21.7 us: local(): lax.all_to_all(send_tok, 'expert', split_axis=0, concat_axis=0, tiled=True)]
    ppermute x0 -> x32, starting transfers between devices: none -> 40.3 us  [shift(): lax.ppermute(value, axis, [(i, (i + step) % size) for i in range(size)])]
    dot_general x10 -> x0, matrix products: 28.6 us -> none  [the longest x1 4.71 us: front_half(): up_act = jnp.dot(row_block, up_full, preferred_element_type=jnp.float32)]
    all_to_all x1 -> x0, blocking collectives: 25.3 us -> none  [local(): lax.all_to_all(spread(expert_out), 'expert', split_axis=0, concat_axis=0,...]
    pallas_call x0 -> x22, Pallas kernels: none -> 14.1 us  [call(): pl.pallas_call(body, out_shape=out_shape, in_specs=[VMEM] * given + [ANY]...]
    all_to_all x3 -> x0, starting transfers between devices: 13.4 us -> none  [the longest x1 6.32 us: local(): lax.all_to_all(send_cot, 'expert', split_axis=0, concat_axis=0, tiled=True)]
  transfers between devices with their start and end apart: 9 -> 32, of which waited for: 8 -> 17; matrix products, arithmetic and copies ran while one was open for 14% -> 0% of each run, Pallas kernels for 0% -> 6%
where the time goes in v3:
time: 137 us
  waiting for transfers between devices  79.1 us (58%)
  starting transfers between devices  40.3 us (29%)
  Pallas kernels  14.1 us (10%)
  local copies, waits for them, and re-layouts  2.3 us (2%)
    ppermute x32, waiting for transfers between devices, shift(): lax.ppermute(value, axis, [(i, (i + step) % size) for i in range(size)])  79.1 us
    ppermute x32, starting transfers between devices, shift(): lax.ppermute(value, axis, [(i, (i + step) % size) for i in range(size)])  40.3 us
    pallas_call x22, Pallas kernels, call(): pl.pallas_call(body, out_shape=out_shape, in_specs=[VMEM] * given + [ANY]...  14.1 us
  transfers between devices with their start and end apart: 32, of which 17 were waited for; matrix products, arithmetic and copies ran while one was open for 0% of the time, Pallas kernels for 6%

profile of v3, /device:TPU:0, one launch (start us, length us, event | category | flops | bytes accessed | tf_op | source)
XLA Modules:
  0.0 137.3 jit_solution(18093649164751200843)
XLA Ops:
  3.5 3.1 %collective-permute-start = (bf16[96,1024]{1,0:T(8,128)(2,1)S(1)}, bf16[96,1024]{1,0:T(8,128)(2,1)S(1)}, u32[]{:S(2)}, u32[]{:S(2)}) collective-permute-start(bf16[96,1024]{1,0:T(8,128)(2,1)S(1)} %get-tuple-element.40), channel_id=1, source_target_pairs={{0,4},{4,8},{8,12},{12,0},{1,5},{5,9},{9,13},{13,1},{2,6},{6,10},{... | collective-permute-start | bytes 589832 | tf_op jit(solution)/shard_map/ppermute | solution.py:244
  6.5 2.6 %collective-permute-start.1 = (bf16[96,1024]{1,0:T(8,128)(2,1)S(1)}, bf16[96,1024]{1,0:T(8,128)(2,1)S(1)}, u32[]{:S(2)}, u32[]{:S(2)}) collective-permute-start(bf16[96,1024]{1,0:T(8,128)(2,1)S(1)} %get-tuple-element.41), channel_id=1, source_target_pairs={{0,8},{4,12},{8,0},{12,4},{1,9},{5,13},{9,1},{13,5},{2,10},{6,14},... | collective-permute-start | bytes 589832 | tf_op jit(solution)/shard_map/ppermute | solution.py:244
  12.6 1.8 %collective-permute-done.refs_1_.refs_3_.refs_4_.refs_5_ = bf16[96,1024]{1,0:T(8,128)(2,1)S(1)} collective-permute-done((bf16[96,1024]{1,0:T(8,128)(2,1)S(1)}, bf16[96,1024]{1,0:T(8,128)(2,1)S(1)}, u32[]{:S(2)}, u32[]{:S(2)}) %collective-permute-start) | collective-permute-done | bytes 196640 | tf_op jit(solution)/shard_map/ppermute | solution.py:244
  14.4 7.6 %collective-permute-done.1.refs_2_.refs_3_.refs_4_ = bf16[96,1024]{1,0:T(8,128)(2,1)S(1)} collective-permute-done((bf16[96,1024]{1,0:T(8,128)(2,1)S(1)}, bf16[96,1024]{1,0:T(8,128)(2,1)S(1)}, u32[]{:S(2)}, u32[]{:S(2)}) %collective-permute-start.1) | collective-permute-done | bytes 196640 | tf_op jit(solution)/shard_map/ppermute | solution.py:244
  22.2 1.5 %collective-permute-start.5 = (bf16[176,1024]{1,0:T(8,128)(2,1)S(1)}, bf16[176,1024]{1,0:T(8,128)(2,1)S(1)}, u32[]{:S(2)}, u32[]{:S(2)}) collective-permute-start(bf16[176,1024]{1,0:T(8,128)(2,1)S(1)} %shard_map.98.refs_4_), channel_id=1, source_target_pairs={{0,2},{2,0},{1,3},{3,1},{4,6},{6,4},{5,7},{7,5},{8,10},{10,8},{9,1... | collective-permute-start | bytes 1081352 | tf_op jit(solution)/shard_map/ppermute | solution.py:244
  23.8 5.8 %collective-permute-done.7.refs_1_.refs_5_ = bf16[176,1024]{1,0:T(8,128)(2,1)S(1)} collective-permute-done((bf16[176,1024]{1,0:T(8,128)(2,1)S(1)}, bf16[176,1024]{1,0:T(8,128)(2,1)S(1)}, u32[]{:S(2)}, u32[]{:S(2)}) %collective-permute-start.7) | collective-permute-done | bytes 360480 | tf_op jit(solution)/shard_map/ppermute | solution.py:244
  29.6 1.6 %collective-permute-start.8 = (bf16[176,1024]{1,0:T(8,128)(2,1)S(1)}, bf16[176,1024]{1,0:T(8,128)(2,1)S(1)}, u32[]{:S(2)}, u32[]{:S(2)}) collective-permute-start(bf16[176,1024]{1,0:T(8,128)(2,1)S(1)} %shard_map.99.refs_5_), channel_id=1, source_target_pairs={{0,2},{2,0},{1,3},{3,1},{4,6},{6,4},{5,7},{7,5},{8,10},{10,8},{9,1... | collective-permute-start | bytes 1081352 | tf_op jit(solution)/shard_map/ppermute | solution.py:244
  31.7 1.6 %collective-permute-start.11 = (bf16[176,1024]{1,0:T(8,128)(2,1)S(1)}, bf16[176,1024]{1,0:T(8,128)(2,1)S(1)}, u32[]{:S(2)}, u32[]{:S(2)}) collective-permute-start(bf16[176,1024]{1,0:T(8,128)(2,1)S(1)} %collective-permute-done.7.refs_1_.refs_5_), channel_id=1, source_target_pairs={{0,16},{16,0},{1,17},{17,1},{2,18},{18,2},{3,19},{19,3},{4,20},{20... | collective-permute-start | bytes 1081352 | tf_op jit(solution)/shard_map/ppermute | solution.py:244
  33.3 6.1 %collective-permute-done.12.refs_3_.refs_2_ = bf16[96,1024]{1,0:T(8,128)(2,1)S(1)} collective-permute-done((bf16[96,1024]{1,0:T(8,128)(2,1)S(1)}, bf16[96,1024]{1,0:T(8,128)(2,1)S(1)}, u32[]{:S(2)}, u32[]{:S(2)}) %collective-permute-start.12) | collective-permute-done | bytes 196640 | tf_op jit(solution)/shard_map/ppermute | solution.py:244
  39.4 1.5 %collective-permute-start.10 = (bf16[176,1024]{1,0:T(8,128)(2,1)S(1)}, bf16[176,1024]{1,0:T(8,128)(2,1)S(1)}, u32[]{:S(2)}, u32[]{:S(2)}) collective-permute-start(bf16[176,1024]{1,0:T(8,128)(2,1)S(1)} %collective-permute-done.4.refs_1_.refs_3_), channel_id=1, source_target_pairs={{0,16},{16,0},{1,17},{17,1},{2,18},{18,2},{3,19},{19,3},{4,20},{20... | collective-permute-start | bytes 1081352 | tf_op jit(solution)/shard_map/ppermute | solution.py:244
  41.4 1.5 %collective-permute-done.8.refs_5_.refs_1_ = bf16[176,1024]{1,0:T(8,128)(2,1)S(1)} collective-permute-done((bf16[176,1024]{1,0:T(8,128)(2,1)S(1)}, bf16[176,1024]{1,0:T(8,128)(2,1)S(1)}, u32[]{:S(2)}, u32[]{:S(2)}) %collective-permute-start.8) | collective-permute-done | bytes 360480 | tf_op jit(solution)/shard_map/ppermute | solution.py:244
  43.0 1.5 %collective-permute-start.9 = (bf16[176,1024]{1,0:T(8,128)(2,1)S(1)}, bf16[176,1024]{1,0:T(8,128)(2,1)S(1)}, u32[]{:S(2)}, u32[]{:S(2)}) collective-permute-start(bf16[176,1024]{1,0:T(8,128)(2,1)S(1)} %collective-permute-done.8.refs_5_.refs_1_), channel_id=1, source_target_pairs={{0,16},{16,0},{1,17},{17,1},{2,18},{18,2},{3,19},{19,3},{4,20},{20... | collective-permute-start | bytes 1081352 | tf_op jit(solution)/shard_map/ppermute | solution.py:244
  44.8 2.6 %collective-permute-start.13 = (bf16[96,1024]{1,0:T(8,128)(2,1)S(1)}, bf16[96,1024]{1,0:T(8,128)(2,1)S(1)}, u32[]{:S(2)}, u32[]{:S(2)}) collective-permute-start(bf16[96,1024]{1,0:T(8,128)(2,1)S(1)} %shard_map.102), channel_id=1, source_target_pairs={{0,4},{4,8},{8,12},{12,0},{1,5},{5,9},{9,13},{13,1},{2,6},{6,10},{... | collective-permute-start | bytes 589832 | tf_op jit(solution)/shard_map/ppermute | solution.py:244
  47.5 3.3 %collective-permute-done.10.refs_4_ = bf16[176,1024]{1,0:T(8,128)(2,1)S(1)} collective-permute-done((bf16[176,1024]{1,0:T(8,128)(2,1)S(1)}, bf16[176,1024]{1,0:T(8,128)(2,1)S(1)}, u32[]{:S(2)}, u32[]{:S(2)}) %collective-permute-start.10) | collective-permute-done | bytes 360480 | tf_op jit(solution)/shard_map/ppermute | solution.py:244
  52.8 1.6 %shard_map.100 = (bf16[768,2048]{1,0:T(8,128)(2,1)S(1)}, f32[384,768]{1,0:T(8,128)S(1)}) custom-call(bf16[384,1024]{1,0:T(8,128)(2,1)S(1)} %shard_map.96.refs_0_, bf16[384,1024]{1,0:T(8,128)(2,1)S(1)} %collective-permute-done.3.refs_1_, bf16[704,1024]{1,0:T(8,128)(2,1)S(1)} %bitcast.17, bf16[176,1024]{1,0:T(8,128)(2,1)S(1)} %collective-permute-done.4.refs_1_.refs_3_, ...), custom_call_target="tpu_custom_call" | custom-call | flops 1107296256 | bytes 4456448 | tf_op jit(solution)/shard_map/pallas_call | solution.py:32
  54.4 4.0 %collective-permute-done.6.refs_4_ = bf16[176,1024]{1,0:T(8,128)(2,1)S(1)} collective-permute-done((bf16[176,1024]{1,0:T(8,128)(2,1)S(1)}, bf16[176,1024]{1,0:T(8,128)(2,1)S(1)}, u32[]{:S(2)}, u32[]{:S(2)}) %collective-permute-start.6) | collective-permute-done | bytes 360480 | tf_op jit(solution)/shard_map/ppermute | solution.py:244
  58.5 5.1 %collective-permute-done.9.refs_6_ = bf16[176,1024]{1,0:T(8,128)(2,1)S(1)} collective-permute-done((bf16[176,1024]{1,0:T(8,128)(2,1)S(1)}, bf16[176,1024]{1,0:T(8,128)(2,1)S(1)}, u32[]{:S(2)}, u32[]{:S(2)}) %collective-permute-start.9) | collective-permute-done | bytes 360480 | tf_op jit(solution)/shard_map/ppermute | solution.py:244
  63.6 1.6 %shard_map.103 = (bf16[384,768]{1,0:T(8,128)(2,1)S(1)}, bf16[768,2048]{1,0:T(8,128)(2,1)S(1)}, f32[384,768]{1,0:T(8,128)S(1)}) custom-call(bf16[384,1024]{1,0:T(8,128)(2,1)S(1)} %shard_map.96.refs_0_, bf16[384,1024]{1,0:T(8,128)(2,1)S(1)} %collective-permute-done.3.refs_1_, bf16[704,1024]{1,0:T(8,128)(2,1)S(1)} %bitcast.20, ...), custom_call_target="tpu_custom_call" | custom-call | flops 1107296256 | bytes 4456448 | tf_op jit(solution)/shard_map/pallas_call | solution.py:32
  65.3 1.6 %collective-permute-start.18 = (bf16[704,256]{1,0:T(8,128)(2,1)S(1)}, bf16[704,256]{1,0:T(8,128)(2,1)S(1)}, u32[]{:S(2)}, u32[]{:S(2)}) collective-permute-start(bf16[704,256]{1,0:T(8,128)(2,1)S(1)} %collective-permute-done.17.refs_3_), channel_id=1, source_target_pairs={{0,16},{16,0},{1,17},{17,1},{2,18},{18,2},{3,19},{19,3},{4,20},{20... | collective-permute-start | bytes 1081352 | tf_op jit(solution)/shard_map/ppermute | solution.py:244
  67.7 3.7 %collective-permute-start.22 = (bf16[96,1024]{1,0:T(8,128)(2,1)S(1)}, bf16[96,1024]{1,0:T(8,128)(2,1)S(1)}, u32[]{:S(2)}, u32[]{:S(2)}) collective-permute-start(bf16[96,1024]{1,0:T(8,128)(2,1)S(1)} %shard_map.109), channel_id=1, source_target_pairs={{0,12},{4,0},{8,4},{12,8},{1,13},{5,1},{9,5},{13,9},{2,14},{6,2},{... | collective-permute-start | bytes 589832 | tf_op jit(solution)/shard_map/ppermute | solution.py:244
  71.4 4.2 %collective-permute-done.22.refs_3_ = bf16[96,1024]{1,0:T(8,128)(2,1)S(1)} collective-permute-done((bf16[96,1024]{1,0:T(8,128)(2,1)S(1)}, bf16[96,1024]{1,0:T(8,128)(2,1)S(1)}, u32[]{:S(2)}, u32[]{:S(2)}) %collective-permute-start.22) | collective-permute-done | bytes 196640 | tf_op jit(solution)/shard_map/ppermute | solution.py:244
  77.5 6.4 %collective-permute-done.16.refs_4_ = bf16[704,256]{1,0:T(8,128)(2,1)S(1)} collective-permute-done((bf16[704,256]{1,0:T(8,128)(2,1)S(1)}, bf16[704,256]{1,0:T(8,128)(2,1)S(1)}, u32[]{:S(2)}, u32[]{:S(2)}) %collective-permute-start.16) | collective-permute-done | bytes 360480 | tf_op jit(solution)/shard_map/ppermute | solution.py:244
  86.2 3.7 %collective-permute-start.24 = (bf16[96,512]{1,0:T(8,128)(2,1)S(1)}, bf16[96,512]{1,0:T(8,128)(2,1)S(1)}, u32[]{:S(2)}, u32[]{:S(2)}) collective-permute-start(bf16[96,512]{1,0:T(8,128)(2,1)S(1)} %get-tuple-element.60), channel_id=1, source_target_pairs={{0,12},{4,0},{8,4},{12,8},{1,13},{5,1},{9,5},{13,9},{2,14},{6,2},{... | collective-permute-start | bytes 294920 | tf_op jit(solution)/shard_map/ppermute | solution.py:244
  90.6 2.5 %collective-permute-done.24.refs_4_ = bf16[96,512]{1,0:T(8,128)(2,1)S(1)} collective-permute-done((bf16[96,512]{1,0:T(8,128)(2,1)S(1)}, bf16[96,512]{1,0:T(8,128)(2,1)S(1)}, u32[]{:S(2)}, u32[]{:S(2)}) %collective-permute-start.24) | collective-permute-done | bytes 98336 | tf_op jit(solution)/shard_map/ppermute | solution.py:244
  93.1 6.6 %collective-permute-done.25.refs_5_ = bf16[96,512]{1,0:T(8,128)(2,1)S(1)} collective-permute-done((bf16[96,512]{1,0:T(8,128)(2,1)S(1)}, bf16[96,512]{1,0:T(8,128)(2,1)S(1)}, u32[]{:S(2)}, u32[]{:S(2)}) %collective-permute-start.25) | collective-permute-done | bytes 98336 | tf_op jit(solution)/shard_map/ppermute | solution.py:244
  100.8 2.6 %shard_map.113 = (bf16[384,1024]{1,0:T(8,128)(2,1)S(1)}, f32[384,1024]{1,0:T(8,128)S(1)}) custom-call(f32[384,768]{1,0:T(8,128)S(1)} %get-tuple-element.43.refs_7_.refs_0_, f32[384,768]{1,0:T(8,128)S(1)} %get-tuple-element.52.refs_1_, f32[384,768]{1,0:T(8,128)S(1)} %get-tuple-element.56.refs_2_, bf16[384,768]{1,0:T(8,128)(2,1)S(1)} %collective-permute-done.23.refs_3_, ...), custom_call_target="tpu_custom_call" | custom-call | flops 2214592512 | bytes 5767168 | tf_op jit(solution)/shard_map/pallas_call | solution.py:32
  105.4 1.9 %collective-permute-start.21 = (bf16[96,512]{1,0:T(8,128)(2,1)S(1)}, bf16[96,512]{1,0:T(8,128)(2,1)S(1)}, u32[]{:S(2)}, u32[]{:S(2)}) collective-permute-start(bf16[96,512]{1,0:T(8,128)(2,1)S(1)} %get-tuple-element.50), channel_id=1, source_target_pairs={{0,4},{4,8},{8,12},{12,0},{1,5},{5,9},{9,13},{13,1},{2,6},{6,10},{... | collective-permute-start | bytes 294920 | tf_op jit(solution)/shard_map/ppermute | solution.py:244
  107.4 1.6 %collective-permute-done.19.refs_4_.refs_2_ = bf16[96,512]{1,0:T(8,128)(2,1)S(1)} collective-permute-done((bf16[96,512]{1,0:T(8,128)(2,1)S(1)}, bf16[96,512]{1,0:T(8,128)(2,1)S(1)}, u32[]{:S(2)}, u32[]{:S(2)}) %collective-permute-start.19) | collective-permute-done | bytes 98336 | tf_op jit(solution)/shard_map/ppermute | solution.py:244
  109.0 6.1 %collective-permute-done.20.refs_5_.refs_3_ = bf16[96,512]{1,0:T(8,128)(2,1)S(1)} collective-permute-done((bf16[96,512]{1,0:T(8,128)(2,1)S(1)}, bf16[96,512]{1,0:T(8,128)(2,1)S(1)}, u32[]{:S(2)}, u32[]{:S(2)}) %collective-permute-start.20) | collective-permute-done | bytes 98336 | tf_op jit(solution)/shard_map/ppermute | solution.py:244
  118.1 1.9 %collective-permute-start.30 = (bf16[96,1024]{1,0:T(8,128)(2,1)S(1)}, bf16[96,1024]{1,0:T(8,128)(2,1)S(1)}, u32[]{:S(2)}, u32[]{:S(2)}) collective-permute-start(bf16[96,1024]{1,0:T(8,128)(2,1)S(1)} %get-tuple-element.69), channel_id=1, source_target_pairs={{0,4},{4,8},{8,12},{12,0},{1,5},{5,9},{9,13},{13,1},{2,6},{6,10},{... | collective-permute-start | bytes 589832 | tf_op jit(solution)/shard_map/ppermute | solution.py:244
  120.6 2.7 %collective-permute-done.28.refs_2_ = bf16[96,1024]{1,0:T(8,128)(2,1)S(1)} collective-permute-done((bf16[96,1024]{1,0:T(8,128)(2,1)S(1)}, bf16[96,1024]{1,0:T(8,128)(2,1)S(1)}, u32[]{:S(2)}, u32[]{:S(2)}) %collective-permute-start.28) | collective-permute-done | bytes 196640 | tf_op jit(solution)/shard_map/ppermute | solution.py:244
  123.3 12.9 %collective-permute-done.29.refs_3_ = bf16[96,1024]{1,0:T(8,128)(2,1)S(1)} collective-permute-done((bf16[96,1024]{1,0:T(8,128)(2,1)S(1)}, bf16[96,1024]{1,0:T(8,128)(2,1)S(1)}, u32[]{:S(2)}, u32[]{:S(2)}) %collective-permute-start.29) | collective-permute-done | bytes 196640 | tf_op jit(solution)/shard_map/ppermute | solution.py:244
  (72 shorter events, 23.6 us)
Async XLA Ops:
  3.5 11.0 %collective-permute-start = (bf16[96,1024]{1,0:T(8,128)(2,1)S(1)}, bf16[96,1024]{1,0:T(8,128)(2,1)S(1)}, u32[]{:S(2)}, u32[]{:S(2)}) collective-permute-start(bf16[96,1024]{1,0:T(8,128)(2,1)S(1)} %get-tuple-element.40), channel_id=1, source_target_pairs={{0,4},{4,8},{8,12},{12,0},{1,5},{5,9},{9,13},{13,1},{2,6},{6,10},{... | collective-permute-start | bytes 589832 | tf_op jit(solution)/shard_map/ppermute | solution.py:244
  6.5 15.5 %collective-permute-start.1 = (bf16[96,1024]{1,0:T(8,128)(2,1)S(1)}, bf16[96,1024]{1,0:T(8,128)(2,1)S(1)}, u32[]{:S(2)}, u32[]{:S(2)}) collective-permute-start(bf16[96,1024]{1,0:T(8,128)(2,1)S(1)} %get-tuple-element.41), channel_id=1, source_target_pairs={{0,8},{4,12},{8,0},{12,4},{1,9},{5,13},{9,1},{13,5},{2,10},{6,14},... | collective-permute-start | bytes 589832 | tf_op jit(solution)/shard_map/ppermute | solution.py:244
  9.1 12.9 %collective-permute-start.2 = (bf16[96,1024]{1,0:T(8,128)(2,1)S(1)}, bf16[96,1024]{1,0:T(8,128)(2,1)S(1)}, u32[]{:S(2)}, u32[]{:S(2)}) collective-permute-start(bf16[96,1024]{1,0:T(8,128)(2,1)S(1)} %get-tuple-element.42), channel_id=1, source_target_pairs={{0,12},{4,0},{8,4},{12,8},{1,13},{5,1},{9,5},{13,9},{2,14},{6,2},{... | collective-permute-start | bytes 589832 | tf_op jit(solution)/shard_map/ppermute | solution.py:244
  10.5 11.7 %collective-permute-start.4 = (bf16[176,1024]{1,0:T(8,128)(2,1)S(1)}, bf16[176,1024]{1,0:T(8,128)(2,1)S(1)}, u32[]{:S(2)}, u32[]{:S(2)}) collective-permute-start(bf16[176,1024]{1,0:T(8,128)(2,1)S(1)} %shard_map.94.refs_2_.refs_1_), channel_id=1, source_target_pairs={{0,2},{2,0},{1,3},{3,1},{4,6},{6,4},{5,7},{7,5},{8,10},{10,8},{9,1... | collective-permute-start | bytes 1081352 | tf_op jit(solution)/shard_map/ppermute | solution.py:244
  12.0 17.6 %collective-permute-start.7 = (bf16[176,1024]{1,0:T(8,128)(2,1)S(1)}, bf16[176,1024]{1,0:T(8,128)(2,1)S(1)}, u32[]{:S(2)}, u32[]{:S(2)}) collective-permute-start(bf16[176,1024]{1,0:T(8,128)(2,1)S(1)} %shard_map.97.refs_2_), channel_id=1, source_target_pairs={{0,2},{2,0},{1,3},{3,1},{4,6},{6,4},{5,7},{7,5},{8,10},{10,8},{9,1... | collective-permute-start | bytes 1081352 | tf_op jit(solution)/shard_map/ppermute | solution.py:244
  22.1 29.6 %collective-permute-start.3 = (bf16[384,1024]{1,0:T(8,128)(2,1)S(1)}, bf16[384,1024]{1,0:T(8,128)(2,1)S(1)}, u32[]{:S(2)}, u32[]{:S(2)}) collective-permute-start(bf16[384,1024]{1,0:T(8,128)(2,1)S(1)} %shard_map.96.refs_0_), channel_id=1, source_target_pairs={{0,1},{1,0},{2,3},{3,2},{4,5},{5,4},{6,7},{7,6},{8,9},{9,8},{10,11... | collective-permute-start | bytes 2359304 | tf_op jit(solution)/shard_map/ppermute | solution.py:244
  22.2 18.7 %collective-permute-start.5 = (bf16[176,1024]{1,0:T(8,128)(2,1)S(1)}, bf16[176,1024]{1,0:T(8,128)(2,1)S(1)}, u32[]{:S(2)}, u32[]{:S(2)}) collective-permute-start(bf16[176,1024]{1,0:T(8,128)(2,1)S(1)} %shard_map.98.refs_4_), channel_id=1, source_target_pairs={{0,2},{2,0},{1,3},{3,1},{4,6},{6,4},{5,7},{7,5},{8,10},{10,8},{9,1... | collective-permute-start | bytes 1081352 | tf_op jit(solution)/shard_map/ppermute | solution.py:244
  29.6 13.4 %collective-permute-start.8 = (bf16[176,1024]{1,0:T(8,128)(2,1)S(1)}, bf16[176,1024]{1,0:T(8,128)(2,1)S(1)}, u32[]{:S(2)}, u32[]{:S(2)}) collective-permute-start(bf16[176,1024]{1,0:T(8,128)(2,1)S(1)} %shard_map.99.refs_5_), channel_id=1, source_target_pairs={{0,2},{2,0},{1,3},{3,1},{4,6},{6,4},{5,7},{7,5},{8,10},{10,8},{9,1... | collective-permute-start | bytes 1081352 | tf_op jit(solution)/shard_map/ppermute | solution.py:244
  31.7 7.7 %collective-permute-start.12 = (bf16[96,1024]{1,0:T(8,128)(2,1)S(1)}, bf16[96,1024]{1,0:T(8,128)(2,1)S(1)}, u32[]{:S(2)}, u32[]{:S(2)}) collective-permute-start(bf16[96,1024]{1,0:T(8,128)(2,1)S(1)} %get-tuple-element.44), channel_id=1, source_target_pairs={{0,8},{4,12},{8,0},{12,4},{1,9},{5,13},{9,1},{13,5},{2,10},{6,14},... | collective-permute-start | bytes 589832 | tf_op jit(solution)/shard_map/ppermute | solution.py:244
  31.7 13.1 %collective-permute-start.11 = (bf16[176,1024]{1,0:T(8,128)(2,1)S(1)}, bf16[176,1024]{1,0:T(8,128)(2,1)S(1)}, u32[]{:S(2)}, u32[]{:S(2)}) collective-permute-start(bf16[176,1024]{1,0:T(8,128)(2,1)S(1)} %collective-permute-done.7.refs_1_.refs_5_), channel_id=1, source_target_pairs={{0,16},{16,0},{1,17},{17,1},{2,18},{18,2},{3,19},{19,3},{4,20},{20... | collective-permute-start | bytes 1081352 | tf_op jit(solution)/shard_map/ppermute | solution.py:244
  39.4 11.3 %collective-permute-start.10 = (bf16[176,1024]{1,0:T(8,128)(2,1)S(1)}, bf16[176,1024]{1,0:T(8,128)(2,1)S(1)}, u32[]{:S(2)}, u32[]{:S(2)}) collective-permute-start(bf16[176,1024]{1,0:T(8,128)(2,1)S(1)} %collective-permute-done.4.refs_1_.refs_3_), channel_id=1, source_target_pairs={{0,16},{16,0},{1,17},{17,1},{2,18},{18,2},{3,19},{19,3},{4,20},{20... | collective-permute-start | bytes 1081352 | tf_op jit(solution)/shard_map/ppermute | solution.py:244
  40.9 17.6 %collective-permute-start.6 = (bf16[176,1024]{1,0:T(8,128)(2,1)S(1)}, bf16[176,1024]{1,0:T(8,128)(2,1)S(1)}, u32[]{:S(2)}, u32[]{:S(2)}) collective-permute-start(bf16[176,1024]{1,0:T(8,128)(2,1)S(1)} %collective-permute-done.5.refs_3_.refs_1_), channel_id=1, source_target_pairs={{0,16},{16,0},{1,17},{17,1},{2,18},{18,2},{3,19},{19,3},{4,20},{20... | collective-permute-start | bytes 1081352 | tf_op jit(solution)/shard_map/ppermute | solution.py:244
  43.0 20.6 %collective-permute-start.9 = (bf16[176,1024]{1,0:T(8,128)(2,1)S(1)}, bf16[176,1024]{1,0:T(8,128)(2,1)S(1)}, u32[]{:S(2)}, u32[]{:S(2)}) collective-permute-start(bf16[176,1024]{1,0:T(8,128)(2,1)S(1)} %collective-permute-done.8.refs_5_.refs_1_), channel_id=1, source_target_pairs={{0,16},{16,0},{1,17},{17,1},{2,18},{18,2},{3,19},{19,3},{4,20},{20... | collective-permute-start | bytes 1081352 | tf_op jit(solution)/shard_map/ppermute | solution.py:244
  44.8 9.6 %collective-permute-start.13 = (bf16[96,1024]{1,0:T(8,128)(2,1)S(1)}, bf16[96,1024]{1,0:T(8,128)(2,1)S(1)}, u32[]{:S(2)}, u32[]{:S(2)}) collective-permute-start(bf16[96,1024]{1,0:T(8,128)(2,1)S(1)} %shard_map.102), channel_id=1, source_target_pairs={{0,4},{4,8},{8,12},{12,0},{1,5},{5,9},{9,13},{13,1},{2,6},{6,10},{... | collective-permute-start | bytes 589832 | tf_op jit(solution)/shard_map/ppermute | solution.py:244
  50.8 14.5 %collective-permute-start.17 = (bf16[704,256]{1,0:T(8,128)(2,1)S(1)}, bf16[704,256]{1,0:T(8,128)(2,1)S(1)}, u32[]{:S(2)}, u32[]{:S(2)}) collective-permute-start(bf16[704,256]{1,0:T(8,128)(2,1)S(1)} %shard_map.104.refs_3_), channel_id=1, source_target_pairs={{0,2},{2,0},{1,3},{3,1},{4,6},{6,4},{5,7},{7,5},{8,10},{10,8},{9,1... | collective-permute-start | bytes 1081352 | tf_op jit(solution)/shard_map/ppermute | solution.py:244
  51.7 15.2 %collective-permute-start.15 = (bf16[704,256]{1,0:T(8,128)(2,1)S(1)}, bf16[704,256]{1,0:T(8,128)(2,1)S(1)}, u32[]{:S(2)}, u32[]{:S(2)}) collective-permute-start(bf16[704,256]{1,0:T(8,128)(2,1)S(1)} %shard_map.105), channel_id=1, source_target_pairs={{0,2},{2,0},{1,3},{3,1},{4,6},{6,4},{5,7},{7,5},{8,10},{10,8},{9,1... | collective-permute-start | bytes 1081352 | tf_op jit(solution)/shard_map/ppermute | solution.py:244
  65.2 11.4 %collective-permute-start.14 = (bf16[384,768]{1,0:T(8,128)(2,1)S(1)}, bf16[384,768]{1,0:T(8,128)(2,1)S(1)}, u32[]{:S(2)}, u32[]{:S(2)}) collective-permute-start(bf16[384,768]{1,0:T(8,128)(2,1)S(1)} %get-tuple-element.45.refs_0_), channel_id=1, source_target_pairs={{0,1},{1,0},{2,3},{3,2},{4,5},{5,4},{6,7},{7,6},{8,9},{9,8},{10,11... | collective-permute-start | bytes 1769480 | tf_op jit(solution)/shard_map/ppermute | solution.py:244
  65.3 11.3 %collective-permute-start.18 = (bf16[704,256]{1,0:T(8,128)(2,1)S(1)}, bf16[704,256]{1,0:T(8,128)(2,1)S(1)}, u32[]{:S(2)}, u32[]{:S(2)}) collective-permute-start(bf16[704,256]{1,0:T(8,128)(2,1)S(1)} %collective-permute-done.17.refs_3_), channel_id=1, source_target_pairs={{0,16},{16,0},{1,17},{17,1},{2,18},{18,2},{3,19},{19,3},{4,20},{20... | collective-permute-start | bytes 1081352 | tf_op jit(solution)/shard_map/ppermute | solution.py:244
  66.9 16.9 %collective-permute-start.16 = (bf16[704,256]{1,0:T(8,128)(2,1)S(1)}, bf16[704,256]{1,0:T(8,128)(2,1)S(1)}, u32[]{:S(2)}, u32[]{:S(2)}) collective-permute-start(bf16[704,256]{1,0:T(8,128)(2,1)S(1)} %collective-permute-done.15.refs_3_), channel_id=1, source_target_pairs={{0,16},{16,0},{1,17},{17,1},{2,18},{18,2},{3,19},{19,3},{4,20},{20... | collective-permute-start | bytes 1081352 | tf_op jit(solution)/shard_map/ppermute | solution.py:244
  67.7 7.9 %collective-permute-start.22 = (bf16[96,1024]{1,0:T(8,128)(2,1)S(1)}, bf16[96,1024]{1,0:T(8,128)(2,1)S(1)}, u32[]{:S(2)}, u32[]{:S(2)}) collective-permute-start(bf16[96,1024]{1,0:T(8,128)(2,1)S(1)} %shard_map.109), channel_id=1, source_target_pairs={{0,12},{4,0},{8,4},{12,8},{1,13},{5,1},{9,5},{13,9},{2,14},{6,2},{... | collective-permute-start | bytes 589832 | tf_op jit(solution)/shard_map/ppermute | solution.py:244
  86.2 14.7 %collective-permute-start.23 = (bf16[384,768]{1,0:T(8,128)(2,1)S(1)}, bf16[384,768]{1,0:T(8,128)(2,1)S(1)}, u32[]{:S(2)}, u32[]{:S(2)}) collective-permute-start(bf16[384,768]{1,0:T(8,128)(2,1)S(1)} %get-tuple-element.57), channel_id=1, source_target_pairs={{0,1},{1,0},{2,3},{3,2},{4,5},{5,4},{6,7},{7,6},{8,9},{9,8},{10,11... | collective-permute-start | bytes 1769480 | tf_op jit(solution)/shard_map/ppermute | solution.py:244
  86.2 6.8 %collective-permute-start.24 = (bf16[96,512]{1,0:T(8,128)(2,1)S(1)}, bf16[96,512]{1,0:T(8,128)(2,1)S(1)}, u32[]{:S(2)}, u32[]{:S(2)}) collective-permute-start(bf16[96,512]{1,0:T(8,128)(2,1)S(1)} %get-tuple-element.60), channel_id=1, source_target_pairs={{0,12},{4,0},{8,4},{12,8},{1,13},{5,1},{9,5},{13,9},{2,14},{6,2},{... | collective-permute-start | bytes 294920 | tf_op jit(solution)/shard_map/ppermute | solution.py:244
  89.9 9.7 %collective-permute-start.25 = (bf16[96,512]{1,0:T(8,128)(2,1)S(1)}, bf16[96,512]{1,0:T(8,128)(2,1)S(1)}, u32[]{:S(2)}, u32[]{:S(2)}) collective-permute-start(bf16[96,512]{1,0:T(8,128)(2,1)S(1)} %get-tuple-element.61), channel_id=1, source_target_pairs={{0,8},{4,12},{8,0},{12,4},{1,9},{5,13},{9,1},{13,5},{2,10},{6,14},... | collective-permute-start | bytes 294920 | tf_op jit(solution)/shard_map/ppermute | solution.py:244
  89.9 9.7 %collective-permute-start.26 = (bf16[96,512]{1,0:T(8,128)(2,1)S(1)}, bf16[96,512]{1,0:T(8,128)(2,1)S(1)}, u32[]{:S(2)}, u32[]{:S(2)}) collective-permute-start(bf16[96,512]{1,0:T(8,128)(2,1)S(1)} %get-tuple-element.62), channel_id=1, source_target_pairs={{0,4},{4,8},{8,12},{12,0},{1,5},{5,9},{9,13},{13,1},{2,6},{6,10},{... | collective-permute-start | bytes 294920 | tf_op jit(solution)/shard_map/ppermute | solution.py:244
  103.5 12.3 %collective-permute-start.27 = (bf16[384,1024]{1,0:T(8,128)(2,1)S(1)}, bf16[384,1024]{1,0:T(8,128)(2,1)S(1)}, u32[]{:S(2)}, u32[]{:S(2)}) collective-permute-start(bf16[384,1024]{1,0:T(8,128)(2,1)S(1)} %get-tuple-element.65), channel_id=1, source_target_pairs={{0,1},{1,0},{2,3},{3,2},{4,5},{5,4},{6,7},{7,6},{8,9},{9,8},{10,11... | collective-permute-start | bytes 2359304 | tf_op jit(solution)/shard_map/ppermute | solution.py:244
  103.6 5.4 %collective-permute-start.19 = (bf16[96,512]{1,0:T(8,128)(2,1)S(1)}, bf16[96,512]{1,0:T(8,128)(2,1)S(1)}, u32[]{:S(2)}, u32[]{:S(2)}) collective-permute-start(bf16[96,512]{1,0:T(8,128)(2,1)S(1)} %get-tuple-element.48), channel_id=1, source_target_pairs={{0,12},{4,0},{8,4},{12,8},{1,13},{5,1},{9,5},{13,9},{2,14},{6,2},{... | collective-permute-start | bytes 294920 | tf_op jit(solution)/shard_map/ppermute | solution.py:244
  104.7 10.4 %collective-permute-start.20 = (bf16[96,512]{1,0:T(8,128)(2,1)S(1)}, bf16[96,512]{1,0:T(8,128)(2,1)S(1)}, u32[]{:S(2)}, u32[]{:S(2)}) collective-permute-start(bf16[96,512]{1,0:T(8,128)(2,1)S(1)} %get-tuple-element.49), channel_id=1, source_target_pairs={{0,8},{4,12},{8,0},{12,4},{1,9},{5,13},{9,1},{13,5},{2,10},{6,14},... | collective-permute-start | bytes 294920 | tf_op jit(solution)/shard_map/ppermute | solution.py:244
  105.4 9.6 %collective-permute-start.21 = (bf16[96,512]{1,0:T(8,128)(2,1)S(1)}, bf16[96,512]{1,0:T(8,128)(2,1)S(1)}, u32[]{:S(2)}, u32[]{:S(2)}) collective-permute-start(bf16[96,512]{1,0:T(8,128)(2,1)S(1)} %get-tuple-element.50), channel_id=1, source_target_pairs={{0,4},{4,8},{8,12},{12,0},{1,5},{5,9},{9,13},{13,1},{2,6},{6,10},{... | collective-permute-start | bytes 294920 | tf_op jit(solution)/shard_map/ppermute | solution.py:244
  115.8 4.3 %collective-permute-start.31 = (f32[2,128]{1,0:T(2,128)S(1)}, f32[2,128]{1,0:T(2,128)S(1)}, u32[]{:S(2)}, u32[]{:S(2)}) collective-permute-start(f32[2,128]{1,0:T(2,128)S(1)} %add.6), channel_id=1, source_target_pairs={{0,1},{1,0},{2,3},{3,2},{4,5},{5,4},{6,7},{7,6},{8,9},{9,8},{10,11... | collective-permute-start | bytes 3080 | tf_op jit(solution)/shard_map/ppermute | solution.py:244
  116.0 7.3 %collective-permute-start.28 = (bf16[96,1024]{1,0:T(8,128)(2,1)S(1)}, bf16[96,1024]{1,0:T(8,128)(2,1)S(1)}, u32[]{:S(2)}, u32[]{:S(2)}) collective-permute-start(bf16[96,1024]{1,0:T(8,128)(2,1)S(1)} %get-tuple-element.67), channel_id=1, source_target_pairs={{0,12},{4,0},{8,4},{12,8},{1,13},{5,1},{9,5},{13,9},{2,14},{6,2},{... | collective-permute-start | bytes 589832 | tf_op jit(solution)/shard_map/ppermute | solution.py:244
  116.9 19.3 %collective-permute-start.29 = (bf16[96,1024]{1,0:T(8,128)(2,1)S(1)}, bf16[96,1024]{1,0:T(8,128)(2,1)S(1)}, u32[]{:S(2)}, u32[]{:S(2)}) collective-permute-start(bf16[96,1024]{1,0:T(8,128)(2,1)S(1)} %get-tuple-element.68), channel_id=1, source_target_pairs={{0,8},{4,12},{8,0},{12,4},{1,9},{5,13},{9,1},{13,5},{2,10},{6,14},... | collective-permute-start | bytes 589832 | tf_op jit(solution)/shard_map/ppermute | solution.py:244
  118.1 18.1 %collective-permute-start.30 = (bf16[96,1024]{1,0:T(8,128)(2,1)S(1)}, bf16[96,1024]{1,0:T(8,128)(2,1)S(1)}, u32[]{:S(2)}, u32[]{:S(2)}) collective-permute-start(bf16[96,1024]{1,0:T(8,128)(2,1)S(1)} %get-tuple-element.69), channel_id=1, source_target_pairs={{0,4},{4,8},{8,12},{12,0},{1,5},{5,9},{9,13},{13,1},{2,6},{6,10},{... | collective-permute-start | bytes 589832 | tf_op jit(solution)/shard_map/ppermute | solution.py:244
  (8 other events, 62.4 us)

commit v4 on v3

--- a/solution.py
+++ b/solution.py
@@ -12,6 +12,7 @@
 LAST = (((1,), (1,)), ((), ()))
 ROW_CHUNKS = 2
 COL_CHUNKS = 2
+SWAPS = 4
 SHIFTED_UP_TO = 8
 
 VMEM = pl.BlockSpec(memory_space=pltpu.VMEM)
@@ -22,7 +23,7 @@
     return lax.dot_general(a, b, dims, preferred_element_type=F32)
 
 
-def call(kernel, out_shape, args, held=(), scratch=(), flops=0, moved=0):
+def call(kernel, out_shape, args, held=(), scratch=()):
     several = isinstance(out_shape, list)
     given = len(args)
 
@@ -36,12 +37,16 @@
         out_specs=[VMEM] * len(out_shape) if several else VMEM,
         scratch_shapes=list(scratch),
         compiler_params=pltpu.CompilerParams(vmem_limit_bytes=24 * 1024 * 1024),
-        cost_estimate=pl.CostEstimate(flops=flops, bytes_accessed=moved, transcendentals=0),
+        cost_estimate=pl.CostEstimate(flops=1, bytes_accessed=1, transcendentals=0),
     )(*args, *held)
 
 
 def shape(rows, cols, dtype):
     return jax.ShapeDtypeStruct((rows, cols), dtype)
+
+
+def made_shape(value):
+    return shape(*value.shape, value.dtype)
 
 
 def padded(size):
@@ -78,12 +83,11 @@
     return first & here, second & here
 
 
-def token_rows_kernel(experts, cap, rotated, ids_t, tok, *outs):
+def token_rows_kernel(experts, cap, rotated, blocks, ids_t, tok, *outs):
     each = outs[0].shape[0]
-    first, second = places(experts, cap, rotated, 0, each * len(outs), ids_t)
-    rows = dot((first | second).astype(F32).astype(BF16), tok[...]).astype(BF16)
-    for i, out in enumerate(outs):
-        out[...] = rows[i * each : (i + 1) * each]
+    for block, out in zip(blocks, outs):
+        first, second = places(experts, cap, rotated, block * each, each, ids_t)
+        out[...] = dot((first | second).astype(F32).astype(BF16), tok[...]).astype(BF16)
 
 
 def cot_rows_kernel(experts, cap, rotated, blocks, ids_t, probs_t, cot, *outs):
@@ -146,6 +150,12 @@
             dst[side * half + used : (side + 1) * half, :] = jnp.zeros((half - used, dst.shape[1]), dst.dtype)
 
 
+def put_rows(value, outs):
+    each = outs[0].shape[0]
+    for i, out in enumerate(outs):
+        out[...] = value[i * each : (i + 1) * each].astype(out.dtype)
+
+
 def halves(size):
     core = lax.axis_index("tensor")
     return core * size, (1 - core) * size
@@ -153,15 +163,16 @@
 
 def front_kernel(sizes, keys, final, own_tok, other_tok, own, *refs):
     pieces, refs = list(zip(keys, refs[: len(keys)])), refs[len(keys) :]
-    weight, act_out = refs[-2:]
+    weight, act_out = refs[:2] if not final else refs[1:3]
     fill_wide(sizes, own, pieces, weight)
     half = own_tok.shape[1]
     mine, theirs = halves(half)
     value = dot(own_tok[...], weight[:, cols_at(mine, half)], LAST) + dot(other_tok[...], weight[:, cols_at(theirs, half)], LAST)
     act_out[...] = value
     if final:
-        gate, hidden_out = refs[:2]
-        hidden_out[...] = (gate[...] * jax.nn.sigmoid(gate[...]) * value).astype(BF16)
+        gate, hidden_out = refs[0], refs[3:]
+        hidden = (gate[...] * jax.nn.sigmoid(gate[...]) * value).astype(BF16)
+        put_rows(hidden, hidden_out)
 
 
 def out_kernel(sizes, keys, part, own_hidden, other_hidden, own, *refs):
@@ -170,28 +181,25 @@
     half = own_hidden.shape[1]
     mine, theirs = halves(half)
     value = dot(own_hidden[...], weight[rows_at(mine, half), :]) + dot(other_hidden[...], weight[rows_at(theirs, half), :])
-    value = value.astype(BF16)
-    each = outs[0].shape[0]
-    for i, out in enumerate(outs):
-        out[...] = value[i * each : (i + 1) * each]
+    put_rows(value, outs)
 
 
 def cot_kernel(n_groups, cots, *refs):
-    weights, (send, keep) = refs[:-2], refs[-2:]
-    half = send.shape[1]
+    weights, keep, send = refs[:COL_CHUNKS], refs[COL_CHUNKS], refs[COL_CHUNKS + 1 :]
+    half = keep.shape[1]
     share = cots.shape[1] // n_groups
     width = share // COL_CHUNKS
     mine, theirs = halves(half)
-    for start, out in ((theirs, send), (mine, keep)):
+    for start, outs in ((theirs, send), (mine, [keep])):
         total = 0.0
         for part, weight in enumerate(weights):
             for g in range(n_groups):
                 rows = cots[:, pl.ds(g * share + part * width, width)]
                 total = total + dot(rows, weight[rows_at(start, half), pl.ds(g * width, width)], LAST)
-        out[...] = total.astype(out.dtype)
-
-
-def grad_kernel(gate, up, kept, received, w_gate, w_up, send, keep):
+        put_rows(total, outs)
+
+
+def grad_kernel(gate, up, kept, received, w_gate, w_up, keep, *send):
     gate_act = gate[...]
     sigmoid_g = jax.nn.sigmoid(gate_act)
     hidden_grad = kept[...] + received[...].astype(F32)
@@ -199,16 +207,13 @@
     up_grad = (hidden_grad * gate_act * sigmoid_g).astype(BF16)
     half = keep.shape[1]
     mine, theirs = halves(half)
-    for start, out in ((theirs, send), (mine, keep)):
+    for start, outs in ((theirs, send), (mine, [keep])):
         cols = cols_at(start, half)
-        out[...] = (dot(gate_grad, w_gate[:, cols]) + dot(up_grad, w_up[:, cols])).astype(out.dtype)
+        put_rows(dot(gate_grad, w_gate[:, cols]) + dot(up_grad, w_up[:, cols]), outs)
 
 
 def add_kernel(kept, received, *outs):
-    value = (kept[...] + received[...].astype(F32)).astype(BF16)
-    each = outs[0].shape[0]
-    for i, out in enumerate(outs):
-        out[...] = value[i * each : (i + 1) * each]
+    put_rows(kept[...] + received[...].astype(F32), outs)
 
 
 def layer_kernel(experts, cap, rotated, n_groups, part, ids_t, probs_t, cot, *refs):
@@ -244,6 +249,16 @@
     return lax.ppermute(value, axis, [(i, (i + step) % size) for i in range(size)])
 
 
+def swapped(parts):
+    return [shift(part, "tensor", 1) for part in parts]
+
+
+def joined(parts):
+    if len(parts) == 1:
+        return parts[0]
+    return call(join_kernel, shape(sum(p.shape[0] for p in parts), parts[0].shape[1], parts[0].dtype), parts)
+
+
 def local(tokens, cotangent, expert_ids, gate_probs, w_gate, w_up, w_down):
     count, half = tokens.shape
     experts, n_dp, n_groups = lax.axis_size("expert"), lax.axis_size("dp"), lax.axis_size("groups")
@@ -254,7 +269,7 @@
     blocks = experts if shifted else 1
     each = rows // blocks
     routing = (experts, cap, shifted)
-    order = [experts // 2] + [s for s in range(1, experts) if s != experts // 2]
+    order = [s for s in range(1, experts) if s != experts // 2] + [experts // 2]
 
     def travel(part, sign, s):
         if shifted:
@@ -283,58 +298,53 @@
         cuts.append(mine)
         x[i] = [shift(mine, "dp", step) for step in range(1, n_dp)]
 
-    def turn_over(i):
+    def turn_over(i, *held):
         y[i] = []
         for step, here in enumerate(x[i], 1):
+            on = call(join_kernel, made_shape(here), (here,), held)
             for turn in range(n_groups):
-                y[i].append(((plan[i][2], step, turn), shift(here, "groups", turn) if turn else here))
+                y[i].append(((plan[i][2], step, turn), shift(on, "groups", turn) if turn else here))
 
     cut(0)
-    tok_send = call(
-        functools.partial(token_rows_kernel, *routing),
-        [shape(each, half, BF16)] * blocks,
-        (ids_t, tokens),
-        cuts[-1:],
-        flops=2 * rows * count * half,
-        moved=2 * (count + rows) * half,
-    )
     cut(1)
 
-    def send_cot(picked, *held):
+    def send(kernel, args, picked, *held):
         made = call(
-            functools.partial(cot_rows_kernel, *routing, picked),
+            functools.partial(kernel, *routing, picked),
             [shape(each, half, BF16)] * len(picked),
-            (ids_t, probs_t, cotangent),
+            args,
             held,
-            flops=2 * each * len(picked) * count * half,
-            moved=2 * (count + each * len(picked)) * half,
         )
         return [travel(part, 1, s) for part, s in zip(made, picked)]
 
-    tok = [travel(part, 1, s) for s, part in enumerate(tok_send)]
-    turn_over(0)
-    turn_over(1)
+    send_tok = functools.partial(send, token_rows_kernel, (ids_t, tokens))
+    send_cot = functools.partial(send, cot_rows_kernel, (ids_t, probs_t, cotangent))
+    last = [()] * len(plan)
+    cot_parts = []
     if shifted:
-        t = [tok[s] for s in order]
-        cut(2, x[0][-1])
-        cut(3, x[1][-1], t[0], t[1])
-        cot = dict(zip((0, order[0]), send_cot((0, order[0]), *t[:-1], x[1][-1])))
-        cut(4, x[2][-1], *t)
-        for i in range(1, len(order)):
-            (cot[order[i]],) = send_cot((order[i],), cot[order[i - 1]], *t)
-        cut(5, x[3][-1], cot[order[0]])
+        tok, cot, now = {}, {}, ()
+        for i, (made, blocks_in, name) in enumerate([(tok, send_tok, s) for s in order] + [(cot, send_cot, s) for s in order]):
+            picked = (name,) if name != order[0] else (0, name)
+            waits = [*now, x[i - 1][-1]] if 0 < i <= len(plan) else list(now)
+            if i:
+                turn_over(i - 1, *(y[i - 3][-1][1:] if i >= 3 else ()), *last[i - 1])
+                if i + 1 < len(plan):
+                    cut(i + 1, x[i - 1][-1], *(y[i - 2][-1][1:] if i >= 2 else ()))
+            made.update(zip(picked, blocks_in(picked, *waits, *(cuts[:1] if i == 0 else ()))))
+            now = (made[name],)
+            if i + 1 < len(plan):
+                last[i + 1] = now
+        turn_over(5, y[3][-1][1], *now)
         cot_parts = [cot[s] for s in range(blocks)]
-        tok_all = call(join_kernel, shape(rows, half, BF16), tok)
+        tok_parts = [tok[s] for s in range(blocks)]
     else:
-        cut(2, x[0][-1])
-        cut(3, x[1][-1])
-        cut(4, x[2][-1])
-        cut(5, x[3][-1])
+        for i in range(len(plan)):
+            if i > 1:
+                cut(i, x[i - 2][-1])
+            turn_over(i)
         cot_parts = send_cot((0,))
-        (tok_all,) = tok
-    for i in range(2, len(plan)):
-        turn_over(i)
-    other_tok = shift(tok_all, "tensor", 1)
+        tok_parts = send_tok((0,))
+    tok_all, other_tok = joined(tok_parts), joined(swapped(tok_parts))
 
     def front(own, picked, gate, *held):
         final = gate is not None
@@ -342,18 +352,16 @@
         act = shape(rows, wide, F32)
         return call(
             functools.partial(front_kernel, sizes, keys, final),
-            ([shape(rows, wide, BF16)] if final else []) + [shape(wide, feats, BF16), act],
+            [shape(wide, feats, BF16), act] + ([shape(rows // SWAPS, wide, BF16)] * SWAPS if final else []),
             (tok_all, other_tok, own, *pieces, *([gate] if final else [])),
             held,
-            flops=2 * rows * feats * units,
-            moved=2 * feats * (rows + units),
         )
 
     first_pieces = range(ROW_CHUNKS)
     gate_weight, gate = front(gate_t, list(first_pieces), None)
-    hidden, up_weight, up = front(up_t, [ROW_CHUNKS + i for i in first_pieces], gate, *cot_parts[1:2])
-    other_hidden = shift(hidden, "tensor", 1)
-    cot_all = call(join_kernel, shape(rows, half, BF16), cot_parts) if shifted else cot_parts[0]
+    up_weight, up, *hidden = front(up_t, [ROW_CHUNKS + i for i in first_pieces], gate)
+    hidden, other_hidden = joined(hidden), joined(swapped(hidden))
+    cot_all = joined(cot_parts)
 
     width = half // n_groups // COL_CHUNKS
     down_weights, layers, sent, prob_part = [], [], [], 0.0
@@ -365,49 +373,47 @@
             [shape(2 * wide, n_groups * width, BF16)] + [shape(each, n_groups * width, BF16)] * blocks,
             (hidden, other_hidden, down, *pieces),
             made[:1],
-            flops=4 * rows * units * n_groups * width,
-            moved=4 * units * n_groups * width,
         )
         down_weights.append(weight)
-        back = [travel(out, -1, s) for s, out in enumerate(made)]
+        back = list(made)
+        if shifted:
+            for lane in ([order[-1]], order[:-1]):
+                for i, s in enumerate(lane):
+                    held = back[lane[i - 1]] if i else sent[-1][lane[-1]] if sent else None
+                    out = back[s] if held is None else call(join_kernel, made_shape(back[s]), (back[s],), (held,))
+                    back[s] = travel(out, -1, s)
+        else:
+            back = [travel(back[0], -1, 0)]
         sent.append(back)
         layer, prob, both = call(
             functools.partial(layer_kernel, *routing, n_groups, part),
             [shape(count, n_groups * width, BF16), shape(expert_ids.shape[1], count, F32), shape(count, rows, BF16)],
             (ids_t, probs_t, cotangent, *back),
-            flops=4 * count * rows * n_groups * width,
-            moved=2 * rows * n_groups * width,
         )
         layers.append(layer)
         prob_part = prob_part + prob
 
-    crossing, kept = call(
+    kept, *crossing = call(
         functools.partial(cot_kernel, n_groups),
-        [shape(rows, wide, BF16), shape(rows, wide, F32)],
+        [shape(rows, wide, F32)] + [shape(rows // SWAPS, wide, BF16)] * SWAPS,
         (cot_all, *down_weights),
         made[:1],
-        flops=4 * rows * half * units,
-        moved=4 * half * units,
     )
-    received = shift(crossing, "tensor", 1)
-    crossing, kept = call(
+    received = joined(swapped(crossing))
+    kept, *crossing = call(
         grad_kernel,
-        [shape(rows, half, BF16), shape(rows, half, F32)],
+        [shape(rows, half, F32)] + [shape(rows // SWAPS, half, BF16)] * SWAPS,
         (gate, up, kept, received, gate_weight, up_weight),
         layers[:1],
-        flops=4 * rows * feats * units,
-        moved=4 * feats * units,
     )
-    received = shift(crossing, "tensor", 1)
-    slots = call(add_kernel, [shape(each, half, BF16)] * blocks, (kept, received), sent[-1][1:3], moved=8 * rows * half)
+    received = joined(swapped(crossing))
+    slots = call(add_kernel, [shape(each, half, BF16)] * blocks, (kept, received), [sent[-1][s] for s in order[::2] if shifted])
     grad_back = [travel(part, -1, s) for s, part in enumerate(slots)]
     grad_probs = (prob_part + shift(prob_part, "tensor", 1)).T
     grad_tokens, layer_out = call(
         functools.partial(token_kernel, n_groups),
         [shape(count, half, BF16)] * 2,
         (both, *grad_back, *layers),
-        flops=2 * count * rows * half,
-        moved=2 * rows * half,
     )
     return (layer_out, grad_tokens, grad_probs)
 

time: 137 us -> 116 us (0.85)
  waiting for transfers between devices: 79.1 us -> 53.3 us
  starting transfers between devices: 40.3 us -> 43.8 us
    ppermute x32 -> x44, waiting for transfers between devices: 79.1 us -> 53.3 us  [shift(): lax.ppermute(value, axis, [(i, (i + step) % size) for i in range(size)])]
    ppermute x32 -> x44, starting transfers between devices: 40.3 us -> 43.8 us  [shift(): lax.ppermute(value, axis, [(i, (i + step) % size) for i in range(size)])]
    pallas_call x22 -> x39, Pallas kernels: 14.1 us -> 15.2 us  [call(): pl.pallas_call(body, out_shape=out_shape, in_specs=[VMEM] * given + [ANY]...]
  transfers between devices with their start and end apart: 32 -> 44, of which waited for: 17 -> 16; matrix products, arithmetic and copies ran while one was open for 0% -> 0% of each run, Pallas kernels for 6% -> 12%
where the time goes in v4:
time: 116 us; the launch traced here: 115 us
  waiting for transfers between devices  53.3 us (46%)
  starting transfers between devices  43.8 us (38%)
  Pallas kernels  15.2 us (13%)
  local copies, waits for them, and re-layouts  1.57 us (1%)
    ppermute x44, waiting for transfers between devices, shift(): lax.ppermute(value, axis, [(i, (i + step) % size) for i in range(size)])  53.3 us
    ppermute x44, starting transfers between devices, shift(): lax.ppermute(value, axis, [(i, (i + step) % size) for i in range(size)])  43.8 us
    pallas_call x39, Pallas kernels, call(): pl.pallas_call(body, out_shape=out_shape, in_specs=[VMEM] * given + [ANY]...  15.2 us
  transfers between devices with their start and end apart: 44, of which 16 were waited for; matrix products, arithmetic and copies ran while one was open for 0% of the time, Pallas kernels for 12%

profile of v4, /device:TPU:0, one launch (start us, length us, event | category | flops | bytes accessed | tf_op | source)
XLA Modules:
  0.0 115.4 jit_solution(9945789009396574248)
XLA Ops:
  0.6 1.4 %copy-done.1 = bf16[1,1024,704]{1,2,0:T(8,128)(2,1)S(1)} copy-done((bf16[1,1024,704]{1,2,0:T(8,128)(2,1)S(1)}, bf16[1,1024,704]{1,2,0:T(8,128)(2,1)}, u32[]{:S(2)}) %copy-start.1) | copy-done | bytes 1441816
  2.0 3.0 %collective-permute-start.1 = (bf16[176,1024]{1,0:T(8,128)(2,1)S(1)}, bf16[176,1024]{1,0:T(8,128)(2,1)S(1)}, u32[]{:S(2)}, u32[]{:S(2)}) collective-permute-start(bf16[176,1024]{1,0:T(8,128)(2,1)S(1)} %shard_map.94.refs_2_.refs_1_), channel_id=1, source_target_pairs={{0,2},{2,0},{1,3},{3,1},{4,6},{6,4},{5,7},{7,5},{8,10},{10,8},{9,1... | collective-permute-start | bytes 1081352 | tf_op jit(solution)/shard_map/ppermute | solution.py:249
  5.7 2.1 %collective-permute-start = (bf16[96,1024]{1,0:T(8,128)(2,1)S(1)}, bf16[96,1024]{1,0:T(8,128)(2,1)S(1)}, u32[]{:S(2)}, u32[]{:S(2)}) collective-permute-start(bf16[96,1024]{1,0:T(8,128)(2,1)S(1)} %get-tuple-element.47), channel_id=1, source_target_pairs={{0,4},{4,8},{8,12},{12,0},{1,5},{5,9},{9,13},{13,1},{2,6},{6,10},{... | collective-permute-start | bytes 589832 | tf_op jit(solution)/shard_map/ppermute | solution.py:249
  7.8 6.5 %collective-permute-done.1.refs_3_.refs_1_.refs_0_ = bf16[176,1024]{1,0:T(8,128)(2,1)S(1)} collective-permute-done((bf16[176,1024]{1,0:T(8,128)(2,1)S(1)}, bf16[176,1024]{1,0:T(8,128)(2,1)S(1)}, u32[]{:S(2)}, u32[]{:S(2)}) %collective-permute-start.1) | collective-permute-done | bytes 360480 | tf_op jit(solution)/shard_map/ppermute | solution.py:249
  14.3 2.2 %collective-permute-start.10 = (bf16[176,1024]{1,0:T(8,128)(2,1)S(1)}, bf16[176,1024]{1,0:T(8,128)(2,1)S(1)}, u32[]{:S(2)}, u32[]{:S(2)}) collective-permute-start(bf16[176,1024]{1,0:T(8,128)(2,1)S(1)} %shard_map.102), channel_id=1, source_target_pairs={{0,16},{16,0},{1,17},{17,1},{2,18},{18,2},{3,19},{19,3},{4,20},{20... | collective-permute-start | bytes 1081352 | tf_op jit(solution)/shard_map/ppermute | solution.py:249
  16.8 3.7 %collective-permute-start.2 = (bf16[96,1024]{1,0:T(8,128)(2,1)S(1)}, bf16[96,1024]{1,0:T(8,128)(2,1)S(1)}, u32[]{:S(2)}, u32[]{:S(2)}) collective-permute-start(bf16[96,1024]{1,0:T(8,128)(2,1)S(1)} %shard_map.96), channel_id=1, source_target_pairs={{0,12},{4,0},{8,4},{12,8},{1,13},{5,1},{9,5},{13,9},{2,14},{6,2},{... | collective-permute-start | bytes 589832 | tf_op jit(solution)/shard_map/ppermute | solution.py:249
  20.5 1.6 %collective-permute-start.9 = (bf16[176,1024]{1,0:T(8,128)(2,1)S(1)}, bf16[176,1024]{1,0:T(8,128)(2,1)S(1)}, u32[]{:S(2)}, u32[]{:S(2)}) collective-permute-start(bf16[176,1024]{1,0:T(8,128)(2,1)S(1)} %shard_map.101.refs_3_), channel_id=1, source_target_pairs={{0,2},{2,0},{1,3},{3,1},{4,6},{6,4},{5,7},{7,5},{8,10},{10,8},{9,1... | collective-permute-start | bytes 1081352 | tf_op jit(solution)/shard_map/ppermute | solution.py:249
  22.1 2.1 %collective-permute-start.13 = (bf16[176,1024]{1,0:T(8,128)(2,1)S(1)}, bf16[176,1024]{1,0:T(8,128)(2,1)S(1)}, u32[]{:S(2)}, u32[]{:S(2)}) collective-permute-start(bf16[176,1024]{1,0:T(8,128)(2,1)S(1)} %shard_map.105), channel_id=1, source_target_pairs={{0,16},{16,0},{1,17},{17,1},{2,18},{18,2},{3,19},{19,3},{4,20},{20... | collective-permute-start | bytes 1081352 | tf_op jit(solution)/shard_map/ppermute | solution.py:249
  24.6 2.7 %collective-permute-start.4 = (bf16[96,1024]{1,0:T(8,128)(2,1)S(1)}, bf16[96,1024]{1,0:T(8,128)(2,1)S(1)}, u32[]{:S(2)}, u32[]{:S(2)}) collective-permute-start(bf16[96,1024]{1,0:T(8,128)(2,1)S(1)} %shard_map.98), channel_id=1, source_target_pairs={{0,8},{4,12},{8,0},{12,4},{1,9},{5,13},{9,1},{13,5},{2,10},{6,14},... | collective-permute-start | bytes 589832 | tf_op jit(solution)/shard_map/ppermute | solution.py:249
  27.3 1.6 %collective-permute-start.12 = (bf16[176,1024]{1,0:T(8,128)(2,1)S(1)}, bf16[176,1024]{1,0:T(8,128)(2,1)S(1)}, u32[]{:S(2)}, u32[]{:S(2)}) collective-permute-start(bf16[176,1024]{1,0:T(8,128)(2,1)S(1)} %shard_map.104.refs_3_), channel_id=1, source_target_pairs={{0,2},{2,0},{1,3},{3,1},{4,6},{6,4},{5,7},{7,5},{8,10},{10,8},{9,1... | collective-permute-start | bytes 1081352 | tf_op jit(solution)/shard_map/ppermute | solution.py:249
  28.8 1.8 %collective-permute-done.9.refs_0_.refs_3_.refs_1_.refs_4_ = bf16[176,1024]{1,0:T(8,128)(2,1)S(1)} collective-permute-done((bf16[176,1024]{1,0:T(8,128)(2,1)S(1)}, bf16[176,1024]{1,0:T(8,128)(2,1)S(1)}, u32[]{:S(2)}, u32[]{:S(2)}) %collective-permute-start.9) | collective-permute-done | bytes 360480 | tf_op jit(solution)/shard_map/ppermute | solution.py:249
  30.6 1.9 %collective-permute-start.11 = (bf16[176,1024]{1,0:T(8,128)(2,1)S(1)}, bf16[176,1024]{1,0:T(8,128)(2,1)S(1)}, u32[]{:S(2)}, u32[]{:S(2)}) collective-permute-start(bf16[176,1024]{1,0:T(8,128)(2,1)S(1)} %shard_map.103), channel_id=1, source_target_pairs={{0,16},{16,0},{1,17},{17,1},{2,18},{18,2},{3,19},{19,3},{4,20},{20... | collective-permute-start | bytes 1081352 | tf_op jit(solution)/shard_map/ppermute | solution.py:249
  32.5 1.6 %collective-permute-done.4.refs_2_.refs_3_ = bf16[96,1024]{1,0:T(8,128)(2,1)S(1)} collective-permute-done((bf16[96,1024]{1,0:T(8,128)(2,1)S(1)}, bf16[96,1024]{1,0:T(8,128)(2,1)S(1)}, u32[]{:S(2)}, u32[]{:S(2)}) %collective-permute-start.4) | collective-permute-done | bytes 196640 | tf_op jit(solution)/shard_map/ppermute | solution.py:249
  35.7 1.6 %collective-permute-start.22 = (bf16[704,256]{1,0:T(8,128)(2,1)S(1)}, bf16[704,256]{1,0:T(8,128)(2,1)S(1)}, u32[]{:S(2)}, u32[]{:S(2)}) collective-permute-start(bf16[704,256]{1,0:T(8,128)(2,1)S(1)} %shard_map.111.refs_3_), channel_id=1, source_target_pairs={{0,2},{2,0},{1,3},{3,1},{4,6},{6,4},{5,7},{7,5},{8,10},{10,8},{9,1... | collective-permute-start | bytes 1081352 | tf_op jit(solution)/shard_map/ppermute | solution.py:249
  37.3 4.9 %collective-permute-done.20.refs_3_.refs_2_.refs_1_ = bf16[96,1024]{1,0:T(8,128)(2,1)S(1)} collective-permute-done((bf16[96,1024]{1,0:T(8,128)(2,1)S(1)}, bf16[96,1024]{1,0:T(8,128)(2,1)S(1)}, u32[]{:S(2)}, u32[]{:S(2)}) %collective-permute-start.20) | collective-permute-done | bytes 196640 | tf_op jit(solution)/shard_map/ppermute | solution.py:249
  42.5 2.1 %collective-permute-start.21 = (bf16[96,1024]{1,0:T(8,128)(2,1)S(1)}, bf16[96,1024]{1,0:T(8,128)(2,1)S(1)}, u32[]{:S(2)}, u32[]{:S(2)}) collective-permute-start(bf16[96,1024]{1,0:T(8,128)(2,1)S(1)} %shard_map.114), channel_id=1, source_target_pairs={{0,12},{4,0},{8,4},{12,8},{1,13},{5,1},{9,5},{13,9},{2,14},{6,2},{... | collective-permute-start | bytes 589832 | tf_op jit(solution)/shard_map/ppermute | solution.py:249
  45.7 1.6 %collective-permute-start.19 = (bf16[704,256]{1,0:T(8,128)(2,1)S(1)}, bf16[704,256]{1,0:T(8,128)(2,1)S(1)}, u32[]{:S(2)}, u32[]{:S(2)}) collective-permute-start(bf16[704,256]{1,0:T(8,128)(2,1)S(1)} %shard_map.112), channel_id=1, source_target_pairs={{0,2},{2,0},{1,3},{3,1},{4,6},{6,4},{5,7},{7,5},{8,10},{10,8},{9,1... | collective-permute-start | bytes 1081352 | tf_op jit(solution)/shard_map/ppermute | solution.py:249
  51.0 1.6 %shard_map.107 = (bf16[768,2048]{1,0:T(8,128)(2,1)S(1)}, f32[384,768]{1,0:T(8,128)S(1)}) custom-call(bf16[384,1024]{1,0:T(8,128)(2,1)S(1)} %shard_map.99.refs_0_, bf16[384,1024]{1,0:T(8,128)(2,1)S(1)} %shard_map.100.refs_1_, bf16[704,1024]{1,0:T(8,128)(2,1)S(1)} %bitcast.17, bf16[176,1024]{1,0:T(8,128)(2,1)S(1)} %collective-permute-done.1.refs_3_.refs_1_.refs_0_, ...), custom_call_target="tpu_custom_call" | custom-call | flops 1 | bytes 1 | tf_op jit(solution)/shard_map/pallas_call | solution.py:33
  52.7 1.6 %shard_map.108 = (bf16[768,2048]{1,0:T(8,128)(2,1)S(1)}, f32[384,768]{1,0:T(8,128)S(1)}, bf16[96,768]{1,0:T(8,128)(2,1)S(1)}, bf16[96,768]{1,0:T(8,128)(2,1)S(1)...) custom-call(bf16[384,1024]{1,0:T(8,128)(2,1)S(1)} %shard_map.99.refs_0_, ...), custom_call_target="tpu_custom_call" | custom-call | flops 1 | bytes 1 | tf_op jit(solution)/shard_map/pallas_call | solution.py:33
  54.6 1.5 %collective-permute-done.19.refs_0_.refs_3_ = bf16[704,256]{1,0:T(8,128)(2,1)S(1)} collective-permute-done((bf16[704,256]{1,0:T(8,128)(2,1)S(1)}, bf16[704,256]{1,0:T(8,128)(2,1)S(1)}, u32[]{:S(2)}, u32[]{:S(2)}) %collective-permute-start.19) | collective-permute-done | bytes 360480 | tf_op jit(solution)/shard_map/ppermute | solution.py:249
  56.2 4.9 %collective-permute-done.23.refs_2_ = bf16[96,1024]{1,0:T(8,128)(2,1)S(1)} collective-permute-done((bf16[96,1024]{1,0:T(8,128)(2,1)S(1)}, bf16[96,1024]{1,0:T(8,128)(2,1)S(1)}, u32[]{:S(2)}, u32[]{:S(2)}) %collective-permute-start.23) | collective-permute-done | bytes 196640 | tf_op jit(solution)/shard_map/ppermute | solution.py:249
  64.7 2.3 %collective-permute-start.26 = (bf16[96,512]{1,0:T(8,128)(2,1)S(1)}, bf16[96,512]{1,0:T(8,128)(2,1)S(1)}, u32[]{:S(2)}, u32[]{:S(2)}) collective-permute-start(bf16[96,512]{1,0:T(8,128)(2,1)S(1)} %get-tuple-element.58), channel_id=1, source_target_pairs={{0,12},{4,0},{8,4},{12,8},{1,13},{5,1},{9,5},{13,9},{2,14},{6,2},{... | collective-permute-start | bytes 294920 | tf_op jit(solution)/shard_map/ppermute | solution.py:249
  66.9 2.7 %collective-permute-done.26.refs_1_.refs_4_ = bf16[96,512]{1,0:T(8,128)(2,1)S(1)} collective-permute-done((bf16[96,512]{1,0:T(8,128)(2,1)S(1)}, bf16[96,512]{1,0:T(8,128)(2,1)S(1)}, u32[]{:S(2)}, u32[]{:S(2)}) %collective-permute-start.26) | collective-permute-done | bytes 98336 | tf_op jit(solution)/shard_map/ppermute | solution.py:249
  70.0 4.3 %collective-permute-start.29 = (bf16[96,512]{1,0:T(8,128)(2,1)S(1)}, bf16[96,512]{1,0:T(8,128)(2,1)S(1)}, u32[]{:S(2)}, u32[]{:S(2)}) collective-permute-start(bf16[96,512]{1,0:T(8,128)(2,1)S(1)} %get-tuple-element.60), channel_id=1, source_target_pairs={{0,8},{4,12},{8,0},{12,4},{1,9},{5,13},{9,1},{13,5},{2,10},{6,14},... | collective-permute-start | bytes 294920 | tf_op jit(solution)/shard_map/ppermute | solution.py:249
  75.2 1.4 %shard_map.126 = (f32[384,768]{1,0:T(8,128)S(1)}, bf16[96,768]{1,0:T(8,128)(2,1)S(1)}, bf16[96,768]{1,0:T(8,128)(2,1)S(1)}, bf16[96,768]{1,0:T(8,128)(2,1)S(1)}, bf16[96,768]{1,0:T(8,128)(2,1)S(1)}) custom-call(bf16[384,1024]{1,0:T(8,128)(2,1)S(1)} %shard_map.125.refs_0_, bf16[1536,512]{1,0:T(8,128)(2,1)S(1)} %get-tuple-element.65.refs_1_, ...), custom_call_target="tpu_custom_call" | custom-call | flops 1 | bytes 1 | tf_op jit(solution)/shard_map/pallas_call | solution.py:33
  77.8 2.5 %collective-permute-done.29.refs_1_.refs_5_ = bf16[96,512]{1,0:T(8,128)(2,1)S(1)} collective-permute-done((bf16[96,512]{1,0:T(8,128)(2,1)S(1)}, bf16[96,512]{1,0:T(8,128)(2,1)S(1)}, u32[]{:S(2)}, u32[]{:S(2)}) %collective-permute-start.29) | collective-permute-done | bytes 98336 | tf_op jit(solution)/shard_map/ppermute | solution.py:249
  82.3 2.7 %shard_map.129 = (f32[384,1024]{1,0:T(8,128)S(1)}, bf16[96,1024]{1,0:T(8,128)(2,1)S(1)}, bf16[96,1024]{1,0:T(8,128)(2,1)S(1)}, bf16[96,1024]{1,0:T(8,128)(2,1)S(1)}, bf16[96,1024]{1,0:T(8,128)(2,1)S(1)}) custom-call(f32[384,768]{1,0:T(8,128)S(1)} %get-tuple-element.48.refs_7_.refs_0_, f32[384,768]{1,0:T(8,128)S(1)} %get-tuple-element.63.refs_1_, ...), custom_call_target="tpu_custom_call" | custom-call | flops 1 | bytes 1 | tf_op jit(solution)/shard_map/pallas_call | solution.py:33
  86.0 3.3 %collective-permute-done.30.refs_5_.refs_3_ = bf16[96,512]{1,0:T(8,128)(2,1)S(1)} collective-permute-done((bf16[96,512]{1,0:T(8,128)(2,1)S(1)}, bf16[96,512]{1,0:T(8,128)(2,1)S(1)}, u32[]{:S(2)}, u32[]{:S(2)}) %collective-permute-start.30) | collective-permute-done | bytes 98336 | tf_op jit(solution)/shard_map/ppermute | solution.py:249
  89.4 6.4 %collective-permute-done.31.refs_6_ = bf16[96,512]{1,0:T(8,128)(2,1)S(1)} collective-permute-done((bf16[96,512]{1,0:T(8,128)(2,1)S(1)}, bf16[96,512]{1,0:T(8,128)(2,1)S(1)}, u32[]{:S(2)}, u32[]{:S(2)}) %collective-permute-start.31) | collective-permute-done | bytes 98336 | tf_op jit(solution)/shard_map/ppermute | solution.py:249
  97.2 1.6 %collective-permute-start.42 = (bf16[96,1024]{1,0:T(8,128)(2,1)S(1)}, bf16[96,1024]{1,0:T(8,128)(2,1)S(1)}, u32[]{:S(2)}, u32[]{:S(2)}) collective-permute-start(bf16[96,1024]{1,0:T(8,128)(2,1)S(1)} %get-tuple-element.83), channel_id=1, source_target_pairs={{0,4},{4,8},{8,12},{12,0},{1,5},{5,9},{9,13},{13,1},{2,6},{6,10},{... | collective-permute-start | bytes 589832 | tf_op jit(solution)/shard_map/ppermute | solution.py:249
  99.4 5.8 %collective-permute-done.40.refs_2_ = bf16[96,1024]{1,0:T(8,128)(2,1)S(1)} collective-permute-done((bf16[96,1024]{1,0:T(8,128)(2,1)S(1)}, bf16[96,1024]{1,0:T(8,128)(2,1)S(1)}, u32[]{:S(2)}, u32[]{:S(2)}) %collective-permute-start.40) | collective-permute-done | bytes 196640 | tf_op jit(solution)/shard_map/ppermute | solution.py:249
  105.2 9.1 %collective-permute-done.41.refs_3_ = bf16[96,1024]{1,0:T(8,128)(2,1)S(1)} collective-permute-done((bf16[96,1024]{1,0:T(8,128)(2,1)S(1)}, bf16[96,1024]{1,0:T(8,128)(2,1)S(1)}, u32[]{:S(2)}, u32[]{:S(2)}) %collective-permute-start.41) | collective-permute-done | bytes 196640 | tf_op jit(solution)/shard_map/ppermute | solution.py:249
  (113 shorter events, 20.6 us)
Async XLA Ops:
  2.0 12.2 %collective-permute-start.1 = (bf16[176,1024]{1,0:T(8,128)(2,1)S(1)}, bf16[176,1024]{1,0:T(8,128)(2,1)S(1)}, u32[]{:S(2)}, u32[]{:S(2)}) collective-permute-start(bf16[176,1024]{1,0:T(8,128)(2,1)S(1)} %shard_map.94.refs_2_.refs_1_), channel_id=1, source_target_pairs={{0,2},{2,0},{1,3},{3,1},{4,6},{6,4},{5,7},{7,5},{8,10},{10,8},{9,1... | collective-permute-start | bytes 1081352 | tf_op jit(solution)/shard_map/ppermute | solution.py:249
  5.1 17.0 %collective-permute-start.3 = (bf16[176,1024]{1,0:T(8,128)(2,1)S(1)}, bf16[176,1024]{1,0:T(8,128)(2,1)S(1)}, u32[]{:S(2)}, u32[]{:S(2)}) collective-permute-start(bf16[176,1024]{1,0:T(8,128)(2,1)S(1)} %shard_map.97.refs_2_), channel_id=1, source_target_pairs={{0,2},{2,0},{1,3},{3,1},{4,6},{6,4},{5,7},{7,5},{8,10},{10,8},{9,1... | collective-permute-start | bytes 1081352 | tf_op jit(solution)/shard_map/ppermute | solution.py:249
  5.7 10.8 %collective-permute-start = (bf16[96,1024]{1,0:T(8,128)(2,1)S(1)}, bf16[96,1024]{1,0:T(8,128)(2,1)S(1)}, u32[]{:S(2)}, u32[]{:S(2)}) collective-permute-start(bf16[96,1024]{1,0:T(8,128)(2,1)S(1)} %get-tuple-element.47), channel_id=1, source_target_pairs={{0,4},{4,8},{8,12},{12,0},{1,5},{5,9},{9,13},{13,1},{2,6},{6,10},{... | collective-permute-start | bytes 589832 | tf_op jit(solution)/shard_map/ppermute | solution.py:249
  14.3 12.9 %collective-permute-start.10 = (bf16[176,1024]{1,0:T(8,128)(2,1)S(1)}, bf16[176,1024]{1,0:T(8,128)(2,1)S(1)}, u32[]{:S(2)}, u32[]{:S(2)}) collective-permute-start(bf16[176,1024]{1,0:T(8,128)(2,1)S(1)} %shard_map.102), channel_id=1, source_target_pairs={{0,16},{16,0},{1,17},{17,1},{2,18},{18,2},{3,19},{19,3},{4,20},{20... | collective-permute-start | bytes 1081352 | tf_op jit(solution)/shard_map/ppermute | solution.py:249
  16.8 7.4 %collective-permute-start.2 = (bf16[96,1024]{1,0:T(8,128)(2,1)S(1)}, bf16[96,1024]{1,0:T(8,128)(2,1)S(1)}, u32[]{:S(2)}, u32[]{:S(2)}) collective-permute-start(bf16[96,1024]{1,0:T(8,128)(2,1)S(1)} %shard_map.96), channel_id=1, source_target_pairs={{0,12},{4,0},{8,4},{12,8},{1,13},{5,1},{9,5},{13,9},{2,14},{6,2},{... | collective-permute-start | bytes 589832 | tf_op jit(solution)/shard_map/ppermute | solution.py:249
  20.5 10.1 %collective-permute-start.9 = (bf16[176,1024]{1,0:T(8,128)(2,1)S(1)}, bf16[176,1024]{1,0:T(8,128)(2,1)S(1)}, u32[]{:S(2)}, u32[]{:S(2)}) collective-permute-start(bf16[176,1024]{1,0:T(8,128)(2,1)S(1)} %shard_map.101.refs_3_), channel_id=1, source_target_pairs={{0,2},{2,0},{1,3},{3,1},{4,6},{6,4},{5,7},{7,5},{8,10},{10,8},{9,1... | collective-permute-start | bytes 1081352 | tf_op jit(solution)/shard_map/ppermute | solution.py:249
  22.1 13.6 %collective-permute-start.13 = (bf16[176,1024]{1,0:T(8,128)(2,1)S(1)}, bf16[176,1024]{1,0:T(8,128)(2,1)S(1)}, u32[]{:S(2)}, u32[]{:S(2)}) collective-permute-start(bf16[176,1024]{1,0:T(8,128)(2,1)S(1)} %shard_map.105), channel_id=1, source_target_pairs={{0,16},{16,0},{1,17},{17,1},{2,18},{18,2},{3,19},{19,3},{4,20},{20... | collective-permute-start | bytes 1081352 | tf_op jit(solution)/shard_map/ppermute | solution.py:249
  24.6 9.5 %collective-permute-start.4 = (bf16[96,1024]{1,0:T(8,128)(2,1)S(1)}, bf16[96,1024]{1,0:T(8,128)(2,1)S(1)}, u32[]{:S(2)}, u32[]{:S(2)}) collective-permute-start(bf16[96,1024]{1,0:T(8,128)(2,1)S(1)} %shard_map.98), channel_id=1, source_target_pairs={{0,8},{4,12},{8,0},{12,4},{1,9},{5,13},{9,1},{13,5},{2,10},{6,14},... | collective-permute-start | bytes 589832 | tf_op jit(solution)/shard_map/ppermute | solution.py:249
  27.3 14.9 %collective-permute-start.12 = (bf16[176,1024]{1,0:T(8,128)(2,1)S(1)}, bf16[176,1024]{1,0:T(8,128)(2,1)S(1)}, u32[]{:S(2)}, u32[]{:S(2)}) collective-permute-start(bf16[176,1024]{1,0:T(8,128)(2,1)S(1)} %shard_map.104.refs_3_), channel_id=1, source_target_pairs={{0,2},{2,0},{1,3},{3,1},{4,6},{6,4},{5,7},{7,5},{8,10},{10,8},{9,1... | collective-permute-start | bytes 1081352 | tf_op jit(solution)/shard_map/ppermute | solution.py:249
  30.6 14.5 %collective-permute-start.11 = (bf16[176,1024]{1,0:T(8,128)(2,1)S(1)}, bf16[176,1024]{1,0:T(8,128)(2,1)S(1)}, u32[]{:S(2)}, u32[]{:S(2)}) collective-permute-start(bf16[176,1024]{1,0:T(8,128)(2,1)S(1)} %shard_map.103), channel_id=1, source_target_pairs={{0,16},{16,0},{1,17},{17,1},{2,18},{18,2},{3,19},{19,3},{4,20},{20... | collective-permute-start | bytes 1081352 | tf_op jit(solution)/shard_map/ppermute | solution.py:249
  34.6 7.5 %collective-permute-start.20 = (bf16[96,1024]{1,0:T(8,128)(2,1)S(1)}, bf16[96,1024]{1,0:T(8,128)(2,1)S(1)}, u32[]{:S(2)}, u32[]{:S(2)}) collective-permute-start(bf16[96,1024]{1,0:T(8,128)(2,1)S(1)} %get-tuple-element.53), channel_id=1, source_target_pairs={{0,4},{4,8},{8,12},{12,0},{1,5},{5,9},{9,13},{13,1},{2,6},{6,10},{... | collective-permute-start | bytes 589832 | tf_op jit(solution)/shard_map/ppermute | solution.py:249
  35.7 10.0 %collective-permute-start.22 = (bf16[704,256]{1,0:T(8,128)(2,1)S(1)}, bf16[704,256]{1,0:T(8,128)(2,1)S(1)}, u32[]{:S(2)}, u32[]{:S(2)}) collective-permute-start(bf16[704,256]{1,0:T(8,128)(2,1)S(1)} %shard_map.111.refs_3_), channel_id=1, source_target_pairs={{0,2},{2,0},{1,3},{3,1},{4,6},{6,4},{5,7},{7,5},{8,10},{10,8},{9,1... | collective-permute-start | bytes 1081352 | tf_op jit(solution)/shard_map/ppermute | solution.py:249
  37.3 7.9 %collective-permute-start.5 = (bf16[96,1024]{1,0:T(8,128)(2,1)S(1)}, bf16[96,1024]{1,0:T(8,128)(2,1)S(1)}, u32[]{:S(2)}, u32[]{:S(2)}) collective-permute-start(bf16[96,1024]{1,0:T(8,128)(2,1)S(1)} %get-tuple-element.46.refs_0_), channel_id=1, source_target_pairs={{0,1},{1,0},{2,3},{3,2},{4,5},{5,4},{6,7},{7,6},{8,9},{9,8},{10,11... | collective-permute-start | bytes 589832 | tf_op jit(solution)/shard_map/ppermute | solution.py:249
  42.5 5.7 %collective-permute-start.21 = (bf16[96,1024]{1,0:T(8,128)(2,1)S(1)}, bf16[96,1024]{1,0:T(8,128)(2,1)S(1)}, u32[]{:S(2)}, u32[]{:S(2)}) collective-permute-start(bf16[96,1024]{1,0:T(8,128)(2,1)S(1)} %shard_map.114), channel_id=1, source_target_pairs={{0,12},{4,0},{8,4},{12,8},{1,13},{5,1},{9,5},{13,9},{2,14},{6,2},{... | collective-permute-start | bytes 589832 | tf_op jit(solution)/shard_map/ppermute | solution.py:249
  44.6 8.1 %collective-permute-start.14 = (bf16[176,1024]{1,0:T(8,128)(2,1)S(1)}, bf16[176,1024]{1,0:T(8,128)(2,1)S(1)}, u32[]{:S(2)}, u32[]{:S(2)}) collective-permute-start(bf16[176,1024]{1,0:T(8,128)(2,1)S(1)} %shard_map.106), channel_id=1, source_target_pairs={{0,16},{16,0},{1,17},{17,1},{2,18},{18,2},{3,19},{19,3},{4,20},{20... | collective-permute-start | bytes 1081352 | tf_op jit(solution)/shard_map/ppermute | solution.py:249
  45.7 10.5 %collective-permute-start.19 = (bf16[704,256]{1,0:T(8,128)(2,1)S(1)}, bf16[704,256]{1,0:T(8,128)(2,1)S(1)}, u32[]{:S(2)}, u32[]{:S(2)}) collective-permute-start(bf16[704,256]{1,0:T(8,128)(2,1)S(1)} %shard_map.112), channel_id=1, source_target_pairs={{0,2},{2,0},{1,3},{3,1},{4,6},{6,4},{5,7},{7,5},{8,10},{10,8},{9,1... | collective-permute-start | bytes 1081352 | tf_op jit(solution)/shard_map/ppermute | solution.py:249
  48.5 12.5 %collective-permute-start.23 = (bf16[96,1024]{1,0:T(8,128)(2,1)S(1)}, bf16[96,1024]{1,0:T(8,128)(2,1)S(1)}, u32[]{:S(2)}, u32[]{:S(2)}) collective-permute-start(bf16[96,1024]{1,0:T(8,128)(2,1)S(1)} %shard_map.115), channel_id=1, source_target_pairs={{0,8},{4,12},{8,0},{12,4},{1,9},{5,13},{9,1},{13,5},{2,10},{6,14},... | collective-permute-start | bytes 589832 | tf_op jit(solution)/shard_map/ppermute | solution.py:249
  49.7 14.1 %collective-permute-start.25 = (bf16[704,256]{1,0:T(8,128)(2,1)S(1)}, bf16[704,256]{1,0:T(8,128)(2,1)S(1)}, u32[]{:S(2)}, u32[]{:S(2)}) collective-permute-start(bf16[704,256]{1,0:T(8,128)(2,1)S(1)} %shard_map.117), channel_id=1, source_target_pairs={{0,16},{16,0},{1,17},{17,1},{2,18},{18,2},{3,19},{19,3},{4,20},{20... | collective-permute-start | bytes 1081352 | tf_op jit(solution)/shard_map/ppermute | solution.py:249
  54.3 8.0 %collective-permute-start.15 = (bf16[96,768]{1,0:T(8,128)(2,1)S(1)}, bf16[96,768]{1,0:T(8,128)(2,1)S(1)}, u32[]{:S(2)}, u32[]{:S(2)}) collective-permute-start(bf16[96,768]{1,0:T(8,128)(2,1)S(1)} %get-tuple-element.49.refs_0_), channel_id=1, source_target_pairs={{0,1},{1,0},{2,3},{3,2},{4,5},{5,4},{6,7},{7,6},{8,9},{9,8},{10,11... | collective-permute-start | bytes 442376 | tf_op jit(solution)/shard_map/ppermute | solution.py:249
  61.1 13.3 %collective-permute-start.24 = (bf16[704,256]{1,0:T(8,128)(2,1)S(1)}, bf16[704,256]{1,0:T(8,128)(2,1)S(1)}, u32[]{:S(2)}, u32[]{:S(2)}) collective-permute-start(bf16[704,256]{1,0:T(8,128)(2,1)S(1)} %shard_map.116), channel_id=1, source_target_pairs={{0,16},{16,0},{1,17},{17,1},{2,18},{18,2},{3,19},{19,3},{4,20},{20... | collective-permute-start | bytes 1081352 | tf_op jit(solution)/shard_map/ppermute | solution.py:249
  69.6 7.7 %collective-permute-start.27 = (bf16[96,512]{1,0:T(8,128)(2,1)S(1)}, bf16[96,512]{1,0:T(8,128)(2,1)S(1)}, u32[]{:S(2)}, u32[]{:S(2)}) collective-permute-start(bf16[96,512]{1,0:T(8,128)(2,1)S(1)} %shard_map.120), channel_id=1, source_target_pairs={{0,4},{4,8},{8,12},{12,0},{1,5},{5,9},{9,13},{13,1},{2,6},{6,10},{... | collective-permute-start | bytes 294920 | tf_op jit(solution)/shard_map/ppermute | solution.py:249
  70.0 10.3 %collective-permute-start.29 = (bf16[96,512]{1,0:T(8,128)(2,1)S(1)}, bf16[96,512]{1,0:T(8,128)(2,1)S(1)}, u32[]{:S(2)}, u32[]{:S(2)}) collective-permute-start(bf16[96,512]{1,0:T(8,128)(2,1)S(1)} %get-tuple-element.60), channel_id=1, source_target_pairs={{0,8},{4,12},{8,0},{12,4},{1,9},{5,13},{9,1},{13,5},{2,10},{6,14},... | collective-permute-start | bytes 294920 | tf_op jit(solution)/shard_map/ppermute | solution.py:249
  76.7 5.5 %collective-permute-start.33 = (bf16[96,768]{1,0:T(8,128)(2,1)S(1)}, bf16[96,768]{1,0:T(8,128)(2,1)S(1)}, u32[]{:S(2)}, u32[]{:S(2)}) collective-permute-start(bf16[96,768]{1,0:T(8,128)(2,1)S(1)} %get-tuple-element.69), channel_id=1, source_target_pairs={{0,1},{1,0},{2,3},{3,2},{4,5},{5,4},{6,7},{7,6},{8,9},{9,8},{10,11... | collective-permute-start | bytes 442376 | tf_op jit(solution)/shard_map/ppermute | solution.py:249
  82.1 7.3 %collective-permute-start.30 = (bf16[96,512]{1,0:T(8,128)(2,1)S(1)}, bf16[96,512]{1,0:T(8,128)(2,1)S(1)}, u32[]{:S(2)}, u32[]{:S(2)}) collective-permute-start(bf16[96,512]{1,0:T(8,128)(2,1)S(1)} %shard_map.122), channel_id=1, source_target_pairs={{0,8},{4,12},{8,0},{12,4},{1,9},{5,13},{9,1},{13,5},{2,10},{6,14},... | collective-permute-start | bytes 294920 | tf_op jit(solution)/shard_map/ppermute | solution.py:249
  84.9 11.6 %collective-permute-start.36 = (bf16[96,1024]{1,0:T(8,128)(2,1)S(1)}, bf16[96,1024]{1,0:T(8,128)(2,1)S(1)}, u32[]{:S(2)}, u32[]{:S(2)}) collective-permute-start(bf16[96,1024]{1,0:T(8,128)(2,1)S(1)} %get-tuple-element.76), channel_id=1, source_target_pairs={{0,1},{1,0},{2,3},{3,2},{4,5},{5,4},{6,7},{7,6},{8,9},{9,8},{10,11... | collective-permute-start | bytes 589832 | tf_op jit(solution)/shard_map/ppermute | solution.py:249
  85.0 11.5 %collective-permute-start.37 = (bf16[96,1024]{1,0:T(8,128)(2,1)S(1)}, bf16[96,1024]{1,0:T(8,128)(2,1)S(1)}, u32[]{:S(2)}, u32[]{:S(2)}) collective-permute-start(bf16[96,1024]{1,0:T(8,128)(2,1)S(1)} %get-tuple-element.77), channel_id=1, source_target_pairs={{0,1},{1,0},{2,3},{3,2},{4,5},{5,4},{6,7},{7,6},{8,9},{9,8},{10,11... | collective-permute-start | bytes 589832 | tf_op jit(solution)/shard_map/ppermute | solution.py:249
  85.5 11.0 %collective-permute-start.38 = (bf16[96,1024]{1,0:T(8,128)(2,1)S(1)}, bf16[96,1024]{1,0:T(8,128)(2,1)S(1)}, u32[]{:S(2)}, u32[]{:S(2)}) collective-permute-start(bf16[96,1024]{1,0:T(8,128)(2,1)S(1)} %get-tuple-element.78), channel_id=1, source_target_pairs={{0,1},{1,0},{2,3},{3,2},{4,5},{5,4},{6,7},{7,6},{8,9},{9,8},{10,11... | collective-permute-start | bytes 589832 | tf_op jit(solution)/shard_map/ppermute | solution.py:249
  85.6 11.0 %collective-permute-start.39 = (bf16[96,1024]{1,0:T(8,128)(2,1)S(1)}, bf16[96,1024]{1,0:T(8,128)(2,1)S(1)}, u32[]{:S(2)}, u32[]{:S(2)}) collective-permute-start(bf16[96,1024]{1,0:T(8,128)(2,1)S(1)} %get-tuple-element.79), channel_id=1, source_target_pairs={{0,1},{1,0},{2,3},{3,2},{4,5},{5,4},{6,7},{7,6},{8,9},{9,8},{10,11... | collective-permute-start | bytes 589832 | tf_op jit(solution)/shard_map/ppermute | solution.py:249
  89.4 6.4 %collective-permute-start.31 = (bf16[96,512]{1,0:T(8,128)(2,1)S(1)}, bf16[96,512]{1,0:T(8,128)(2,1)S(1)}, u32[]{:S(2)}, u32[]{:S(2)}) collective-permute-start(bf16[96,512]{1,0:T(8,128)(2,1)S(1)} %shard_map.123), channel_id=1, source_target_pairs={{0,4},{4,8},{8,12},{12,0},{1,5},{5,9},{9,13},{13,1},{2,6},{6,10},{... | collective-permute-start | bytes 294920 | tf_op jit(solution)/shard_map/ppermute | solution.py:249
  96.8 8.5 %collective-permute-start.40 = (bf16[96,1024]{1,0:T(8,128)(2,1)S(1)}, bf16[96,1024]{1,0:T(8,128)(2,1)S(1)}, u32[]{:S(2)}, u32[]{:S(2)}) collective-permute-start(bf16[96,1024]{1,0:T(8,128)(2,1)S(1)} %get-tuple-element.81), channel_id=1, source_target_pairs={{0,12},{4,0},{8,4},{12,8},{1,13},{5,1},{9,5},{13,9},{2,14},{6,2},{... | collective-permute-start | bytes 589832 | tf_op jit(solution)/shard_map/ppermute | solution.py:249
  97.2 17.2 %collective-permute-start.41 = (bf16[96,1024]{1,0:T(8,128)(2,1)S(1)}, bf16[96,1024]{1,0:T(8,128)(2,1)S(1)}, u32[]{:S(2)}, u32[]{:S(2)}) collective-permute-start(bf16[96,1024]{1,0:T(8,128)(2,1)S(1)} %get-tuple-element.82), channel_id=1, source_target_pairs={{0,8},{4,12},{8,0},{12,4},{1,9},{5,13},{9,1},{13,5},{2,10},{6,14},... | collective-permute-start | bytes 589832 | tf_op jit(solution)/shard_map/ppermute | solution.py:249
  97.2 17.2 %collective-permute-start.42 = (bf16[96,1024]{1,0:T(8,128)(2,1)S(1)}, bf16[96,1024]{1,0:T(8,128)(2,1)S(1)}, u32[]{:S(2)}, u32[]{:S(2)}) collective-permute-start(bf16[96,1024]{1,0:T(8,128)(2,1)S(1)} %get-tuple-element.83), channel_id=1, source_target_pairs={{0,4},{4,8},{8,12},{12,0},{1,5},{5,9},{9,13},{13,1},{2,6},{6,10},{... | collective-permute-start | bytes 589832 | tf_op jit(solution)/shard_map/ppermute | solution.py:249
  (20 other events, 94.9 us)

commit v5 on v4

--- a/solution.py
+++ b/solution.py
@@ -83,21 +83,19 @@
     return first & here, second & here
 
 
-def token_rows_kernel(experts, cap, rotated, blocks, ids_t, tok, *outs):
-    each = outs[0].shape[0]
-    for block, out in zip(blocks, outs):
-        first, second = places(experts, cap, rotated, block * each, each, ids_t)
-        out[...] = dot((first | second).astype(F32).astype(BF16), tok[...]).astype(BF16)
-
-
-def cot_rows_kernel(experts, cap, rotated, blocks, ids_t, probs_t, cot, *outs):
-    each = outs[0].shape[0]
+def rows_kernel(experts, cap, rotated, blocks, ids_t, probs_t, tok, cot, *outs):
+    each = outs[0].shape[0] // 2
     for block, out in zip(blocks, outs):
         first, second = places(experts, cap, rotated, block * each, each, ids_t)
         weight = jnp.where(first, probs_t[0:1, :], jnp.where(second, probs_t[1:2, :], 0.0))
         weight = jnp.sum(weight, axis=1, keepdims=True)
-        rows = dot((first | second).astype(F32).astype(BF16), cot[...])
-        out[...] = (weight * rows).astype(BF16)
+        chosen = (first | second).astype(F32).astype(BF16)
+        out[pl.ds(0, each), :] = dot(chosen, tok[...]).astype(BF16)
+        out[pl.ds(each, each), :] = (weight * dot(chosen, cot[...])).astype(BF16)
+
+
+def halve_kernel(both, *outs):
+    put_rows(both[...], outs)
 
 
 def cut_kernel(axis, chunk, n_groups, weight, out):
@@ -178,15 +176,22 @@
 def out_kernel(sizes, keys, part, own_hidden, other_hidden, own, *refs):
     pieces, (weight, *outs) = list(zip(keys, refs[: len(keys)])), refs[len(keys) :]
     fill_down(sizes, part, own, pieces, weight)
+    last_out_kernel(own_hidden, other_hidden, weight, *outs)
+
+
+def last_out_kernel(own_hidden, other_hidden, weight, *outs):
     half = own_hidden.shape[1]
     mine, theirs = halves(half)
     value = dot(own_hidden[...], weight[rows_at(mine, half), :]) + dot(other_hidden[...], weight[rows_at(theirs, half), :])
     put_rows(value, outs)
 
 
-def cot_kernel(n_groups, cots, *refs):
-    weights, keep, send = refs[:COL_CHUNKS], refs[COL_CHUNKS], refs[COL_CHUNKS + 1 :]
-    half = keep.shape[1]
+def cot_kernel(sizes, keys, cots, own, *refs):
+    pieces, refs = list(zip(keys, refs[: len(keys)])), refs[len(keys) :]
+    weights, (made, keep), send = refs[: COL_CHUNKS - 1], refs[COL_CHUNKS - 1 : COL_CHUNKS + 1], refs[COL_CHUNKS + 1 :]
+    fill_down(sizes, COL_CHUNKS - 1, own, pieces, made)
+    weights = [*weights, made]
+    half, n_groups = keep.shape[1], sizes[1]
     share = cots.shape[1] // n_groups
     width = share // COL_CHUNKS
     mine, theirs = halves(half)
@@ -269,7 +274,7 @@
     blocks = experts if shifted else 1
     each = rows // blocks
     routing = (experts, cap, shifted)
-    order = [s for s in range(1, experts) if s != experts // 2] + [experts // 2]
+    order = sorted(range(1, experts), key=lambda s: min(s, experts - s))
 
     def travel(part, sign, s):
         if shifted:
@@ -284,7 +289,10 @@
     feats = n_dp * gate_t.shape[1]
     plan = [(gate_t, 0, c) for c in range(ROW_CHUNKS)] + [(up_t, 0, c) for c in range(ROW_CHUNKS)]
     plan += [(down, 1, c) for c in range(COL_CHUNKS)]
-    x, y, cuts = {}, {}, []
+    x, y, cuts, turned = {}, {}, [], {}
+
+    def last_y(i):
+        return y[i][-1][1]
 
     def cut(i, *held):
         weight, axis, chunk = plan[i]
@@ -302,51 +310,47 @@
         y[i] = []
         for step, here in enumerate(x[i], 1):
             on = call(join_kernel, made_shape(here), (here,), held)
+            turned[i] = on
             for turn in range(n_groups):
                 y[i].append(((plan[i][2], step, turn), shift(on, "groups", turn) if turn else here))
 
     cut(0)
     cut(1)
 
-    def send(kernel, args, picked, *held):
+    def send(picked, *held):
         made = call(
-            functools.partial(kernel, *routing, picked),
-            [shape(each, half, BF16)] * len(picked),
-            args,
+            functools.partial(rows_kernel, *routing, picked),
+            [shape(2 * each, half, BF16)] * len(picked),
+            (ids_t, probs_t, tokens, cotangent),
             held,
         )
-        return [travel(part, 1, s) for part, s in zip(made, picked)]
-
-    send_tok = functools.partial(send, token_rows_kernel, (ids_t, tokens))
-    send_cot = functools.partial(send, cot_rows_kernel, (ids_t, probs_t, cotangent))
-    last = [()] * len(plan)
-    cot_parts = []
+        return [travel(part, 1, s) if shifted else part for part, s in zip(made, picked)]
+
+    def halved(both):
+        return call(halve_kernel, [shape(each, half, BF16)] * 2, (both,))
+
+    blocks_in = {}
+    for i in range(len(plan)):
+        turn = i // 2
+        if shifted and i % 2 == 0 and turn < len(order):
+            s = order[turn]
+            if turn:
+                (blocks_in[s],) = send((s,), blocks_in[order[turn - 1]], turned[i - 2])
+            else:
+                blocks_in[0], blocks_in[s] = send((0, s), cuts[0])
+        turn_over(i, *([last_y(i - 2)] if i > 1 else []))
+        if i + 2 < len(plan):
+            cut(i + 2, x[i][-1], *([last_y(i - 1)] if i else []))
+    for turn in range(len(plan) // 2, len(order) if shifted else 0):
+        (blocks_in[order[turn]],) = send((order[turn],), blocks_in[order[turn - 1]])
     if shifted:
-        tok, cot, now = {}, {}, ()
-        for i, (made, blocks_in, name) in enumerate([(tok, send_tok, s) for s in order] + [(cot, send_cot, s) for s in order]):
-            picked = (name,) if name != order[0] else (0, name)
-            waits = [*now, x[i - 1][-1]] if 0 < i <= len(plan) else list(now)
-            if i:
-                turn_over(i - 1, *(y[i - 3][-1][1:] if i >= 3 else ()), *last[i - 1])
-                if i + 1 < len(plan):
-                    cut(i + 1, x[i - 1][-1], *(y[i - 2][-1][1:] if i >= 2 else ()))
-            made.update(zip(picked, blocks_in(picked, *waits, *(cuts[:1] if i == 0 else ()))))
-            now = (made[name],)
-            if i + 1 < len(plan):
-                last[i + 1] = now
-        turn_over(5, y[3][-1][1], *now)
-        cot_parts = [cot[s] for s in range(blocks)]
-        tok_parts = [tok[s] for s in range(blocks)]
+        tok_parts, cot_parts = zip(*[halved(blocks_in[s]) for s in range(blocks)])
     else:
-        for i in range(len(plan)):
-            if i > 1:
-                cut(i, x[i - 2][-1])
-            turn_over(i)
-        cot_parts = send_cot((0,))
-        tok_parts = send_tok((0,))
+        tok_part, cot_part = halved(send((0,))[0])
+        tok_parts, cot_parts = [travel(tok_part, 1, 0)], [travel(cot_part, 1, 0)]
     tok_all, other_tok = joined(tok_parts), joined(swapped(tok_parts))
 
-    def front(own, picked, gate, *held):
+    def front(own, picked, gate):
         final = gate is not None
         keys, pieces = zip(*[kp for i in picked for kp in y[i]])
         act = shape(rows, wide, F32)
@@ -354,7 +358,6 @@
             functools.partial(front_kernel, sizes, keys, final),
             [shape(wide, feats, BF16), act] + ([shape(rows // SWAPS, wide, BF16)] * SWAPS if final else []),
             (tok_all, other_tok, own, *pieces, *([gate] if final else [])),
-            held,
         )
 
     first_pieces = range(ROW_CHUNKS)
@@ -364,51 +367,55 @@
     cot_all = joined(cot_parts)
 
     width = half // n_groups // COL_CHUNKS
-    down_weights, layers, sent, prob_part = [], [], [], 0.0
-    made = ()
-    for part in range(COL_CHUNKS):
+
+    def outputs(part):
         keys, pieces = zip(*y[2 * ROW_CHUNKS + part])
         weight, *made = call(
             functools.partial(out_kernel, sizes, keys, part),
             [shape(2 * wide, n_groups * width, BF16)] + [shape(each, n_groups * width, BF16)] * blocks,
             (hidden, other_hidden, down, *pieces),
-            made[:1],
         )
-        down_weights.append(weight)
-        back = list(made)
-        if shifted:
-            for lane in ([order[-1]], order[:-1]):
-                for i, s in enumerate(lane):
-                    held = back[lane[i - 1]] if i else sent[-1][lane[-1]] if sent else None
-                    out = back[s] if held is None else call(join_kernel, made_shape(back[s]), (back[s],), (held,))
-                    back[s] = travel(out, -1, s)
-        else:
-            back = [travel(back[0], -1, 0)]
-        sent.append(back)
-        layer, prob, both = call(
+        return weight, [travel(out, -1, s) for s, out in enumerate(made)]
+
+    def layer(part, back):
+        return call(
             functools.partial(layer_kernel, *routing, n_groups, part),
             [shape(count, n_groups * width, BF16), shape(expert_ids.shape[1], count, F32), shape(count, rows, BF16)],
             (ids_t, probs_t, cotangent, *back),
         )
-        layers.append(layer)
-        prob_part = prob_part + prob
-
-    kept, *crossing = call(
-        functools.partial(cot_kernel, n_groups),
-        [shape(rows, wide, F32)] + [shape(rows // SWAPS, wide, BF16)] * SWAPS,
-        (cot_all, *down_weights),
-        made[:1],
+
+    down_weights, sent = [None] * COL_CHUNKS, [None] * COL_CHUNKS
+    for part in range(COL_CHUNKS - 1):
+        down_weights[part], sent[part] = outputs(part)
+    early = [sent[0][s] for s in order] if shifted else []
+    weight, kept, *crossing = call(
+        functools.partial(cot_kernel, sizes, [key for key, _ in y[len(plan) - 1]]),
+        [shape(2 * wide, n_groups * width, BF16), shape(rows, wide, F32)] + [shape(rows // SWAPS, wide, BF16)] * SWAPS,
+        (cot_all, down, *[piece for _, piece in y[len(plan) - 1]], *down_weights[:-1]),
+        early[:2],
     )
+    down_weights[-1] = weight
+    last_made = call(
+        last_out_kernel,
+        [shape(each, n_groups * width, BF16)] * blocks,
+        (hidden, other_hidden, weight),
+        [kept, *early[2:]],
+    )
+    sent[-1] = [travel(out, -1, s) for s, out in enumerate(last_made)]
     received = joined(swapped(crossing))
     kept, *crossing = call(
         grad_kernel,
         [shape(rows, half, F32)] + [shape(rows // SWAPS, half, BF16)] * SWAPS,
         (gate, up, kept, received, gate_weight, up_weight),
-        layers[:1],
+        early,
     )
     received = joined(swapped(crossing))
     slots = call(add_kernel, [shape(each, half, BF16)] * blocks, (kept, received), [sent[-1][s] for s in order[::2] if shifted])
     grad_back = [travel(part, -1, s) for s, part in enumerate(slots)]
+    layers = [layer(part, back) for part, back in enumerate(sent)]
+    prob_part = sum(prob for _, prob, _ in layers)
+    both = layers[0][2]
+    layers = [out for out, _, _ in layers]
     grad_probs = (prob_part + shift(prob_part, "tensor", 1)).T
     grad_tokens, layer_out = call(
         functools.partial(token_kernel, n_groups),

time: 116 us -> 113 us (0.974)
  starting transfers between devices: 43.8 us -> 32.5 us
  waiting for transfers between devices: 53.3 us -> 61.8 us
    ppermute x44 -> x41, starting transfers between devices: 43.8 us -> 32.5 us  [shift(): lax.ppermute(value, axis, [(i, (i + step) % size) for i in range(size)])]
    ppermute x44 -> x41, waiting for transfers between devices: 53.3 us -> 61.8 us  [shift(): lax.ppermute(value, axis, [(i, (i + step) % size) for i in range(size)])]
    pallas_call x39 -> x36, Pallas kernels: 15.2 us -> 14.3 us  [call(): pl.pallas_call(body, out_shape=out_shape, in_specs=[VMEM] * given + [ANY]...]
    unnamed x16 -> x18, local copies, waits for them, and re-layouts: 1.57 us -> 2.34 us
  transfers between devices with their start and end apart: 44 -> 41, of which waited for: 16 -> 18; matrix products, arithmetic and copies ran while one was open for 0% -> 1% of each run, Pallas kernels for 12% -> 12%
where the time goes in v5:
time: 113 us; the launch traced here: 112 us
  waiting for transfers between devices  61.8 us (55%)
  starting transfers between devices  32.5 us (29%)
  Pallas kernels  14.3 us (13%)
  local copies, waits for them, and re-layouts  2.34 us (2%)
    ppermute x41, waiting for transfers between devices, shift(): lax.ppermute(value, axis, [(i, (i + step) % size) for i in range(size)])  61.8 us
    ppermute x41, starting transfers between devices, shift(): lax.ppermute(value, axis, [(i, (i + step) % size) for i in range(size)])  32.5 us
    pallas_call x36, Pallas kernels, call(): pl.pallas_call(body, out_shape=out_shape, in_specs=[VMEM] * given + [ANY]...  14.3 us
    unnamed x18, local copies, waits for them, and re-layouts  2.34 us
  transfers between devices with their start and end apart: 41, of which 18 were waited for; matrix products, arithmetic and copies ran while one was open for 1% of the time, Pallas kernels for 12%

profile of v5, /device:TPU:0, one launch (start us, length us, event | category | flops | bytes accessed | tf_op | source)
XLA Modules:
  0.0 112.4 jit_solution(5560187753456303506)
XLA Ops:
  0.7 1.4 %copy-done.1 = bf16[1,1024,704]{1,2,0:T(8,128)(2,1)S(1)} copy-done((bf16[1,1024,704]{1,2,0:T(8,128)(2,1)S(1)}, bf16[1,1024,704]{1,2,0:T(8,128)(2,1)}, u32[]{:S(2)}) %copy-start.1) | copy-done | bytes 1441816
  2.0 3.0 %collective-permute-start.1 = (bf16[176,1024]{1,0:T(8,128)(2,1)S(1)}, bf16[176,1024]{1,0:T(8,128)(2,1)S(1)}, u32[]{:S(2)}, u32[]{:S(2)}) collective-permute-start(bf16[176,1024]{1,0:T(8,128)(2,1)S(1)} %shard_map.94.refs_4_.refs_1_), channel_id=1, source_target_pairs={{0,2},{2,0},{1,3},{3,1},{4,6},{6,4},{5,7},{7,5},{8,10},{10,8},{9,1... | collective-permute-start | bytes 1081352 | tf_op jit(solution)/shard_map/ppermute | solution.py:254
  6.7 1.6 %collective-permute-start = (bf16[192,1024]{1,0:T(8,128)(2,1)S(1)}, bf16[192,1024]{1,0:T(8,128)(2,1)S(1)}, u32[]{:S(2)}, u32[]{:S(2)}) collective-permute-start(bf16[192,1024]{1,0:T(8,128)(2,1)S(1)} %get-tuple-element.54), channel_id=1, source_target_pairs={{0,4},{4,8},{8,12},{12,0},{1,5},{5,9},{9,13},{13,1},{2,6},{6,10},{... | collective-permute-start | bytes 1179656 | tf_op jit(solution)/shard_map/ppermute | solution.py:254
  9.2 5.0 %collective-permute-done.1.refs_0_.refs_1_.refs_3_ = bf16[176,1024]{1,0:T(8,128)(2,1)S(1)} collective-permute-done((bf16[176,1024]{1,0:T(8,128)(2,1)S(1)}, bf16[176,1024]{1,0:T(8,128)(2,1)S(1)}, u32[]{:S(2)}, u32[]{:S(2)}) %collective-permute-start.1) | collective-permute-done | bytes 360480 | tf_op jit(solution)/shard_map/ppermute | solution.py:254
  14.3 2.2 %collective-permute-start.4 = (bf16[176,1024]{1,0:T(8,128)(2,1)S(1)}, bf16[176,1024]{1,0:T(8,128)(2,1)S(1)}, u32[]{:S(2)}, u32[]{:S(2)}) collective-permute-start(bf16[176,1024]{1,0:T(8,128)(2,1)S(1)} %shard_map.98.refs_5_), channel_id=1, source_target_pairs={{0,16},{16,0},{1,17},{17,1},{2,18},{18,2},{3,19},{19,3},{4,20},{20... | collective-permute-start | bytes 1081352 | tf_op jit(solution)/shard_map/ppermute | solution.py:254
  16.5 2.7 %collective-permute-done.refs_0_.refs_4_ = bf16[192,1024]{1,0:T(8,128)(2,1)S(1)} collective-permute-done((bf16[192,1024]{1,0:T(8,128)(2,1)S(1)}, bf16[192,1024]{1,0:T(8,128)(2,1)S(1)}, u32[]{:S(2)}, u32[]{:S(2)}) %collective-permute-start) | collective-permute-done | bytes 393248 | tf_op jit(solution)/shard_map/ppermute | solution.py:254
  19.5 1.8 %collective-permute-start.2 = (bf16[192,1024]{1,0:T(8,128)(2,1)S(1)}, bf16[192,1024]{1,0:T(8,128)(2,1)S(1)}, u32[]{:S(2)}, u32[]{:S(2)}) collective-permute-start(bf16[192,1024]{1,0:T(8,128)(2,1)S(1)} %shard_map.99), channel_id=1, source_target_pairs={{0,12},{4,0},{8,4},{12,8},{1,13},{5,1},{9,5},{13,9},{2,14},{6,2},{... | collective-permute-start | bytes 1179656 | tf_op jit(solution)/shard_map/ppermute | solution.py:254
  21.4 1.2 %collective-permute-start.3 = (bf16[176,1024]{1,0:T(8,128)(2,1)S(1)}, bf16[176,1024]{1,0:T(8,128)(2,1)S(1)}, u32[]{:S(2)}, u32[]{:S(2)}) collective-permute-start(bf16[176,1024]{1,0:T(8,128)(2,1)S(1)} %shard_map.101.refs_3_), channel_id=1, source_target_pairs={{0,2},{2,0},{1,3},{3,1},{4,6},{6,4},{5,7},{7,5},{8,10},{10,8},{9,1... | collective-permute-start | bytes 1081352 | tf_op jit(solution)/shard_map/ppermute | solution.py:254
  22.6 1.6 %collective-permute-start.13 = (bf16[176,1024]{1,0:T(8,128)(2,1)S(1)}, bf16[176,1024]{1,0:T(8,128)(2,1)S(1)}, u32[]{:S(2)}, u32[]{:S(2)}) collective-permute-start(bf16[176,1024]{1,0:T(8,128)(2,1)S(1)} %shard_map.109), channel_id=1, source_target_pairs={{0,16},{16,0},{1,17},{17,1},{2,18},{18,2},{3,19},{19,3},{4,20},{20... | collective-permute-start | bytes 1081352 | tf_op jit(solution)/shard_map/ppermute | solution.py:254
  25.2 7.6 %collective-permute-done.3.refs_0_.refs_3_.refs_1_ = bf16[176,1024]{1,0:T(8,128)(2,1)S(1)} collective-permute-done((bf16[176,1024]{1,0:T(8,128)(2,1)S(1)}, bf16[176,1024]{1,0:T(8,128)(2,1)S(1)}, u32[]{:S(2)}, u32[]{:S(2)}) %collective-permute-start.3) | collective-permute-done | bytes 360480 | tf_op jit(solution)/shard_map/ppermute | solution.py:254
  32.8 1.6 %collective-permute-start.10 = (bf16[176,1024]{1,0:T(8,128)(2,1)S(1)}, bf16[176,1024]{1,0:T(8,128)(2,1)S(1)}, u32[]{:S(2)}, u32[]{:S(2)}) collective-permute-start(bf16[176,1024]{1,0:T(8,128)(2,1)S(1)} %shard_map.102.refs_5_), channel_id=1, source_target_pairs={{0,16},{16,0},{1,17},{17,1},{2,18},{18,2},{3,19},{19,3},{4,20},{20... | collective-permute-start | bytes 1081352 | tf_op jit(solution)/shard_map/ppermute | solution.py:254
  35.0 1.6 %collective-permute-start.19 = (bf16[704,256]{1,0:T(8,128)(2,1)S(1)}, bf16[704,256]{1,0:T(8,128)(2,1)S(1)}, u32[]{:S(2)}, u32[]{:S(2)}) collective-permute-start(bf16[704,256]{1,0:T(8,128)(2,1)S(1)} %shard_map.115.refs_3_), channel_id=1, source_target_pairs={{0,2},{2,0},{1,3},{3,1},{4,6},{6,4},{5,7},{7,5},{8,10},{10,8},{9,1... | collective-permute-start | bytes 1081352 | tf_op jit(solution)/shard_map/ppermute | solution.py:254
  36.7 3.8 %collective-permute-done.12.refs_0_.refs_5_.refs_1_ = bf16[176,1024]{1,0:T(8,128)(2,1)S(1)} collective-permute-done((bf16[176,1024]{1,0:T(8,128)(2,1)S(1)}, bf16[176,1024]{1,0:T(8,128)(2,1)S(1)}, u32[]{:S(2)}, u32[]{:S(2)}) %collective-permute-start.12) | collective-permute-done | bytes 360480 | tf_op jit(solution)/shard_map/ppermute | solution.py:254
  40.5 1.6 %collective-permute-start.14 = (bf16[176,1024]{1,0:T(8,128)(2,1)S(1)}, bf16[176,1024]{1,0:T(8,128)(2,1)S(1)}, u32[]{:S(2)}, u32[]{:S(2)}) collective-permute-start(bf16[176,1024]{1,0:T(8,128)(2,1)S(1)} %shard_map.110), channel_id=1, source_target_pairs={{0,16},{16,0},{1,17},{17,1},{2,18},{18,2},{3,19},{19,3},{4,20},{20... | collective-permute-start | bytes 1081352 | tf_op jit(solution)/shard_map/ppermute | solution.py:254
  42.2 1.2 %collective-permute-start.24 = (bf16[704,256]{1,0:T(8,128)(2,1)S(1)}, bf16[704,256]{1,0:T(8,128)(2,1)S(1)}, u32[]{:S(2)}, u32[]{:S(2)}) collective-permute-start(bf16[704,256]{1,0:T(8,128)(2,1)S(1)} %shard_map.120), channel_id=1, source_target_pairs={{0,2},{2,0},{1,3},{3,1},{4,6},{6,4},{5,7},{7,5},{8,10},{10,8},{9,1... | collective-permute-start | bytes 1081352 | tf_op jit(solution)/shard_map/ppermute | solution.py:254
  43.4 6.8 %collective-permute-done.5.refs_0_ = bf16[192,1024]{1,0:T(8,128)(2,1)S(1)} collective-permute-done((bf16[192,1024]{1,0:T(8,128)(2,1)S(1)}, bf16[192,1024]{1,0:T(8,128)(2,1)S(1)}, u32[]{:S(2)}, u32[]{:S(2)}) %collective-permute-start.5) | collective-permute-done | bytes 393248 | tf_op jit(solution)/shard_map/ppermute | solution.py:254
  52.4 1.6 %shard_map.111 = (bf16[768,2048]{1,0:T(8,128)(2,1)S(1)}, f32[384,768]{1,0:T(8,128)S(1)}) custom-call(bf16[384,1024]{1,0:T(8,128)(2,1)S(1)} %shard_map.106.refs_0_, bf16[384,1024]{1,0:T(8,128)(2,1)S(1)} %shard_map.107.refs_1_, bf16[704,1024]{1,0:T(8,128)(2,1)S(1)} %bitcast.17, bf16[176,1024]{1,0:T(8,128)(2,1)S(1)} %collective-permute-done.1.refs_0_.refs_1_.refs_3_, ...), custom_call_target="tpu_custom_call" | custom-call | flops 1 | bytes 1 | tf_op jit(solution)/shard_map/pallas_call | solution.py:33
  54.0 1.6 %shard_map.112 = (bf16[768,2048]{1,0:T(8,128)(2,1)S(1)}, f32[384,768]{1,0:T(8,128)S(1)}, bf16[96,768]{1,0:T(8,128)(2,1)S(1)}, bf16[96,768]{1,0:T(8,128)(2,1)S(1)...) custom-call(bf16[384,1024]{1,0:T(8,128)(2,1)S(1)} %shard_map.106.refs_0_, ...), custom_call_target="tpu_custom_call" | custom-call | flops 1 | bytes 1 | tf_op jit(solution)/shard_map/pallas_call | solution.py:33
  56.0 1.3 %collective-permute-start.25 = (bf16[704,256]{1,0:T(8,128)(2,1)S(1)}, bf16[704,256]{1,0:T(8,128)(2,1)S(1)}, u32[]{:S(2)}, u32[]{:S(2)}) collective-permute-start(bf16[704,256]{1,0:T(8,128)(2,1)S(1)} %shard_map.121), channel_id=1, source_target_pairs={{0,16},{16,0},{1,17},{17,1},{2,18},{18,2},{3,19},{19,3},{4,20},{20... | collective-permute-start | bytes 1081352 | tf_op jit(solution)/shard_map/ppermute | solution.py:254
  59.2 3.7 %collective-permute-done.20.refs_4_ = bf16[704,256]{1,0:T(8,128)(2,1)S(1)} collective-permute-done((bf16[704,256]{1,0:T(8,128)(2,1)S(1)}, bf16[704,256]{1,0:T(8,128)(2,1)S(1)}, u32[]{:S(2)}, u32[]{:S(2)}) %collective-permute-start.20) | collective-permute-done | bytes 360480 | tf_op jit(solution)/shard_map/ppermute | solution.py:254
  63.8 3.6 %collective-permute-start.21 = (bf16[96,512]{1,0:T(8,128)(2,1)S(1)}, bf16[96,512]{1,0:T(8,128)(2,1)S(1)}, u32[]{:S(2)}, u32[]{:S(2)}) collective-permute-start(bf16[96,512]{1,0:T(8,128)(2,1)S(1)} %get-tuple-element.64), channel_id=1, source_target_pairs={{0,12},{4,0},{8,4},{12,8},{1,13},{5,1},{9,5},{13,9},{2,14},{6,2},{... | collective-permute-start | bytes 294920 | tf_op jit(solution)/shard_map/ppermute | solution.py:254
  68.1 2.2 %collective-permute-done.21.refs_4_.refs_5_.refs_6_ = bf16[96,512]{1,0:T(8,128)(2,1)S(1)} collective-permute-done((bf16[96,512]{1,0:T(8,128)(2,1)S(1)}, bf16[96,512]{1,0:T(8,128)(2,1)S(1)}, u32[]{:S(2)}, u32[]{:S(2)}) %collective-permute-start.21) | collective-permute-done | bytes 98336 | tf_op jit(solution)/shard_map/ppermute | solution.py:254
  70.3 3.7 %collective-permute-done.23.refs_6_.refs_7_ = bf16[96,512]{1,0:T(8,128)(2,1)S(1)} collective-permute-done((bf16[96,512]{1,0:T(8,128)(2,1)S(1)}, bf16[96,512]{1,0:T(8,128)(2,1)S(1)}, u32[]{:S(2)}, u32[]{:S(2)}) %collective-permute-start.23) | collective-permute-done | bytes 98336 | tf_op jit(solution)/shard_map/ppermute | solution.py:254
  73.9 1.5 %shard_map.122 = (bf16[1536,512]{1,0:T(8,128)(2,1)S(1)}, f32[384,768]{1,0:T(8,128)S(1)}, bf16[96,768]{1,0:T(8,128)(2,1)S(1)}, bf16[96,768]{1,0:T(8,128)(2,1)S(1)...) custom-call(bf16[384,1024]{1,0:T(8,128)(2,1)S(1)} %shard_map.119.refs_0_, bf16[704,1024]{1,0:T(8,128)(2,1)S(1)} %bitcast.14, ...), custom_call_target="tpu_custom_call" | custom-call | flops 1 | bytes 1 | tf_op jit(solution)/shard_map/pallas_call | solution.py:33
  77.3 1.3 %collective-permute-start.34 = (bf16[96,512]{1,0:T(8,128)(2,1)S(1)}, bf16[96,512]{1,0:T(8,128)(2,1)S(1)}, u32[]{:S(2)}, u32[]{:S(2)}) collective-permute-start(bf16[96,512]{1,0:T(8,128)(2,1)S(1)} %get-tuple-element.87), channel_id=1, source_target_pairs={{0,12},{4,0},{8,4},{12,8},{1,13},{5,1},{9,5},{13,9},{2,14},{6,2},{... | collective-permute-start | bytes 294920 | tf_op jit(solution)/shard_map/ppermute | solution.py:254
  78.7 2.7 %shard_map.124 = (f32[384,1024]{1,0:T(8,128)S(1)}, bf16[96,1024]{1,0:T(8,128)(2,1)S(1)}, bf16[96,1024]{1,0:T(8,128)(2,1)S(1)}, bf16[96,1024]{1,0:T(8,128)(2,1)S(1)}, bf16[96,1024]{1,0:T(8,128)(2,1)S(1)}) custom-call(f32[384,768]{1,0:T(8,128)S(1)} %get-tuple-element.58.refs_7_.refs_0_, f32[384,768]{1,0:T(8,128)S(1)} %get-tuple-element.68.refs_1_, ...), custom_call_target="tpu_custom_call" | custom-call | flops 1 | bytes 1 | tf_op jit(solution)/shard_map/pallas_call | solution.py:33
  82.9 2.8 %collective-permute-done.35.refs_3_.refs_5_ = bf16[96,512]{1,0:T(8,128)(2,1)S(1)} collective-permute-done((bf16[96,512]{1,0:T(8,128)(2,1)S(1)}, bf16[96,512]{1,0:T(8,128)(2,1)S(1)}, u32[]{:S(2)}, u32[]{:S(2)}) %collective-permute-start.35) | collective-permute-done | bytes 98336 | tf_op jit(solution)/shard_map/ppermute | solution.py:254
  86.5 5.5 %collective-permute-done.39.refs_6_ = bf16[96,512]{1,0:T(8,128)(2,1)S(1)} collective-permute-done((bf16[96,512]{1,0:T(8,128)(2,1)S(1)}, bf16[96,512]{1,0:T(8,128)(2,1)S(1)}, u32[]{:S(2)}, u32[]{:S(2)}) %collective-permute-start.39) | collective-permute-done | bytes 98336 | tf_op jit(solution)/shard_map/ppermute | solution.py:254
  92.0 1.2 %shard_map.128 = (bf16[128,512]{1,0:T(8,128)(2,1)S(1)}, f32[2,128]{1,0:T(2,128)S(1)}, bf16[128,384]{1,0:T(8,128)(2,1)}) custom-call(s32[2,128]{1,0:T(2,128)S(1)} %bitcast.25, f32[2,128]{1,0:T(2,128)S(1)} %bitcast.30, bf16[128,1024]{1,0:T(8,128)(2,1)S(1)} %copy-done.4, bf16[96,512]{1,0:T(8,128)(2,1)S(1)} %get-tuple-element.94.refs_3_, ...), custom_call_target="tpu_custom_call" | custom-call | flops 1 | bytes 1 | tf_op jit(solution)/shard_map/pallas_call | solution.py:33
  93.5 1.3 %collective-permute-start.36 = (bf16[96,1024]{1,0:T(8,128)(2,1)S(1)}, bf16[96,1024]{1,0:T(8,128)(2,1)S(1)}, u32[]{:S(2)}, u32[]{:S(2)}) collective-permute-start(bf16[96,1024]{1,0:T(8,128)(2,1)S(1)} %get-tuple-element.90), channel_id=1, source_target_pairs={{0,12},{4,0},{8,4},{12,8},{1,13},{5,1},{9,5},{13,9},{2,14},{6,2},{... | collective-permute-start | bytes 589832 | tf_op jit(solution)/shard_map/ppermute | solution.py:254
  96.1 6.4 %collective-permute-done.36.refs_2_ = bf16[96,1024]{1,0:T(8,128)(2,1)S(1)} collective-permute-done((bf16[96,1024]{1,0:T(8,128)(2,1)S(1)}, bf16[96,1024]{1,0:T(8,128)(2,1)S(1)}, u32[]{:S(2)}, u32[]{:S(2)}) %collective-permute-start.36) | collective-permute-done | bytes 196640 | tf_op jit(solution)/shard_map/ppermute | solution.py:254
  102.5 8.9 %collective-permute-done.37.refs_3_ = bf16[96,1024]{1,0:T(8,128)(2,1)S(1)} collective-permute-done((bf16[96,1024]{1,0:T(8,128)(2,1)S(1)}, bf16[96,1024]{1,0:T(8,128)(2,1)S(1)}, u32[]{:S(2)}, u32[]{:S(2)}) %collective-permute-start.37) | collective-permute-done | bytes 196640 | tf_op jit(solution)/shard_map/ppermute | solution.py:254
  (106 shorter events, 17.8 us)
Async XLA Ops:
  2.0 12.2 %collective-permute-start.1 = (bf16[176,1024]{1,0:T(8,128)(2,1)S(1)}, bf16[176,1024]{1,0:T(8,128)(2,1)S(1)}, u32[]{:S(2)}, u32[]{:S(2)}) collective-permute-start(bf16[176,1024]{1,0:T(8,128)(2,1)S(1)} %shard_map.94.refs_4_.refs_1_), channel_id=1, source_target_pairs={{0,2},{2,0},{1,3},{3,1},{4,6},{6,4},{5,7},{7,5},{8,10},{10,8},{9,1... | collective-permute-start | bytes 1081352 | tf_op jit(solution)/shard_map/ppermute | solution.py:254
  6.7 12.5 %collective-permute-start = (bf16[192,1024]{1,0:T(8,128)(2,1)S(1)}, bf16[192,1024]{1,0:T(8,128)(2,1)S(1)}, u32[]{:S(2)}, u32[]{:S(2)}) collective-permute-start(bf16[192,1024]{1,0:T(8,128)(2,1)S(1)} %get-tuple-element.54), channel_id=1, source_target_pairs={{0,4},{4,8},{8,12},{12,0},{1,5},{5,9},{9,13},{13,1},{2,6},{6,10},{... | collective-permute-start | bytes 1179656 | tf_op jit(solution)/shard_map/ppermute | solution.py:254
  8.3 14.2 %collective-permute-start.11 = (bf16[176,1024]{1,0:T(8,128)(2,1)S(1)}, bf16[176,1024]{1,0:T(8,128)(2,1)S(1)}, u32[]{:S(2)}, u32[]{:S(2)}) collective-permute-start(bf16[176,1024]{1,0:T(8,128)(2,1)S(1)} %shard_map.100.refs_2_), channel_id=1, source_target_pairs={{0,2},{2,0},{1,3},{3,1},{4,6},{6,4},{5,7},{7,5},{8,10},{10,8},{9,1... | collective-permute-start | bytes 1081352 | tf_op jit(solution)/shard_map/ppermute | solution.py:254
  14.3 9.9 %collective-permute-start.4 = (bf16[176,1024]{1,0:T(8,128)(2,1)S(1)}, bf16[176,1024]{1,0:T(8,128)(2,1)S(1)}, u32[]{:S(2)}, u32[]{:S(2)}) collective-permute-start(bf16[176,1024]{1,0:T(8,128)(2,1)S(1)} %shard_map.98.refs_5_), channel_id=1, source_target_pairs={{0,16},{16,0},{1,17},{17,1},{2,18},{18,2},{3,19},{19,3},{4,20},{20... | collective-permute-start | bytes 1081352 | tf_op jit(solution)/shard_map/ppermute | solution.py:254
  19.5 14.9 %collective-permute-start.2 = (bf16[192,1024]{1,0:T(8,128)(2,1)S(1)}, bf16[192,1024]{1,0:T(8,128)(2,1)S(1)}, u32[]{:S(2)}, u32[]{:S(2)}) collective-permute-start(bf16[192,1024]{1,0:T(8,128)(2,1)S(1)} %shard_map.99), channel_id=1, source_target_pairs={{0,12},{4,0},{8,4},{12,8},{1,13},{5,1},{9,5},{13,9},{2,14},{6,2},{... | collective-permute-start | bytes 1179656 | tf_op jit(solution)/shard_map/ppermute | solution.py:254
  21.4 11.4 %collective-permute-start.3 = (bf16[176,1024]{1,0:T(8,128)(2,1)S(1)}, bf16[176,1024]{1,0:T(8,128)(2,1)S(1)}, u32[]{:S(2)}, u32[]{:S(2)}) collective-permute-start(bf16[176,1024]{1,0:T(8,128)(2,1)S(1)} %shard_map.101.refs_3_), channel_id=1, source_target_pairs={{0,2},{2,0},{1,3},{3,1},{4,6},{6,4},{5,7},{7,5},{8,10},{10,8},{9,1... | collective-permute-start | bytes 1081352 | tf_op jit(solution)/shard_map/ppermute | solution.py:254
  22.6 12.4 %collective-permute-start.13 = (bf16[176,1024]{1,0:T(8,128)(2,1)S(1)}, bf16[176,1024]{1,0:T(8,128)(2,1)S(1)}, u32[]{:S(2)}, u32[]{:S(2)}) collective-permute-start(bf16[176,1024]{1,0:T(8,128)(2,1)S(1)} %shard_map.109), channel_id=1, source_target_pairs={{0,16},{16,0},{1,17},{17,1},{2,18},{18,2},{3,19},{19,3},{4,20},{20... | collective-permute-start | bytes 1081352 | tf_op jit(solution)/shard_map/ppermute | solution.py:254
  24.2 16.3 %collective-permute-start.12 = (bf16[176,1024]{1,0:T(8,128)(2,1)S(1)}, bf16[176,1024]{1,0:T(8,128)(2,1)S(1)}, u32[]{:S(2)}, u32[]{:S(2)}) collective-permute-start(bf16[176,1024]{1,0:T(8,128)(2,1)S(1)} %shard_map.108.refs_3_), channel_id=1, source_target_pairs={{0,2},{2,0},{1,3},{3,1},{4,6},{6,4},{5,7},{7,5},{8,10},{10,8},{9,1... | collective-permute-start | bytes 1081352 | tf_op jit(solution)/shard_map/ppermute | solution.py:254
  32.8 9.3 %collective-permute-start.10 = (bf16[176,1024]{1,0:T(8,128)(2,1)S(1)}, bf16[176,1024]{1,0:T(8,128)(2,1)S(1)}, u32[]{:S(2)}, u32[]{:S(2)}) collective-permute-start(bf16[176,1024]{1,0:T(8,128)(2,1)S(1)} %shard_map.102.refs_5_), channel_id=1, source_target_pairs={{0,16},{16,0},{1,17},{17,1},{2,18},{18,2},{3,19},{19,3},{4,20},{20... | collective-permute-start | bytes 1081352 | tf_op jit(solution)/shard_map/ppermute | solution.py:254
  34.8 15.4 %collective-permute-start.5 = (bf16[192,1024]{1,0:T(8,128)(2,1)S(1)}, bf16[192,1024]{1,0:T(8,128)(2,1)S(1)}, u32[]{:S(2)}, u32[]{:S(2)}) collective-permute-start(bf16[192,1024]{1,0:T(8,128)(2,1)S(1)} %shard_map.103), channel_id=1, source_target_pairs={{0,8},{4,12},{8,0},{12,4},{1,9},{5,13},{9,1},{13,5},{2,10},{6,14},... | collective-permute-start | bytes 1179656 | tf_op jit(solution)/shard_map/ppermute | solution.py:254
  35.0 15.8 %collective-permute-start.19 = (bf16[704,256]{1,0:T(8,128)(2,1)S(1)}, bf16[704,256]{1,0:T(8,128)(2,1)S(1)}, u32[]{:S(2)}, u32[]{:S(2)}) collective-permute-start(bf16[704,256]{1,0:T(8,128)(2,1)S(1)} %shard_map.115.refs_3_), channel_id=1, source_target_pairs={{0,2},{2,0},{1,3},{3,1},{4,6},{6,4},{5,7},{7,5},{8,10},{10,8},{9,1... | collective-permute-start | bytes 1081352 | tf_op jit(solution)/shard_map/ppermute | solution.py:254
  36.6 13.7 %collective-permute-start.6 = (bf16[96,1024]{1,0:T(8,128)(2,1)S(1)}, bf16[96,1024]{1,0:T(8,128)(2,1)S(1)}, u32[]{:S(2)}, u32[]{:S(2)}) collective-permute-start(bf16[96,1024]{1,0:T(8,128)(2,1)S(1)} %get-tuple-element.53.refs_0_), channel_id=1, source_target_pairs={{0,1},{1,0},{2,3},{3,2},{4,5},{5,4},{6,7},{7,6},{8,9},{9,8},{10,11... | collective-permute-start | bytes 589832 | tf_op jit(solution)/shard_map/ppermute | solution.py:254
  40.5 13.5 %collective-permute-start.14 = (bf16[176,1024]{1,0:T(8,128)(2,1)S(1)}, bf16[176,1024]{1,0:T(8,128)(2,1)S(1)}, u32[]{:S(2)}, u32[]{:S(2)}) collective-permute-start(bf16[176,1024]{1,0:T(8,128)(2,1)S(1)} %shard_map.110), channel_id=1, source_target_pairs={{0,16},{16,0},{1,17},{17,1},{2,18},{18,2},{3,19},{19,3},{4,20},{20... | collective-permute-start | bytes 1081352 | tf_op jit(solution)/shard_map/ppermute | solution.py:254
  42.2 13.8 %collective-permute-start.24 = (bf16[704,256]{1,0:T(8,128)(2,1)S(1)}, bf16[704,256]{1,0:T(8,128)(2,1)S(1)}, u32[]{:S(2)}, u32[]{:S(2)}) collective-permute-start(bf16[704,256]{1,0:T(8,128)(2,1)S(1)} %shard_map.120), channel_id=1, source_target_pairs={{0,2},{2,0},{1,3},{3,1},{4,6},{6,4},{5,7},{7,5},{8,10},{10,8},{9,1... | collective-permute-start | bytes 1081352 | tf_op jit(solution)/shard_map/ppermute | solution.py:254
  51.7 11.3 %collective-permute-start.20 = (bf16[704,256]{1,0:T(8,128)(2,1)S(1)}, bf16[704,256]{1,0:T(8,128)(2,1)S(1)}, u32[]{:S(2)}, u32[]{:S(2)}) collective-permute-start(bf16[704,256]{1,0:T(8,128)(2,1)S(1)} %shard_map.116), channel_id=1, source_target_pairs={{0,16},{16,0},{1,17},{17,1},{2,18},{18,2},{3,19},{19,3},{4,20},{20... | collective-permute-start | bytes 1081352 | tf_op jit(solution)/shard_map/ppermute | solution.py:254
  56.0 17.9 %collective-permute-start.25 = (bf16[704,256]{1,0:T(8,128)(2,1)S(1)}, bf16[704,256]{1,0:T(8,128)(2,1)S(1)}, u32[]{:S(2)}, u32[]{:S(2)}) collective-permute-start(bf16[704,256]{1,0:T(8,128)(2,1)S(1)} %shard_map.121), channel_id=1, source_target_pairs={{0,16},{16,0},{1,17},{17,1},{2,18},{18,2},{3,19},{19,3},{4,20},{20... | collective-permute-start | bytes 1081352 | tf_op jit(solution)/shard_map/ppermute | solution.py:254
  63.8 6.5 %collective-permute-start.21 = (bf16[96,512]{1,0:T(8,128)(2,1)S(1)}, bf16[96,512]{1,0:T(8,128)(2,1)S(1)}, u32[]{:S(2)}, u32[]{:S(2)}) collective-permute-start(bf16[96,512]{1,0:T(8,128)(2,1)S(1)} %get-tuple-element.64), channel_id=1, source_target_pairs={{0,12},{4,0},{8,4},{12,8},{1,13},{5,1},{9,5},{13,9},{2,14},{6,2},{... | collective-permute-start | bytes 294920 | tf_op jit(solution)/shard_map/ppermute | solution.py:254
  67.4 6.5 %collective-permute-start.23 = (bf16[96,512]{1,0:T(8,128)(2,1)S(1)}, bf16[96,512]{1,0:T(8,128)(2,1)S(1)}, u32[]{:S(2)}, u32[]{:S(2)}) collective-permute-start(bf16[96,512]{1,0:T(8,128)(2,1)S(1)} %get-tuple-element.66), channel_id=1, source_target_pairs={{0,4},{4,8},{8,12},{12,0},{1,5},{5,9},{9,13},{13,1},{2,6},{6,10},{... | collective-permute-start | bytes 294920 | tf_op jit(solution)/shard_map/ppermute | solution.py:254
  67.4 9.1 %collective-permute-start.22 = (bf16[96,512]{1,0:T(8,128)(2,1)S(1)}, bf16[96,512]{1,0:T(8,128)(2,1)S(1)}, u32[]{:S(2)}, u32[]{:S(2)}) collective-permute-start(bf16[96,512]{1,0:T(8,128)(2,1)S(1)} %get-tuple-element.65), channel_id=1, source_target_pairs={{0,8},{4,12},{8,0},{12,4},{1,9},{5,13},{9,1},{13,5},{2,10},{6,14},... | collective-permute-start | bytes 294920 | tf_op jit(solution)/shard_map/ppermute | solution.py:254
  75.4 3.1 %collective-permute-start.26 = (bf16[96,768]{1,0:T(8,128)(2,1)S(1)}, bf16[96,768]{1,0:T(8,128)(2,1)S(1)}, u32[]{:S(2)}, u32[]{:S(2)}) collective-permute-start(bf16[96,768]{1,0:T(8,128)(2,1)S(1)} %get-tuple-element.75), channel_id=1, source_target_pairs={{0,1},{1,0},{2,3},{3,2},{4,5},{5,4},{6,7},{7,6},{8,9},{9,8},{10,11... | collective-permute-start | bytes 442376 | tf_op jit(solution)/shard_map/ppermute | solution.py:254
  75.5 3.2 %collective-permute-start.27 = (bf16[96,768]{1,0:T(8,128)(2,1)S(1)}, bf16[96,768]{1,0:T(8,128)(2,1)S(1)}, u32[]{:S(2)}, u32[]{:S(2)}) collective-permute-start(bf16[96,768]{1,0:T(8,128)(2,1)S(1)} %get-tuple-element.76), channel_id=1, source_target_pairs={{0,1},{1,0},{2,3},{3,2},{4,5},{5,4},{6,7},{7,6},{8,9},{9,8},{10,11... | collective-permute-start | bytes 442376 | tf_op jit(solution)/shard_map/ppermute | solution.py:254
  76.0 2.7 %collective-permute-start.28 = (bf16[96,768]{1,0:T(8,128)(2,1)S(1)}, bf16[96,768]{1,0:T(8,128)(2,1)S(1)}, u32[]{:S(2)}, u32[]{:S(2)}) collective-permute-start(bf16[96,768]{1,0:T(8,128)(2,1)S(1)} %get-tuple-element.77), channel_id=1, source_target_pairs={{0,1},{1,0},{2,3},{3,2},{4,5},{5,4},{6,7},{7,6},{8,9},{9,8},{10,11... | collective-permute-start | bytes 442376 | tf_op jit(solution)/shard_map/ppermute | solution.py:254
  77.3 5.6 %collective-permute-start.34 = (bf16[96,512]{1,0:T(8,128)(2,1)S(1)}, bf16[96,512]{1,0:T(8,128)(2,1)S(1)}, u32[]{:S(2)}, u32[]{:S(2)}) collective-permute-start(bf16[96,512]{1,0:T(8,128)(2,1)S(1)} %get-tuple-element.87), channel_id=1, source_target_pairs={{0,12},{4,0},{8,4},{12,8},{1,13},{5,1},{9,5},{13,9},{2,14},{6,2},{... | collective-permute-start | bytes 294920 | tf_op jit(solution)/shard_map/ppermute | solution.py:254
  78.5 7.1 %collective-permute-start.35 = (bf16[96,512]{1,0:T(8,128)(2,1)S(1)}, bf16[96,512]{1,0:T(8,128)(2,1)S(1)}, u32[]{:S(2)}, u32[]{:S(2)}) collective-permute-start(bf16[96,512]{1,0:T(8,128)(2,1)S(1)} %get-tuple-element.88), channel_id=1, source_target_pairs={{0,8},{4,12},{8,0},{12,4},{1,9},{5,13},{9,1},{13,5},{2,10},{6,14},... | collective-permute-start | bytes 294920 | tf_op jit(solution)/shard_map/ppermute | solution.py:254
  81.4 11.9 %collective-permute-start.30 = (bf16[96,1024]{1,0:T(8,128)(2,1)S(1)}, bf16[96,1024]{1,0:T(8,128)(2,1)S(1)}, u32[]{:S(2)}, u32[]{:S(2)}) collective-permute-start(bf16[96,1024]{1,0:T(8,128)(2,1)S(1)} %get-tuple-element.82), channel_id=1, source_target_pairs={{0,1},{1,0},{2,3},{3,2},{4,5},{5,4},{6,7},{7,6},{8,9},{9,8},{10,11... | collective-permute-start | bytes 589832 | tf_op jit(solution)/shard_map/ppermute | solution.py:254
  81.5 11.8 %collective-permute-start.31 = (bf16[96,1024]{1,0:T(8,128)(2,1)S(1)}, bf16[96,1024]{1,0:T(8,128)(2,1)S(1)}, u32[]{:S(2)}, u32[]{:S(2)}) collective-permute-start(bf16[96,1024]{1,0:T(8,128)(2,1)S(1)} %get-tuple-element.83), channel_id=1, source_target_pairs={{0,1},{1,0},{2,3},{3,2},{4,5},{5,4},{6,7},{7,6},{8,9},{9,8},{10,11... | collective-permute-start | bytes 589832 | tf_op jit(solution)/shard_map/ppermute | solution.py:254
  82.0 11.3 %collective-permute-start.32 = (bf16[96,1024]{1,0:T(8,128)(2,1)S(1)}, bf16[96,1024]{1,0:T(8,128)(2,1)S(1)}, u32[]{:S(2)}, u32[]{:S(2)}) collective-permute-start(bf16[96,1024]{1,0:T(8,128)(2,1)S(1)} %get-tuple-element.84), channel_id=1, source_target_pairs={{0,1},{1,0},{2,3},{3,2},{4,5},{5,4},{6,7},{7,6},{8,9},{9,8},{10,11... | collective-permute-start | bytes 589832 | tf_op jit(solution)/shard_map/ppermute | solution.py:254
  82.9 10.4 %collective-permute-start.33 = (bf16[96,1024]{1,0:T(8,128)(2,1)S(1)}, bf16[96,1024]{1,0:T(8,128)(2,1)S(1)}, u32[]{:S(2)}, u32[]{:S(2)}) collective-permute-start(bf16[96,1024]{1,0:T(8,128)(2,1)S(1)} %get-tuple-element.85), channel_id=1, source_target_pairs={{0,1},{1,0},{2,3},{3,2},{4,5},{5,4},{6,7},{7,6},{8,9},{9,8},{10,11... | collective-permute-start | bytes 589832 | tf_op jit(solution)/shard_map/ppermute | solution.py:254
  85.6 6.4 %collective-permute-start.39 = (bf16[96,512]{1,0:T(8,128)(2,1)S(1)}, bf16[96,512]{1,0:T(8,128)(2,1)S(1)}, u32[]{:S(2)}, u32[]{:S(2)}) collective-permute-start(bf16[96,512]{1,0:T(8,128)(2,1)S(1)} %get-tuple-element.95), channel_id=1, source_target_pairs={{0,4},{4,8},{8,12},{12,0},{1,5},{5,9},{9,13},{13,1},{2,6},{6,10},{... | collective-permute-start | bytes 294920 | tf_op jit(solution)/shard_map/ppermute | solution.py:254
  93.5 9.1 %collective-permute-start.36 = (bf16[96,1024]{1,0:T(8,128)(2,1)S(1)}, bf16[96,1024]{1,0:T(8,128)(2,1)S(1)}, u32[]{:S(2)}, u32[]{:S(2)}) collective-permute-start(bf16[96,1024]{1,0:T(8,128)(2,1)S(1)} %get-tuple-element.90), channel_id=1, source_target_pairs={{0,12},{4,0},{8,4},{12,8},{1,13},{5,1},{9,5},{13,9},{2,14},{6,2},{... | collective-permute-start | bytes 589832 | tf_op jit(solution)/shard_map/ppermute | solution.py:254
  94.8 16.6 %collective-permute-start.37 = (bf16[96,1024]{1,0:T(8,128)(2,1)S(1)}, bf16[96,1024]{1,0:T(8,128)(2,1)S(1)}, u32[]{:S(2)}, u32[]{:S(2)}) collective-permute-start(bf16[96,1024]{1,0:T(8,128)(2,1)S(1)} %get-tuple-element.91), channel_id=1, source_target_pairs={{0,8},{4,12},{8,0},{12,4},{1,9},{5,13},{9,1},{13,5},{2,10},{6,14},... | collective-permute-start | bytes 589832 | tf_op jit(solution)/shard_map/ppermute | solution.py:254
  94.8 16.6 %collective-permute-start.38 = (bf16[96,1024]{1,0:T(8,128)(2,1)S(1)}, bf16[96,1024]{1,0:T(8,128)(2,1)S(1)}, u32[]{:S(2)}, u32[]{:S(2)}) collective-permute-start(bf16[96,1024]{1,0:T(8,128)(2,1)S(1)} %get-tuple-element.92), channel_id=1, source_target_pairs={{0,4},{4,8},{8,12},{12,0},{1,5},{5,9},{9,13},{13,1},{2,6},{6,10},{... | collective-permute-start | bytes 589832 | tf_op jit(solution)/shard_map/ppermute | solution.py:254
  (18 other events, 71.4 us)
